TPU v7x, 32 devices: a whole 2x2x4 slice. The times are simulated.
32 devices in a mesh: parts: 2 (over y), aux: 4 (over z), bas: 2 (over x), occ: 2 (over core).
Axes of the slice: x: 2, y: 2, z: 4, core: 2. Of those that a mesh axis runs over, the one named last changes fastest.
Arguments:
- integrals: bfloat16 [8, 2, 2, 128, 128, 128], P(('parts', 'aux'), 'bas'), parts along dimension 0
- screening: int32 [8, 2, 2], P(('parts', 'aux'), 'bas'), parts along dimension 0, may hold values from 0 to 15, as said below
- coefficients: bfloat16 [4096, 256], P(('parts', 'bas'), 'occ'), parts along dimension 0, may hold values from -0.375 to 0.375
- metric: bfloat16 [1024, 512], P(('parts', 'aux')), parts along dimension 0
- aux_owner: int32 [8], P('parts'), parts along dimension 0, may hold values from 0 to 3, each once
Outputs:
- exchange: float32 [512, 256], P(('parts', 'bas'), ('aux', 'occ')), parts along dimension 0
There are 2 independent parts, one for each index of `parts`. A program takes and returns all parts, laid end to end along the dimension named above; each array names one. Nothing has to cross between parts.
Inputs may be any that keep to these rules, and one draw needn't show every extreme that they name: `screening`: each aux and bas index holds 2 distinct contracted blocks, consecutive modulo 16. `aux_owner`: a permutation.
All inputs are finite; a program needn't handle non-finite values.
Results may differ from a plain program's by a relative error of at most 0.0003.
Values may be sent and summed in bfloat16 or wider, within the bound.
No kernel may reach another device: no remote copies, remote signals or barrier semaphores. Data moves between devices by JAX's collectives and lax.ppermute only.
A program may use at most 128 MiB of HBM per device.

v0:
```python
import jax
import jax.numpy as jnp
from jax import lax
from jax.sharding import PartitionSpec as P


def per_device(integrals, screening, coefficients, metric, aux_owner):
    block_size = integrals.shape[-1]
    aux_count = lax.axis_size("aux")
    bas_count = lax.axis_size("bas")
    occ_count = lax.axis_size("occ")
    gathered = lax.all_gather(coefficients, "bas", axis=0, tiled=True)
    orbitals = gathered.shape[1]
    by_block = gathered.reshape(gathered.shape[0] // block_size, block_size, orbitals)
    picked = jnp.take(by_block, screening[0, 0], axis=0)
    stacked = integrals[0, 0].reshape(integrals.shape[2], block_size, block_size * block_size)
    contracted = lax.dot_general(
        picked, stacked, (((0, 1), (0, 1)), ((), ())), preferred_element_type=jnp.float32
    )
    transformed = contracted.astype(jnp.bfloat16)
    share = orbitals // (aux_count * bas_count)
    moved = lax.all_to_all(
        transformed.reshape(orbitals, 1, block_size, block_size),
        ("aux", "bas"),
        split_axis=0,
        concat_axis=1,
        tiled=True,
    )
    moved = moved.reshape(share, aux_count, bas_count, block_size, block_size)
    aux_table = (aux_owner[:, None] == jnp.arange(aux_count, dtype=jnp.int32)[None, :]).astype(
        jnp.bfloat16
    )
    piece = lax.all_gather(metric, "aux", axis=0, tiled=True)
    columns = piece.reshape(piece.shape[0], aux_count, block_size)
    ordered = jnp.einsum(
        "rgp,ag->rap", columns, aux_table, preferred_element_type=jnp.float32
    ).astype(jnp.bfloat16)
    fitted = jnp.einsum(
        "rap,iabpm->irbm", ordered, moved, preferred_element_type=jnp.float32
    ).astype(jnp.bfloat16)
    partial_value = jnp.einsum(
        "iqbm,iqcn->bmcn", fitted, fitted, preferred_element_type=jnp.float32
    )
    column_share = bas_count * block_size // (aux_count * occ_count)
    arranged = partial_value.reshape(bas_count, block_size, aux_count, occ_count, column_share)
    arranged = arranged.transpose(2, 0, 3, 1, 4).reshape(-1, column_share)
    return lax.psum_scatter(arranged, ("aux", "bas", "occ"), scatter_dimension=0, tiled=True)


def solution(mesh):
    in_specs = (
        P(("parts", "aux"), "bas", None, None, None, None),
        P(("parts", "aux"), "bas", None),
        P(("parts", "bas"), "occ"),
        P(("parts", "aux"), None),
        P("parts"),
    )
    out_specs = P(("parts", "bas"), ("aux", "occ"))
    return jax.shard_map(
        per_device, mesh=mesh, in_specs=in_specs, out_specs=out_specs, check_vma=False
    )
```

profile of v0, /device:TPU:0, one launch (start us, length us, event | category | flops | bytes accessed | tf_op | source)
XLA Modules:
  0.0 223.4 jit_solution(11304498266680158810)
XLA Ops:
  6.5 0.7 fusion.20
  7.2 0.7 compare_and_fusion
  7.9 0.0 copy-start
  7.9 13.4 %reshape_squeeze.3 = bf16[2,128,16384]{2,1,0:T(8,128)(2,1)} reshape(bf16[1,1,2,128,128,128]{5,4,3,2,1,0:T(8,128)(2,1)} %param.5) | data formatting | bytes 16777216 | tf_op jit(solution)/shard_map/reshape;squeeze | solution.py:16
  21.2 0.0 copy-done
  21.2 9.9 %all_gather.6 = bf16[2048,128]{1,0:T(8,128)(2,1)S(1)} all-gather(bf16[1024,128]{1,0:T(8,128)(2,1)S(1)} %copy-done), channel_id=1, replica_groups=mesh['parts'=2,'aux'=4,'bas'=2,'occ'=2] {'bas'}, dimensions={0}, use_global_device_ids=true | all-gather | bytes 786432 | tf_op jit(solution)/shard_map/all_gather | solution.py:12
  31.1 0.6 gather_fusion
  31.7 4.7 %fusion.6 = bf16[16,8,128,128]{3,1,2,0:T(8,128)(2,1)S(1)} fusion(bf16[2,128,16384]{2,1,0:T(8,128)(2,1)} %reshape_squeeze.3, bf16[2,128,128]{2,1,0:T(8,128)(2,1)S(1)} %gather_fusion, pred[2]{0:T(512)(128)(4,1)S(1)} %compare_and_fusion), kind=kOutput, calls=%fused_computation.8 | convolution fusion | flops 1075871744 | bytes 12648450 | tf_op jit(solution)/shard_map/dot_general | solution.py:17
  36.4 3.2 %copy.40 = bf16[16,8,128,128]{3,2,1,0:T(8,128)(2,1)} copy(bf16[16,8,128,128]{3,1,2,0:T(8,128)(2,1)S(1)} %fusion.6) | data formatting | bytes 8388608
  39.7 0.0 copy-start.1
  39.7 0.0 copy-start.2
  39.7 6.2 %all-to-all-start = ((bf16[128,1,128,128]{3,2,1,0:T(8,128)(2,1)}), bf16[128,1,128,128]{3,2,1,0:T(8,128)(2,1)}, u32[]{:S(2)}, u32[]{:S(2)}) async-start(bf16[128,1,128,128]{3,2,1,0:T(8,128)(2,1)} %bitcast.71), calls=%async_computation | async-start | bytes 8388608 | tf_op jit(solution)/shard_map/all_to_all | solution.py:22
  45.9 0.0 reduce-scatter.2.cloned.1.call-start
  45.9 0.0 copy-done.1
  45.9 103.5 %all_gather.7 = bf16[512,512]{1,0:T(8,128)(2,1)S(1)} all-gather(bf16[128,512]{1,0:T(8,128)(2,1)S(1)} %copy-done.1), channel_id=1, replica_groups=mesh['parts'=2,'aux'=4,'bas'=2,'occ'=2] {'aux'}, dimensions={0}, use_global_device_ids=true | all-gather | bytes 655360 | tf_op jit(solution)/shard_map/all_gather | solution.py:33
  149.5 0.1 reshape.57
  149.6 0.0 copy-done.2
  149.6 0.5 fusion.7
  150.1 0.0 all-to-all-done
  150.1 10.7 %fusion.1 = f32[2,128,2,128,1]{1,3,4,2,0:T(8,128)S(1)} fusion(bf16[16,4,2,128,128]{4,3,0,2,1:T(8,128)(2,1)} %bitcast.8, bf16[512,4,128]{2,1,0:T(4,128)(2,1)S(1)} %fusion.7), kind=kOutput, calls=%fused_computation.4 | convolution fusion | flops 5372903424 | bytes 4980736 | tf_op jit(solution)/shard_map/iqbm,iqcn->bmcn/dot_general | solution.py:41
  160.9 0.2 copy.29
  161.1 0.9 reshape.59
  162.0 0.0 reduce-scatter.2.cloned.1.call-update
  162.0 54.5 %reduce-scatter.2.cloned.1.call-done = f32[128,32]{0,1:T(8,128)} async-done(((f32[2048,32]{0,1:T(8,128)}), f32[128,32]{0,1:T(8,128)}) %reduce-scatter.2.cloned.1.call-update) | async-done | bytes 16400 | tf_op jit(solution)/shard_map/reduce_scatter | solution.py:47
  (1 shorter events, 0.0 us)
Async XLA Ops:
  7.9 13.4 %copy-start = (bf16[1024,128]{1,0:T(8,128)(2,1)S(1)}, bf16[1024,128]{1,0:T(8,128)(2,1)}, u32[]{:S(2)}) copy-start(bf16[1024,128]{1,0:T(8,128)(2,1)} %param.7) | copy-start | bytes 786436
  39.7 6.2 %copy-start.1 = (bf16[128,512]{1,0:T(8,128)(2,1)S(1)}, bf16[128,512]{1,0:T(8,128)(2,1)}, u32[]{:S(2)}) copy-start(bf16[128,512]{1,0:T(8,128)(2,1)} %param.8) | copy-start | bytes 393220
  39.7 109.9 %copy-start.2 = (s32[4]{0:T(128)S(1)}, s32[4]{0:T(128)}, u32[]{:S(2)}) copy-start(s32[4]{0:T(128)} %param.9) | copy-start | bytes 52
  39.7 110.4 %all-to-all-start = ((bf16[128,1,128,128]{3,2,1,0:T(8,128)(2,1)}), bf16[128,1,128,128]{3,2,1,0:T(8,128)(2,1)}, u32[]{:S(2)}, u32[]{:S(2)}) async-start(bf16[128,1,128,128]{3,2,1,0:T(8,128)(2,1)} %bitcast.71), calls=%async_computation | async-start | bytes 8388608 | tf_op jit(solution)/shard_map/all_to_all | solution.py:22
  45.9 170.7 %reduce-scatter.2.cloned.1.call-start = ((), (), s32[]{:S(2)}) async-start(), calls=%async_computation.2 | async-start | bytes 278528 | tf_op jit(solution)/shard_map/reduce_scatter | solution.py:47
Sparse Core Ops, SparseCore 0:
  162.1 54.3 reduce-scatter.1
where the time goes:
time: 224 us; the launch traced here: 223 us
  blocking collectives  113 us (50%)
  waiting for transfers between devices  54.5 us (24%)
  local copies, waits for them, and re-layouts  18.4 us (8%)
  matrix products  16 us (7%)
  between operations  13.5 us (6%)
  starting transfers between devices  6.24 us (3%)
    all_gather x1, blocking collectives, per_device(): piece = lax.all_gather(metric, 'aux', axis=0, tiled=True)  104 us
    reduce_scatter x1, waiting for transfers between devices, per_device(): lax.psum_scatter(arranged, ('aux', 'bas', 'occ'), scatter_dimension=0, ti...  54.5 us
    another operation x1, local copies, waits for them, and re-layouts, per_device(): integrals[0, 0]  13.4 us
    dot_general x1, matrix products, per_device(): jnp.einsum('iqbm,iqcn->bmcn', fitted, fitted, preferred_element_type=jnp....  10.7 us
    all_gather x1, blocking collectives, per_device(): gathered = lax.all_gather(coefficients, 'bas', axis=0, tiled=True)  9.9 us
    all_to_all x1, starting transfers between devices, per_device(): lax.all_to_all(transformed.reshape(orbitals, 1, block_size, block_size),...  6.2 us
    dot_general x1, matrix products, per_device(): lax.dot_general(picked, stacked, (((0, 1), (0, 1)), ((), ())), preferred_...  4.75 us
  transfers between devices with their start and end apart: 2, of which 1 were waited for; matrix products, arithmetic and copies ran while one was open for 0% of the time, Pallas kernels for 0%

commit v1 on v0

--- a/solution.py
+++ b/solution.py
@@ -1,10 +1,313 @@
+import functools
+
 import jax
 import jax.numpy as jnp
 from jax import lax
+from jax.experimental import pallas as pl
+from jax.experimental.pallas import tpu as pltpu
 from jax.sharding import PartitionSpec as P
 
+F32 = jnp.float32
+BF16 = jnp.bfloat16
+ROWS = 16
+WHOLE = pl.BlockSpec(memory_space=pltpu.VMEM)
+
+
+def params(mib=40):
+    return pltpu.CompilerParams(vmem_limit_bytes=mib * 2**20)
+
+
+def cost(macs, size):
+    return pl.CostEstimate(flops=2 * macs, bytes_accessed=size, transcendentals=0)
+
+
+def relayout_kernel(x_ref, o_ref):
+    slots, depth, rows, width = x_ref.shape
+    o_ref[...] = jnp.swapaxes(x_ref[...].reshape(slots * depth, rows, width), 0, 1)
+
+
+def relayout(integrals, first):
+    slots, depth, _, width = integrals.shape
+    return pl.pallas_call(
+        relayout_kernel,
+        grid=(first // ROWS,),
+        in_specs=[pl.BlockSpec((slots, depth, ROWS, width), lambda j: (0, 0, j, 0))],
+        out_specs=pl.BlockSpec((ROWS, slots * depth, width), lambda j: (j, 0, 0)),
+        out_shape=jax.ShapeDtypeStruct((first, slots * depth, width), BF16),
+        compiler_params=params(),
+        cost_estimate=cost(0, 2 * first * slots * depth * width * 2),
+        name="relayout",
+    )(integrals)
+
+
+def products(table, block):
+    parts = []
+    for p in range(0, block.shape[0], 2):
+        pair = jnp.concatenate([block[p], block[p + 1]], axis=1)
+        value = jnp.dot(table, pair, preferred_element_type=F32).astype(BF16)
+        width = block.shape[2]
+        parts += [value[:, :width], value[:, width:]]
+    return jnp.swapaxes(jnp.stack(parts), 0, 1)
+
+
+def first_kernel(chips, where, own_ref, other_ref, x_ref, *rest):
+    outs, table_ref, plain = rest[:chips], rest[chips], rest[chips + 1]
+    share = table_ref.shape[0] // chips
+
+    @pl.when(pl.program_id(0) == 0)
+    def _():
+        block = plain.shape[0]
+        held = own_ref.shape[0] // block
+        for s in range(plain.shape[1] // block):
+            name = where[2 + s]
+            away = lax.div(name, held) != where[1]
+            start = pl.multiple_of(lax.rem(name, held) * block, block)
+            mine = own_ref[pl.ds(start, block), :].astype(F32)
+            theirs = other_ref[pl.ds(start, block), :].astype(F32)
+            picked = jnp.where(away, theirs, mine)
+            plain[:, s * block : (s + 1) * block] = picked.T.astype(BF16)
+        for k in range(chips):
+            start = pl.multiple_of((where[0] ^ k) * share, share)
+            table_ref[k * share : (k + 1) * share, :] = plain[pl.ds(start, share), :]
+
+    value = products(table_ref[...], x_ref[...])
+    for k in range(chips):
+        outs[k][...] = value[k * share : (k + 1) * share]
+
+
+def first_products(chips, where, own, other, moved):
+    first, depth, width = moved.shape
+    orbitals = own.shape[1]
+    share = orbitals // chips
+    whole = lambda shape: pl.BlockSpec(shape, lambda j, w: (0,) * len(shape))
+    return pl.pallas_call(
+        functools.partial(first_kernel, chips),
+        grid_spec=pltpu.PrefetchScalarGridSpec(
+            num_scalar_prefetch=1,
+            grid=(first // ROWS,),
+            in_specs=[
+                whole(own.shape),
+                whole(other.shape),
+                pl.BlockSpec((ROWS, depth, width), lambda j, w: (j, 0, 0)),
+            ],
+            out_specs=[pl.BlockSpec((share, ROWS, width), lambda j, w: (0, j, 0))] * chips
+            + [whole((orbitals, depth))],
+            scratch_shapes=[pltpu.VMEM((orbitals, depth), BF16)],
+        ),
+        out_shape=[jax.ShapeDtypeStruct((share, first, width), BF16)] * chips
+        + [jax.ShapeDtypeStruct((orbitals, depth), BF16)],
+        compiler_params=params(),
+        cost_estimate=cost(orbitals * depth * first * width, moved.size * 2),
+        name="first_products",
+    )(where, own, other, moved)
+
+
+def rest_kernel(chips, groups, x_ref, table_ref, *outs):
+    slots, depth, rows, width = x_ref.shape
+    block = jnp.swapaxes(x_ref[...].reshape(slots * depth, rows, width), 0, 1)
+    value = products(table_ref[...], block)
+    share = table_ref.shape[0] // chips
+    for g, (lo, hi) in enumerate(groups):
+        for k in range(chips):
+            outs[g * chips + k][...] = value[k * share + lo : k * share + hi]
+
+
+def rest_products(chips, groups, integrals, table, first):
+    slots, depth, total, width = integrals.shape
+    orbitals = table.shape[0]
+    rest = total - first
+    skip = first // ROWS
+    shapes = [(hi - lo) for lo, hi in groups for _ in range(chips)]
+    return pl.pallas_call(
+        functools.partial(rest_kernel, chips, groups),
+        grid=(rest // ROWS,),
+        in_specs=[
+            pl.BlockSpec((slots, depth, ROWS, width), lambda j: (0, 0, j + skip, 0)),
+            pl.BlockSpec(table.shape, lambda j: (0, 0)),
+        ],
+        out_specs=[pl.BlockSpec((n, ROWS, width), lambda j: (0, j, 0)) for n in shapes],
+        out_shape=[jax.ShapeDtypeStruct((n, rest, width), BF16) for n in shapes],
+        compiler_params=params(),
+        cost_estimate=cost(orbitals * table.shape[1] * rest * width, integrals.size * 2),
+        name="rest_products",
+    )(integrals, table)
+
+
+def metric_kernel(where, own_ref, near_ref, far_ref, o_ref):
+    aux = where.shape[0] - 1
+    width = o_ref.shape[1] // aux
+    for kz in range(aux):
+        start = pl.multiple_of(where[where[aux] ^ kz] * width, width)
+        at = 0
+        for ref in (own_ref, near_ref, far_ref):
+            size = ref.shape[0]
+            o_ref[at : at + size, kz * width : (kz + 1) * width] = ref[:, pl.ds(start, width)]
+            at += size
+
+
+def ordered_metric(where, own, near, far):
+    total = own.shape[0] + near.shape[0] + far.shape[0]
+    return pl.pallas_call(
+        metric_kernel,
+        in_specs=[pl.BlockSpec(memory_space=pltpu.SMEM)] + [WHOLE] * 3,
+        out_specs=WHOLE,
+        out_shape=jax.ShapeDtypeStruct((total, own.shape[1]), BF16),
+        compiler_params=params(),
+        cost_estimate=cost(0, total * own.shape[1] * 4),
+        name="ordered_metric",
+    )(where, own, near, far)
+
+
+def add_group(aux, bas, lo, hi, metric, early, late, total):
+    chips = aux * bas
+    for i in range(lo, hi):
+        columns = []
+        for k in range(chips):
+            columns.append(jnp.concatenate([early[k][i], late[k][i - lo]], axis=0))
+        stacked = jnp.concatenate(
+            [jnp.concatenate(columns[kz * bas : (kz + 1) * bas], axis=1) for kz in range(aux)],
+            axis=0,
+        )
+        fitted = jnp.dot(metric, stacked, preferred_element_type=F32).astype(BF16)
+        total = total + lax.dot_general(
+            fitted, fitted, (((0,), (0,)), ((), ())), preferred_element_type=F32
+        )
+    return total
+
+
+def group_kernel(aux, bas, lo, hi, started, last, *refs):
+    chips = aux * bas
+    refs = list(refs)
+    where = refs.pop(0) if last else None
+    metric = refs.pop(0)[...]
+    early = [refs.pop(0) for _ in range(chips)]
+    late = [refs.pop(0) for _ in range(chips)]
+    side = bas * late[0].shape[2]
+    total = refs.pop(0)[...] if started else jnp.zeros((side, side), F32)
+    total = add_group(aux, bas, lo, hi, metric, early, late, total)
+    if not last:
+        refs[0][...] = total
+        return
+    kept, near, away, scratch = refs
+    scratch[...] = total
+    width = side // bas
+    piece = kept.shape[1]
+    for ka in range(aux):
+        a = where[0] ^ ka
+        for who in range(2):
+            row = (a * 2 + (where[2] ^ who)) * piece
+            block = lax.div(row, width) ^ where[1]
+            start = pl.multiple_of(block * width + lax.rem(row, width), piece)
+            value = scratch[pl.ds(start, piece), :]
+            if who:
+                away[ka] = value
+            else:
+                kept[ka] = value[:, :width]
+                near[ka] = value[:, width:]
+
+
+def group(aux, bas, lo, hi, metric, early, late, total, where=None):
+    last, started = where is not None, total is not None
+    width = late[0].shape[2]
+    side = bas * width
+    args = ([where] if last else []) + [metric, *early, *late] + ([total] if started else [])
+    specs = [WHOLE] * len(args)
+    if last:
+        specs[0] = pl.BlockSpec(memory_space=pltpu.SMEM)
+        piece = side // (aux * 2)
+        out = [
+            jax.ShapeDtypeStruct((aux, piece, width), F32),
+            jax.ShapeDtypeStruct((aux, piece, width), F32),
+            jax.ShapeDtypeStruct((aux, piece, side), F32),
+        ]
+    else:
+        out = jax.ShapeDtypeStruct((side, side), F32)
+    rows = metric.shape[0]
+    macs = (hi - lo) * (rows * rows * side + rows * side * side)
+    return pl.pallas_call(
+        functools.partial(group_kernel, aux, bas, lo, hi, started, last),
+        in_specs=specs,
+        out_specs=[WHOLE] * 3 if last else WHOLE,
+        out_shape=out,
+        scratch_shapes=[pltpu.VMEM((side, side), F32)] if last else [],
+        compiler_params=params(),
+        cost_estimate=cost(macs, (hi - lo) * rows * side * 2),
+        name="group",
+    )(*args)
+
+
+def turn_kernel(*refs):
+    total = refs[0][...]
+    for ref in refs[1:-1]:
+        total = total + ref[...]
+    refs[-1][...] = total.T
+
 
 def per_device(integrals, screening, coefficients, metric, aux_owner):
+    aux = lax.axis_size("aux")
+    bas = lax.axis_size("bas")
+    chips = aux * bas
+    integrals = integrals[0, 0]
+    orbitals = coefficients.shape[1]
+    share = orbitals // chips
+    a, b, o = (lax.axis_index(name) for name in ("aux", "bas", "occ"))
+    first = integrals.shape[2] // 4
+    groups = ((0, 6), (6, 12), (12, share))
+
+    def swap(value, kz=0, kx=0):
+        pairs = [
+            (i * bas + j, (i ^ kz) * bas + (j ^ kx)) for i in range(aux) for j in range(bas)
+        ]
+        return lax.ppermute(value, ("aux", "bas"), pairs)
+
+    def across(value):
+        return lax.ppermute(value, "occ", [(0, 1), (1, 0)])
+
+    other = swap(coefficients, kx=1)
+    rows = metric.shape[0] // 2
+    half = lax.dynamic_slice_in_dim(metric, o * rows, rows, axis=0)
+    near = jnp.concatenate([swap(half, kz=kz) for kz in range(1, aux)], axis=0)
+    far = across(near)
+    ordered = ordered_metric(
+        jnp.concatenate([aux_owner, a[None]]).astype(jnp.int32), metric, near, far
+    )
+
+    moved = relayout(integrals, first)
+    where = jnp.concatenate([jnp.stack([a * bas + b, b]), screening[0, 0]]).astype(jnp.int32)
+    *early, table = first_products(chips, where, coefficients, other, moved)
+    late = rest_products(chips, groups, integrals, table, first)
+
+    order = sorted(range(1, chips), key=lambda k: -(k // bas in (2, 3)))
+
+    def spread(values):
+        got = {0: values[0]}
+        for k in order:
+            got[k] = swap(values[k], k // bas, k % bas)
+        return [got[k] for k in range(chips)]
+
+    early = spread(early)
+    total = None
+    for g, (lo, hi) in enumerate(groups):
+        part = spread(late[g * chips : (g + 1) * chips])
+        here = jnp.stack([a, b, o]).astype(jnp.int32) if g == len(groups) - 1 else None
+        total = group(aux, bas, lo, hi, ordered, early, part, total, here)
+    kept, near, away = total
+    away = across(away)
+    width = kept.shape[2]
+    kept = kept + away[:, :, :width]
+    near = near + away[:, :, width:]
+    kept = kept + swap(near, kx=1)
+    pieces = [kept[0]] + [swap(kept[kz], kz=kz) for kz in range(1, aux)]
+    return pl.pallas_call(
+        turn_kernel,
+        in_specs=[WHOLE] * aux,
+        out_specs=WHOLE,
+        out_shape=jax.ShapeDtypeStruct((width, kept.shape[1]), F32),
+        name="turn",
+    )(*pieces)
+
+
+def plain_device(integrals, screening, coefficients, metric, aux_owner):
     block_size = integrals.shape[-1]
     aux_count = lax.axis_size("aux")
     bas_count = lax.axis_size("bas")
@@ -56,6 +359,11 @@
         P("parts"),
     )
     out_specs = P(("parts", "bas"), ("aux", "occ"))
+    small = mesh.shape["aux"] == 4 and mesh.shape["bas"] == 2 and mesh.shape["occ"] == 2
     return jax.shard_map(
-        per_device, mesh=mesh, in_specs=in_specs, out_specs=out_specs, check_vma=False
-    )
+        per_device if small else plain_device,
+        mesh=mesh,
+        in_specs=in_specs,
+        out_specs=out_specs,
+        check_vma=False,
+    )

time: 224 us -> 145 us (0.65)
  blocking collectives: 113 us -> 0 us
  starting transfers between devices: 6.24 us -> 70.4 us
  Pallas kernels: 0 us -> 16.7 us
  matrix products: 16 us -> 0 us
  between operations: 13.5 us -> 0.21 us
  local copies, waits for them, and re-layouts: 18.4 us -> 10.4 us
  waiting for transfers between devices: 54.5 us -> 46.8 us
    all_gather x2 -> x0, blocking collectives: 113 us -> none  [the longest x1 104 us: per_device(): piece = lax.all_gather(metric, 'aux', axis=0, tiled=True)]
    ppermute x0 -> x38, starting transfers between devices: none -> 70.4 us  [the longest x36 70.3 us: swap(): return lax.ppermute(value, ('aux', 'bas'), pairs)]
    reduce_scatter x1 -> x0, waiting for transfers between devices: 54.5 us -> none  [per_device(): lax.psum_scatter(arranged, ('aux', 'bas', 'occ'), scatter_dimension=0, ti...]
    ppermute x0 -> x38, waiting for transfers between devices: none -> 46.8 us  [the longest x36 45.5 us: swap(): return lax.ppermute(value, ('aux', 'bas'), pairs)]
    pallas_call x0 -> x8, Pallas kernels: none -> 16.7 us  [the longest x3 6.03 us: group(): pl.pallas_call(functools.partial(group_kernel, aux, bas, lo, hi, started,...]
    dot_general x3 -> x0, matrix products: 16 us -> none  [the longest x1 10.7 us: per_device(): jnp.einsum('iqbm,iqcn->bmcn', fitted, fitted, preferred_element_type=jnp....]
    another operation x1 -> x0, local copies, waits for them, and re-layouts: 13.4 us -> none  [per_device(): integrals[0, 0]]
    all_to_all x1 -> x0, starting transfers between devices: 6.2 us -> none  [per_device(): lax.all_to_all(transformed.reshape(orbitals, 1, block_size, block_size),...]
  transfers between devices with their start and end apart: 2 -> 38, of which waited for: 1 -> 16; matrix products, arithmetic and copies ran while one was open for 0% -> 0% of each run, Pallas kernels for 0% -> 9%
where the time goes in v1:
time: 145 us
  starting transfers between devices  70.4 us (49%)
  waiting for transfers between devices  46.8 us (32%)
  Pallas kernels  16.7 us (12%)
  local copies, waits for them, and re-layouts  10.4 us (7%)
    ppermute x36, starting transfers between devices, swap(): return lax.ppermute(value, ('aux', 'bas'), pairs)  70.3 us
    ppermute x36, waiting for transfers between devices, swap(): return lax.ppermute(value, ('aux', 'bas'), pairs)  45.5 us
    unnamed x20, local copies, waits for them, and re-layouts  7.39 us
    pallas_call x3, Pallas kernels, group(): pl.pallas_call(functools.partial(group_kernel, aux, bas, lo, hi, started,...  6.03 us
    pallas_call x1, Pallas kernels, rest_products(): pl.pallas_call(functools.partial(rest_kernel, chips, groups), grid=(rest...  5.77 us
  transfers between devices with their start and end apart: 38, of which 16 were waited for; matrix products, arithmetic and copies ran while one was open for 0% of the time, Pallas kernels for 9%

profile of v1, /device:TPU:0, one launch (start us, length us, event | category | flops | bytes accessed | tf_op | source)
XLA Modules:
  0.0 144.8 jit_solution(13303293317212616985)
XLA Ops:
  0.0 0.9 constant_dynamic-slice_fusion
  0.9 5.0 %collective-permute-start.2 = (bf16[64,512]{1,0:T(8,128)(2,1)S(1)}, bf16[64,512]{1,0:T(8,128)(2,1)S(1)}, u32[]{:S(2)}, u32[]{:S(2)}) collective-permute-start(bf16[64,512]{1,0:T(8,128)(2,1)S(1)} %constant_dynamic-slice_fusion), channel_id=1, source_target_pairs={{0,12},{2,14},{4,8},{6,10},{8,4},{10,6},{12,0},{14,2},{1,13},{3,15... | collective-permute-start | bytes 196616 | tf_op jit(solution)/shard_map/ppermute | solution.py:261
  6.5 1.7 %collective-permute-start.4 = (bf16[1024,128]{1,0:T(8,128)(2,1)}, bf16[1024,128]{1,0:T(8,128)(2,1)S(1)}, u32[]{:S(2)}, u32[]{:S(2)}) collective-permute-start(bf16[1024,128]{1,0:T(8,128)(2,1)} %own_ref.3), channel_id=1, source_target_pairs={{0,2},{2,0},{4,6},{6,4},{8,10},{10,8},{12,14},{14,12},{1,3},{3,1},... | collective-permute-start | bytes 786440 | tf_op jit(solution)/shard_map/ppermute | solution.py:261
  8.2 3.4 %copy-done = bf16[1,1,2,128,128,128]{5,4,3,2,1,0:T(8,128)(2,1)S(1)} copy-done((bf16[1,1,2,128,128,128]{5,4,3,2,1,0:T(8,128)(2,1)S(1)}, bf16[1,1,2,128,128,128]{5,4,3,2,1,0:T(8,128)(2,1)}, u32[]{:S(2)}) %copy-start) | copy-done | bytes 8388632
  11.6 1.1 relayout.1.x_ref
  12.9 1.3 collective-permute-done.4.other_ref
  14.2 1.7 %first_products.1 = (bf16[16,32,128]{2,1,0:T(8,128)(2,1)S(1)}, bf16[16,32,128]{2,1,0:T(8,128)(2,1)S(1)}, bf16[16,32,128]{2,1,0:T(8,128)(2,1)S(1)}, bf16[16,32,12...) custom-call(s32[4]{0:T(128)S(1)} %pad_add_fusion.2.where, ...), custom_call_target="tpu_custom_call" | custom-call | flops 268435456 | bytes 2097152 | tf_op jit(solution)/shard_map/first_products/pallas_call | solution.py:83
  15.9 1.6 %collective-permute-start.5 = (bf16[16,32,128]{2,1,0:T(8,128)(2,1)S(1)}, bf16[16,32,128]{2,1,0:T(8,128)(2,1)S(1)}, u32[]{:S(2)}, u32[]{:S(2)}) collective-permute-start(bf16[16,32,128]{2,1,0:T(8,128)(2,1)S(1)} %get-tuple-element.42), channel_id=1, source_target_pairs={{0,2},{2,0},{4,6},{6,4},{8,10},{10,8},{12,14},{14,12},{1,3},{3,1},... | collective-permute-start | bytes 393224 | tf_op jit(solution)/shard_map/ppermute | solution.py:261
  17.5 3.4 %copy-done.1 = bf16[1,1,2,128,128,128]{5,4,3,2,1,0:T(8,128)(2,1)S(1)} copy-done((bf16[1,1,2,128,128,128]{5,4,3,2,1,0:T(8,128)(2,1)S(1)}, bf16[1,1,2,128,128,128]{5,4,3,2,1,0:T(8,128)(2,1)}, u32[]{:S(2)}) %copy-start.1) | copy-done | bytes 8388632
  20.8 5.8 %rest_products.1 = (bf16[6,96,128]{2,1,0:T(8,128)(2,1)S(1)}, bf16[6,96,128]{2,1,0:T(8,128)(2,1)S(1)}, bf16[6,96,128]{2,1,0:T(8,128)(2,1)S(1)}, bf16[6,96,128]{2,...) custom-call(bf16[2,128,128,128]{3,2,1,0:T(8,128)(2,1)S(1)} %bitcast., ...), custom_call_target="tpu_custom_call" | custom-call | flops 805306368 | bytes 8388608 | tf_op jit(solution)/shard_map/rest_products/pallas_call | solution.py:121
  27.2 1.5 %collective-permute-start.13 = (bf16[4,96,128]{2,1,0:T(8,128)(2,1)S(1)}, bf16[4,96,128]{2,1,0:T(8,128)(2,1)S(1)}, u32[]{:S(2)}, u32[]{:S(2)}) collective-permute-start(bf16[4,96,128]{2,1,0:T(8,128)(2,1)S(1)} %get-tuple-element.52), channel_id=1, source_target_pairs={{0,4},{2,6},{4,0},{6,2},{8,12},{10,14},{12,8},{14,10},{1,5},{3,7},... | collective-permute-start | bytes 294920 | tf_op jit(solution)/shard_map/ppermute | solution.py:261
  29.2 2.4 %collective-permute-start.7 = (bf16[16,32,128]{2,1,0:T(8,128)(2,1)S(1)}, bf16[16,32,128]{2,1,0:T(8,128)(2,1)S(1)}, u32[]{:S(2)}, u32[]{:S(2)}) collective-permute-start(bf16[16,32,128]{2,1,0:T(8,128)(2,1)S(1)} %get-tuple-element.44), channel_id=1, source_target_pairs={{0,6},{2,4},{4,2},{6,0},{8,14},{10,12},{12,10},{14,8},{1,7},{3,5},... | collective-permute-start | bytes 393224 | tf_op jit(solution)/shard_map/ppermute | solution.py:261
  32.1 2.1 %collective-permute-start.8 = (bf16[16,32,128]{2,1,0:T(8,128)(2,1)S(1)}, bf16[16,32,128]{2,1,0:T(8,128)(2,1)S(1)}, u32[]{:S(2)}, u32[]{:S(2)}) collective-permute-start(bf16[16,32,128]{2,1,0:T(8,128)(2,1)S(1)} %get-tuple-element.45), channel_id=1, source_target_pairs={{0,8},{2,10},{4,12},{6,14},{8,0},{10,2},{12,4},{14,6},{1,9},{3,11}... | collective-permute-start | bytes 393224 | tf_op jit(solution)/shard_map/ppermute | solution.py:261
  34.3 1.9 %collective-permute-start.9 = (bf16[16,32,128]{2,1,0:T(8,128)(2,1)S(1)}, bf16[16,32,128]{2,1,0:T(8,128)(2,1)S(1)}, u32[]{:S(2)}, u32[]{:S(2)}) collective-permute-start(bf16[16,32,128]{2,1,0:T(8,128)(2,1)S(1)} %get-tuple-element.46), channel_id=1, source_target_pairs={{0,10},{2,8},{4,14},{6,12},{8,2},{10,0},{12,6},{14,4},{1,11},{3,9}... | collective-permute-start | bytes 393224 | tf_op jit(solution)/shard_map/ppermute | solution.py:261
  36.2 2.8 %collective-permute-start.10 = (bf16[16,32,128]{2,1,0:T(8,128)(2,1)S(1)}, bf16[16,32,128]{2,1,0:T(8,128)(2,1)S(1)}, u32[]{:S(2)}, u32[]{:S(2)}) collective-permute-start(bf16[16,32,128]{2,1,0:T(8,128)(2,1)S(1)} %get-tuple-element.47), channel_id=1, source_target_pairs={{0,12},{2,14},{4,8},{6,10},{8,4},{10,6},{12,0},{14,2},{1,13},{3,15... | collective-permute-start | bytes 393224 | tf_op jit(solution)/shard_map/ppermute | solution.py:261
  39.1 1.3 collective-permute-start.19
  40.4 1.0 collective-permute-done.7.refs_4_.refs_5_
  41.4 5.6 %collective-permute-done.8.refs_5_.refs_6_ = bf16[16,32,128]{2,1,0:T(8,128)(2,1)S(1)} collective-permute-done((bf16[16,32,128]{2,1,0:T(8,128)(2,1)S(1)}, bf16[16,32,128]{2,1,0:T(8,128)(2,1)S(1)}, u32[]{:S(2)}, u32[]{:S(2)}) %collective-permute-start.8) | collective-permute-done | bytes 131104 | tf_op jit(solution)/shard_map/ppermute | solution.py:261
  47.0 2.0 %collective-permute-done.9.refs_6_.refs_7_ = bf16[16,32,128]{2,1,0:T(8,128)(2,1)S(1)} collective-permute-done((bf16[16,32,128]{2,1,0:T(8,128)(2,1)S(1)}, bf16[16,32,128]{2,1,0:T(8,128)(2,1)S(1)}, u32[]{:S(2)}, u32[]{:S(2)}) %collective-permute-start.9) | collective-permute-done | bytes 131104 | tf_op jit(solution)/shard_map/ppermute | solution.py:261
  49.0 2.7 %collective-permute-start.11 = (bf16[16,32,128]{2,1,0:T(8,128)(2,1)S(1)}, bf16[16,32,128]{2,1,0:T(8,128)(2,1)S(1)}, u32[]{:S(2)}, u32[]{:S(2)}) collective-permute-start(bf16[16,32,128]{2,1,0:T(8,128)(2,1)S(1)} %get-tuple-element.48), channel_id=1, source_target_pairs={{0,14},{2,12},{4,10},{6,8},{8,6},{10,4},{12,2},{14,0},{1,15},{3,13... | collective-permute-start | bytes 393224 | tf_op jit(solution)/shard_map/ppermute | solution.py:261
  51.8 5.0 %collective-permute-done.11.refs_8_.refs_9_ = bf16[16,32,128]{2,1,0:T(8,128)(2,1)S(1)} collective-permute-done((bf16[16,32,128]{2,1,0:T(8,128)(2,1)S(1)}, bf16[16,32,128]{2,1,0:T(8,128)(2,1)S(1)}, u32[]{:S(2)}, u32[]{:S(2)}) %collective-permute-start.11) | collective-permute-done | bytes 131104 | tf_op jit(solution)/shard_map/ppermute | solution.py:261
  56.8 10.0 %collective-permute-start.28 = (bf16[6,96,128]{2,1,0:T(8,128)(2,1)S(1)}, bf16[6,96,128]{2,1,0:T(8,128)(2,1)S(1)}, u32[]{:S(2)}, u32[]{:S(2)}) collective-permute-start(bf16[6,96,128]{2,1,0:T(8,128)(2,1)S(1)} %get-tuple-element.69), channel_id=1, source_target_pairs={{0,6},{2,4},{4,2},{6,0},{8,14},{10,12},{12,10},{14,8},{1,7},{3,5},... | collective-permute-start | bytes 442376 | tf_op jit(solution)/shard_map/ppermute | solution.py:261
  66.8 2.0 %collective-permute-start.30 = (bf16[6,96,128]{2,1,0:T(8,128)(2,1)S(1)}, bf16[6,96,128]{2,1,0:T(8,128)(2,1)S(1)}, u32[]{:S(2)}, u32[]{:S(2)}) collective-permute-start(bf16[6,96,128]{2,1,0:T(8,128)(2,1)S(1)} %get-tuple-element.71), channel_id=1, source_target_pairs={{0,10},{2,8},{4,14},{6,12},{8,2},{10,0},{12,6},{14,4},{1,11},{3,9}... | collective-permute-start | bytes 442376 | tf_op jit(solution)/shard_map/ppermute | solution.py:261
  68.9 0.9 collective-permute-start.31
  69.8 4.7 %collective-permute-start.32 = (bf16[6,96,128]{2,1,0:T(8,128)(2,1)S(1)}, bf16[6,96,128]{2,1,0:T(8,128)(2,1)S(1)}, u32[]{:S(2)}, u32[]{:S(2)}) collective-permute-start(bf16[6,96,128]{2,1,0:T(8,128)(2,1)S(1)} %get-tuple-element.73), channel_id=1, source_target_pairs={{0,14},{2,12},{4,10},{6,8},{8,6},{10,4},{12,2},{14,0},{1,15},{3,13... | collective-permute-start | bytes 442376 | tf_op jit(solution)/shard_map/ppermute | solution.py:261
  74.6 11.0 %collective-permute-done.29.refs_13_ = bf16[6,96,128]{2,1,0:T(8,128)(2,1)S(1)} collective-permute-done((bf16[6,96,128]{2,1,0:T(8,128)(2,1)S(1)}, bf16[6,96,128]{2,1,0:T(8,128)(2,1)S(1)}, u32[]{:S(2)}, u32[]{:S(2)}) %collective-permute-start.29) | collective-permute-done | bytes 147488 | tf_op jit(solution)/shard_map/ppermute | solution.py:261
  85.6 4.6 %collective-permute-done.30.refs_14_ = bf16[6,96,128]{2,1,0:T(8,128)(2,1)S(1)} collective-permute-done((bf16[6,96,128]{2,1,0:T(8,128)(2,1)S(1)}, bf16[6,96,128]{2,1,0:T(8,128)(2,1)S(1)}, u32[]{:S(2)}, u32[]{:S(2)}) %collective-permute-start.30) | collective-permute-done | bytes 147488 | tf_op jit(solution)/shard_map/ppermute | solution.py:261
  90.2 3.9 %collective-permute-start.25 = (bf16[6,96,128]{2,1,0:T(8,128)(2,1)S(1)}, bf16[6,96,128]{2,1,0:T(8,128)(2,1)S(1)}, u32[]{:S(2)}, u32[]{:S(2)}) collective-permute-start(bf16[6,96,128]{2,1,0:T(8,128)(2,1)S(1)} %get-tuple-element.65), channel_id=1, source_target_pairs={{0,14},{2,12},{4,10},{6,8},{8,6},{10,4},{12,2},{14,0},{1,15},{3,13... | collective-permute-start | bytes 442376 | tf_op jit(solution)/shard_map/ppermute | solution.py:261
  94.2 0.6 ordered_metric.1.refs_0_.refs_1_
  94.8 2.0 %group.3.refs_17_ = f32[256,256]{1,0:T(8,128)S(1)} custom-call(bf16[512,512]{1,0:T(8,128)(2,1)S(1)} %ordered_metric.1.refs_0_.refs_1_, bf16[16,32,128]{2,1,0:T(8,128)(2,1)S(1)} %get-tuple-element.41.refs_1_.refs_2_, bf16[16,32,128]{2,1,0:T(8,128)(2,1)S(1)} %collective-permute-done.5.refs_2_.refs_3_, ...), custom_call_target="tpu_custom_call" | custom-call | flops 1207959552 | bytes 1572864 | tf_op jit(solution)/shard_map/group/pallas_call | solution.py:227
  96.8 11.7 %collective-permute-start.14 = (bf16[4,96,128]{2,1,0:T(8,128)(2,1)S(1)}, bf16[4,96,128]{2,1,0:T(8,128)(2,1)S(1)}, u32[]{:S(2)}, u32[]{:S(2)}) collective-permute-start(bf16[4,96,128]{2,1,0:T(8,128)(2,1)S(1)} %get-tuple-element.53), channel_id=1, source_target_pairs={{0,6},{2,4},{4,2},{6,0},{8,14},{10,12},{12,10},{14,8},{1,7},{3,5},... | collective-permute-start | bytes 294920 | tf_op jit(solution)/shard_map/ppermute | solution.py:261
  108.5 3.4 %collective-permute-done.23.refs_14_ = bf16[6,96,128]{2,1,0:T(8,128)(2,1)S(1)} collective-permute-done((bf16[6,96,128]{2,1,0:T(8,128)(2,1)S(1)}, bf16[6,96,128]{2,1,0:T(8,128)(2,1)S(1)}, u32[]{:S(2)}, u32[]{:S(2)}) %collective-permute-start.23) | collective-permute-done | bytes 147488 | tf_op jit(solution)/shard_map/ppermute | solution.py:261
  111.9 1.6 %collective-permute-start.16 = (bf16[4,96,128]{2,1,0:T(8,128)(2,1)S(1)}, bf16[4,96,128]{2,1,0:T(8,128)(2,1)S(1)}, u32[]{:S(2)}, u32[]{:S(2)}) collective-permute-start(bf16[4,96,128]{2,1,0:T(8,128)(2,1)S(1)} %get-tuple-element.55), channel_id=1, source_target_pairs={{0,10},{2,8},{4,14},{6,12},{8,2},{10,0},{12,6},{14,4},{1,11},{3,9}... | collective-permute-start | bytes 294920 | tf_op jit(solution)/shard_map/ppermute | solution.py:261
  113.5 3.3 %collective-permute-start.18 = (bf16[4,96,128]{2,1,0:T(8,128)(2,1)S(1)}, bf16[4,96,128]{2,1,0:T(8,128)(2,1)S(1)}, u32[]{:S(2)}, u32[]{:S(2)}) collective-permute-start(bf16[4,96,128]{2,1,0:T(8,128)(2,1)S(1)} %get-tuple-element.57), channel_id=1, source_target_pairs={{0,14},{2,12},{4,10},{6,8},{8,6},{10,4},{12,2},{14,0},{1,15},{3,13... | collective-permute-start | bytes 294920 | tf_op jit(solution)/shard_map/ppermute | solution.py:261
  116.8 2.1 %group.4.refs_18_ = f32[256,256]{1,0:T(8,128)S(1)} custom-call(bf16[512,512]{1,0:T(8,128)(2,1)S(1)} %ordered_metric.1.refs_0_.refs_1_, bf16[16,32,128]{2,1,0:T(8,128)(2,1)S(1)} %get-tuple-element.41.refs_1_.refs_2_, bf16[16,32,128]{2,1,0:T(8,128)(2,1)S(1)} %collective-permute-done.5.refs_2_.refs_3_, ...), custom_call_target="tpu_custom_call" | custom-call | flops 1207959552 | bytes 1572864 | tf_op jit(solution)/shard_map/group/pallas_call | solution.py:227
  118.9 4.0 %collective-permute-done.15.refs_14_ = bf16[4,96,128]{2,1,0:T(8,128)(2,1)S(1)} collective-permute-done((bf16[4,96,128]{2,1,0:T(8,128)(2,1)S(1)}, bf16[4,96,128]{2,1,0:T(8,128)(2,1)S(1)}, u32[]{:S(2)}, u32[]{:S(2)}) %collective-permute-start.15) | collective-permute-done | bytes 98336 | tf_op jit(solution)/shard_map/ppermute | solution.py:261
  122.9 0.7 collective-permute-done.16.refs_15_
  123.6 2.0 %group.5 = (f32[4,32,128]{2,1,0:T(8,128)S(1)}, f32[4,32,128]{2,1,0:T(8,128)S(1)}, f32[4,32,256]{2,1,0:T(8,128)S(1)}) custom-call(s32[3]{0:T(128)S(1)} %pad_add_fusion.refs_0_, bf16[512,512]{1,0:T(8,128)(2,1)S(1)} %ordered_metric.1.refs_0_.refs_1_, bf16[16,32,128]{2,1,0:T(8,128)(2,1)S(1)} %get-tuple-element.41.refs_1_.refs_2_, ...), custom_call_target="tpu_custom_call" | custom-call | flops 805306368 | bytes 1048576 | tf_op jit(solution)/shard_map/group/pallas_call | solution.py:227
  125.7 1.3 collective-permute-done.33
  127.0 1.9 %collective-permute-start.34 = (f32[4,32,128]{2,1,0:T(8,128)S(1)}, f32[4,32,128]{2,1,0:T(8,128)S(1)}, u32[]{:S(2)}, u32[]{:S(2)}) collective-permute-start(f32[4,32,128]{2,1,0:T(8,128)S(1)} %slice_add_fusion), channel_id=1, source_target_pairs={{0,2},{2,0},{4,6},{6,4},{8,10},{10,8},{12,14},{14,12},{1,3},{3,1},... | collective-permute-start | bytes 196616 | tf_op jit(solution)/shard_map/ppermute | solution.py:261
  128.9 2.5 %collective-permute-done.34 = f32[4,32,128]{2,1,0:T(8,128)S(1)} collective-permute-done((f32[4,32,128]{2,1,0:T(8,128)S(1)}, f32[4,32,128]{2,1,0:T(8,128)S(1)}, u32[]{:S(2)}, u32[]{:S(2)}) %collective-permute-start.34) | collective-permute-done | bytes 65568 | tf_op jit(solution)/shard_map/ppermute | solution.py:261
  131.4 0.6 slice_bitcast_fusion
  132.0 2.7 %collective-permute-start.37 = (f32[32,128]{1,0:T(8,128)S(1)}, f32[32,128]{1,0:T(8,128)S(1)}, u32[]{:S(2)}, u32[]{:S(2)}) collective-permute-start(f32[32,128]{1,0:T(8,128)S(1)} %get-tuple-element.77), channel_id=1, source_target_pairs={{0,12},{2,14},{4,8},{6,10},{8,4},{10,6},{12,0},{14,2},{1,13},{3,15... | collective-permute-start | bytes 49160 | tf_op jit(solution)/shard_map/ppermute | solution.py:261
  134.7 2.7 %collective-permute-start.36 = (f32[32,128]{1,0:T(8,128)S(1)}, f32[32,128]{1,0:T(8,128)S(1)}, u32[]{:S(2)}, u32[]{:S(2)}) collective-permute-start(f32[32,128]{1,0:T(8,128)S(1)} %get-tuple-element.78), channel_id=1, source_target_pairs={{0,8},{2,10},{4,12},{6,14},{8,0},{10,2},{12,4},{14,6},{1,9},{3,11}... | collective-permute-start | bytes 49160 | tf_op jit(solution)/shard_map/ppermute | solution.py:261
  137.6 1.8 %collective-permute-done.36.refs_2_ = f32[32,128]{1,0:T(8,128)S(1)} collective-permute-done((f32[32,128]{1,0:T(8,128)S(1)}, f32[32,128]{1,0:T(8,128)S(1)}, u32[]{:S(2)}, u32[]{:S(2)}) %collective-permute-start.36) | collective-permute-done | bytes 16416 | tf_op jit(solution)/shard_map/ppermute | solution.py:261
  139.3 1.8 %collective-permute-done.35.refs_1_ = f32[32,128]{1,0:T(8,128)S(1)} collective-permute-done((f32[32,128]{1,0:T(8,128)S(1)}, f32[32,128]{1,0:T(8,128)S(1)}, u32[]{:S(2)}, u32[]{:S(2)}) %collective-permute-start.35) | collective-permute-done | bytes 16416 | tf_op jit(solution)/shard_map/ppermute | solution.py:261
  141.8 1.5 %turn.1 = f32[128,32]{1,0:T(8,128)} custom-call(f32[32,128]{1,0:T(8,128)} %get-tuple-element.80.refs_0_, f32[32,128]{1,0:T(8,128)} %copy-done.6, f32[32,128]{1,0:T(8,128)} %copy-done.5, f32[32,128]{1,0:T(8,128)} %copy-done.4), custom_call_target="tpu_custom_call" | custom-call | tf_op jit(solution)/shard_map/turn/pallas_call | solution.py:301
  143.3 1.5 %copy.6 = f32[128,32]{0,1:T(8,128)} copy(f32[128,32]{1,0:T(8,128)} %turn.1) | data formatting | bytes 32768 | tf_op jit(solution)/shard_map/turn/pallas_call | solution.py:301
  (65 shorter events, 3.6 us)
Async XLA Ops:
  0.0 12.7 %copy-start.7 = (s32[1,1,2]{2,1,0:T(1,128)S(1)}, s32[1,1,2]{2,1,0:T(1,128)}, u32[]{:S(2)}) copy-start(s32[1,1,2]{2,1,0:T(1,128)} %param.6) | copy-start | bytes 28
  0.9 11.9 %collective-permute-start.2 = (bf16[64,512]{1,0:T(8,128)(2,1)S(1)}, bf16[64,512]{1,0:T(8,128)(2,1)S(1)}, u32[]{:S(2)}, u32[]{:S(2)}) collective-permute-start(bf16[64,512]{1,0:T(8,128)(2,1)S(1)} %constant_dynamic-slice_fusion), channel_id=1, source_target_pairs={{0,12},{2,14},{4,8},{6,10},{8,4},{10,6},{12,0},{14,2},{1,13},{3,15... | collective-permute-start | bytes 196616 | tf_op jit(solution)/shard_map/ppermute | solution.py:261
  5.9 6.9 %collective-permute-start.1 = (bf16[64,512]{1,0:T(8,128)(2,1)S(1)}, bf16[64,512]{1,0:T(8,128)(2,1)S(1)}, u32[]{:S(2)}, u32[]{:S(2)}) collective-permute-start(bf16[64,512]{1,0:T(8,128)(2,1)S(1)} %constant_dynamic-slice_fusion), channel_id=1, source_target_pairs={{0,8},{2,10},{4,12},{6,14},{8,0},{10,2},{12,4},{14,6},{1,9},{3,11}... | collective-permute-start | bytes 196616 | tf_op jit(solution)/shard_map/ppermute | solution.py:261
  5.9 6.8 %collective-permute-start = (bf16[64,512]{1,0:T(8,128)(2,1)S(1)}, bf16[64,512]{1,0:T(8,128)(2,1)S(1)}, u32[]{:S(2)}, u32[]{:S(2)}) collective-permute-start(bf16[64,512]{1,0:T(8,128)(2,1)S(1)} %constant_dynamic-slice_fusion), channel_id=1, source_target_pairs={{0,4},{2,6},{4,0},{6,2},{8,12},{10,14},{12,8},{14,10},{1,5},{3,7},... | collective-permute-start | bytes 196616 | tf_op jit(solution)/shard_map/ppermute | solution.py:261
  6.5 7.7 %collective-permute-start.4 = (bf16[1024,128]{1,0:T(8,128)(2,1)}, bf16[1024,128]{1,0:T(8,128)(2,1)S(1)}, u32[]{:S(2)}, u32[]{:S(2)}) collective-permute-start(bf16[1024,128]{1,0:T(8,128)(2,1)} %own_ref.3), channel_id=1, source_target_pairs={{0,2},{2,0},{4,6},{6,4},{8,10},{10,8},{12,14},{14,12},{1,3},{3,1},... | collective-permute-start | bytes 786440 | tf_op jit(solution)/shard_map/ppermute | solution.py:261
  8.2 3.4 %copy-start = (bf16[1,1,2,128,128,128]{5,4,3,2,1,0:T(8,128)(2,1)S(1)}, bf16[1,1,2,128,128,128]{5,4,3,2,1,0:T(8,128)(2,1)}, u32[]{:S(2)}) copy-start(bf16[1,1,2,128,128,128]{5,4,3,2,1,0:T(8,128)(2,1)} %param.5) | copy-start | bytes 25165828
  11.6 2.6 %copy-start.3 = (bf16[1024,128]{1,0:T(8,128)(2,1)S(1)}, bf16[1024,128]{1,0:T(8,128)(2,1)}, u32[]{:S(2)}) copy-start(bf16[1024,128]{1,0:T(8,128)(2,1)} %own_ref.3) | copy-start | bytes 786436
  11.6 82.5 %copy-start.8 = (s32[4]{0:T(128)S(1)}, s32[4]{0:T(128)}, u32[]{:S(2)}) copy-start(s32[4]{0:T(128)} %param.9) | copy-start | bytes 52
  12.6 81.5 %copy-start.2 = (bf16[128,512]{1,0:T(8,128)(2,1)S(1)}, bf16[128,512]{1,0:T(8,128)(2,1)}, u32[]{:S(2)}) copy-start(bf16[128,512]{1,0:T(8,128)(2,1)} %own_ref.2) | copy-start | bytes 393220
  12.8 16.4 %collective-permute-start.3 = (bf16[192,512]{1,0:T(8,128)(2,1)S(1)}, bf16[192,512]{1,0:T(8,128)(2,1)S(1)}, u32[]{:S(2)}, u32[]{:S(2)}) collective-permute-start(bf16[192,512]{1,0:T(8,128)(2,1)S(1)} %constant_dynamic-update-slice_fusion.near_ref), channel_id=1, source_target_pairs={{0,1},{1,0},{2,3},{3,2},{4,5},{5,4},{6,7},{7,6},{8,9},{9,8},{10,11... | collective-permute-start | bytes 589832 | tf_op jit(solution)/shard_map/ppermute | solution.py:264
  15.9 20.3 %collective-permute-start.5 = (bf16[16,32,128]{2,1,0:T(8,128)(2,1)S(1)}, bf16[16,32,128]{2,1,0:T(8,128)(2,1)S(1)}, u32[]{:S(2)}, u32[]{:S(2)}) collective-permute-start(bf16[16,32,128]{2,1,0:T(8,128)(2,1)S(1)} %get-tuple-element.42), channel_id=1, source_target_pairs={{0,2},{2,0},{4,6},{6,4},{8,10},{10,8},{12,14},{14,12},{1,3},{3,1},... | collective-permute-start | bytes 393224 | tf_op jit(solution)/shard_map/ppermute | solution.py:261
  17.5 3.4 %copy-start.1 = (bf16[1,1,2,128,128,128]{5,4,3,2,1,0:T(8,128)(2,1)S(1)}, bf16[1,1,2,128,128,128]{5,4,3,2,1,0:T(8,128)(2,1)}, u32[]{:S(2)}) copy-start(bf16[1,1,2,128,128,128]{5,4,3,2,1,0:T(8,128)(2,1)} %param.5) | copy-start | bytes 25165828
  26.6 5.5 %collective-permute-start.12 = (bf16[4,96,128]{2,1,0:T(8,128)(2,1)S(1)}, bf16[4,96,128]{2,1,0:T(8,128)(2,1)S(1)}, u32[]{:S(2)}, u32[]{:S(2)}) collective-permute-start(bf16[4,96,128]{2,1,0:T(8,128)(2,1)S(1)} %get-tuple-element.51), channel_id=1, source_target_pairs={{0,2},{2,0},{4,6},{6,4},{8,10},{10,8},{12,14},{14,12},{1,3},{3,1},... | collective-permute-start | bytes 294920 | tf_op jit(solution)/shard_map/ppermute | solution.py:261
  27.2 7.1 %collective-permute-start.13 = (bf16[4,96,128]{2,1,0:T(8,128)(2,1)S(1)}, bf16[4,96,128]{2,1,0:T(8,128)(2,1)S(1)}, u32[]{:S(2)}, u32[]{:S(2)}) collective-permute-start(bf16[4,96,128]{2,1,0:T(8,128)(2,1)S(1)} %get-tuple-element.52), channel_id=1, source_target_pairs={{0,4},{2,6},{4,0},{6,2},{8,12},{10,14},{12,8},{14,10},{1,5},{3,7},... | collective-permute-start | bytes 294920 | tf_op jit(solution)/shard_map/ppermute | solution.py:261
  28.7 10.4 %collective-permute-start.6 = (bf16[16,32,128]{2,1,0:T(8,128)(2,1)S(1)}, bf16[16,32,128]{2,1,0:T(8,128)(2,1)S(1)}, u32[]{:S(2)}, u32[]{:S(2)}) collective-permute-start(bf16[16,32,128]{2,1,0:T(8,128)(2,1)S(1)} %get-tuple-element.43), channel_id=1, source_target_pairs={{0,4},{2,6},{4,0},{6,2},{8,12},{10,14},{12,8},{14,10},{1,5},{3,7},... | collective-permute-start | bytes 393224 | tf_op jit(solution)/shard_map/ppermute | solution.py:261
  29.2 12.1 %collective-permute-start.7 = (bf16[16,32,128]{2,1,0:T(8,128)(2,1)S(1)}, bf16[16,32,128]{2,1,0:T(8,128)(2,1)S(1)}, u32[]{:S(2)}, u32[]{:S(2)}) collective-permute-start(bf16[16,32,128]{2,1,0:T(8,128)(2,1)S(1)} %get-tuple-element.44), channel_id=1, source_target_pairs={{0,6},{2,4},{4,2},{6,0},{8,14},{10,12},{12,10},{14,8},{1,7},{3,5},... | collective-permute-start | bytes 393224 | tf_op jit(solution)/shard_map/ppermute | solution.py:261
  32.1 14.9 %collective-permute-start.8 = (bf16[16,32,128]{2,1,0:T(8,128)(2,1)S(1)}, bf16[16,32,128]{2,1,0:T(8,128)(2,1)S(1)}, u32[]{:S(2)}, u32[]{:S(2)}) collective-permute-start(bf16[16,32,128]{2,1,0:T(8,128)(2,1)S(1)} %get-tuple-element.45), channel_id=1, source_target_pairs={{0,8},{2,10},{4,12},{6,14},{8,0},{10,2},{12,4},{14,6},{1,9},{3,11}... | collective-permute-start | bytes 393224 | tf_op jit(solution)/shard_map/ppermute | solution.py:261
  34.3 14.7 %collective-permute-start.9 = (bf16[16,32,128]{2,1,0:T(8,128)(2,1)S(1)}, bf16[16,32,128]{2,1,0:T(8,128)(2,1)S(1)}, u32[]{:S(2)}, u32[]{:S(2)}) collective-permute-start(bf16[16,32,128]{2,1,0:T(8,128)(2,1)S(1)} %get-tuple-element.46), channel_id=1, source_target_pairs={{0,10},{2,8},{4,14},{6,12},{8,2},{10,0},{12,6},{14,4},{1,11},{3,9}... | collective-permute-start | bytes 393224 | tf_op jit(solution)/shard_map/ppermute | solution.py:261
  36.2 12.8 %collective-permute-start.10 = (bf16[16,32,128]{2,1,0:T(8,128)(2,1)S(1)}, bf16[16,32,128]{2,1,0:T(8,128)(2,1)S(1)}, u32[]{:S(2)}, u32[]{:S(2)}) collective-permute-start(bf16[16,32,128]{2,1,0:T(8,128)(2,1)S(1)} %get-tuple-element.47), channel_id=1, source_target_pairs={{0,12},{2,14},{4,8},{6,10},{8,4},{10,6},{12,0},{14,2},{1,13},{3,15... | collective-permute-start | bytes 393224 | tf_op jit(solution)/shard_map/ppermute | solution.py:261
  39.1 27.8 %collective-permute-start.19 = (bf16[6,96,128]{2,1,0:T(8,128)(2,1)S(1)}, bf16[6,96,128]{2,1,0:T(8,128)(2,1)S(1)}, u32[]{:S(2)}, u32[]{:S(2)}) collective-permute-start(bf16[6,96,128]{2,1,0:T(8,128)(2,1)S(1)} %get-tuple-element.59), channel_id=1, source_target_pairs={{0,2},{2,0},{4,6},{6,4},{8,10},{10,8},{12,14},{14,12},{1,3},{3,1},... | collective-permute-start | bytes 442376 | tf_op jit(solution)/shard_map/ppermute | solution.py:261
  41.4 25.5 %collective-permute-start.20 = (bf16[6,96,128]{2,1,0:T(8,128)(2,1)S(1)}, bf16[6,96,128]{2,1,0:T(8,128)(2,1)S(1)}, u32[]{:S(2)}, u32[]{:S(2)}) collective-permute-start(bf16[6,96,128]{2,1,0:T(8,128)(2,1)S(1)} %get-tuple-element.60), channel_id=1, source_target_pairs={{0,4},{2,6},{4,0},{6,2},{8,12},{10,14},{12,8},{14,10},{1,5},{3,7},... | collective-permute-start | bytes 442376 | tf_op jit(solution)/shard_map/ppermute | solution.py:261
  47.0 21.9 %collective-permute-start.26 = (bf16[6,96,128]{2,1,0:T(8,128)(2,1)S(1)}, bf16[6,96,128]{2,1,0:T(8,128)(2,1)S(1)}, u32[]{:S(2)}, u32[]{:S(2)}) collective-permute-start(bf16[6,96,128]{2,1,0:T(8,128)(2,1)S(1)} %get-tuple-element.67), channel_id=1, source_target_pairs={{0,2},{2,0},{4,6},{6,4},{8,10},{10,8},{12,14},{14,12},{1,3},{3,1},... | collective-permute-start | bytes 442376 | tf_op jit(solution)/shard_map/ppermute | solution.py:261
  49.0 20.8 %collective-permute-start.27 = (bf16[6,96,128]{2,1,0:T(8,128)(2,1)S(1)}, bf16[6,96,128]{2,1,0:T(8,128)(2,1)S(1)}, u32[]{:S(2)}, u32[]{:S(2)}) collective-permute-start(bf16[6,96,128]{2,1,0:T(8,128)(2,1)S(1)} %get-tuple-element.68), channel_id=1, source_target_pairs={{0,4},{2,6},{4,0},{6,2},{8,12},{10,14},{12,8},{14,10},{1,5},{3,7},... | collective-permute-start | bytes 442376 | tf_op jit(solution)/shard_map/ppermute | solution.py:261
  49.0 7.8 %collective-permute-start.11 = (bf16[16,32,128]{2,1,0:T(8,128)(2,1)S(1)}, bf16[16,32,128]{2,1,0:T(8,128)(2,1)S(1)}, u32[]{:S(2)}, u32[]{:S(2)}) collective-permute-start(bf16[16,32,128]{2,1,0:T(8,128)(2,1)S(1)} %get-tuple-element.48), channel_id=1, source_target_pairs={{0,14},{2,12},{4,10},{6,8},{8,6},{10,4},{12,2},{14,0},{1,15},{3,13... | collective-permute-start | bytes 393224 | tf_op jit(solution)/shard_map/ppermute | solution.py:261
  56.8 17.8 %collective-permute-start.28 = (bf16[6,96,128]{2,1,0:T(8,128)(2,1)S(1)}, bf16[6,96,128]{2,1,0:T(8,128)(2,1)S(1)}, u32[]{:S(2)}, u32[]{:S(2)}) collective-permute-start(bf16[6,96,128]{2,1,0:T(8,128)(2,1)S(1)} %get-tuple-element.69), channel_id=1, source_target_pairs={{0,6},{2,4},{4,2},{6,0},{8,14},{10,12},{12,10},{14,8},{1,7},{3,5},... | collective-permute-start | bytes 442376 | tf_op jit(solution)/shard_map/ppermute | solution.py:261
  66.8 18.8 %collective-permute-start.29 = (bf16[6,96,128]{2,1,0:T(8,128)(2,1)S(1)}, bf16[6,96,128]{2,1,0:T(8,128)(2,1)S(1)}, u32[]{:S(2)}, u32[]{:S(2)}) collective-permute-start(bf16[6,96,128]{2,1,0:T(8,128)(2,1)S(1)} %get-tuple-element.70), channel_id=1, source_target_pairs={{0,8},{2,10},{4,12},{6,14},{8,0},{10,2},{12,4},{14,6},{1,9},{3,11}... | collective-permute-start | bytes 442376 | tf_op jit(solution)/shard_map/ppermute | solution.py:261
  66.8 23.4 %collective-permute-start.30 = (bf16[6,96,128]{2,1,0:T(8,128)(2,1)S(1)}, bf16[6,96,128]{2,1,0:T(8,128)(2,1)S(1)}, u32[]{:S(2)}, u32[]{:S(2)}) collective-permute-start(bf16[6,96,128]{2,1,0:T(8,128)(2,1)S(1)} %get-tuple-element.71), channel_id=1, source_target_pairs={{0,10},{2,8},{4,14},{6,12},{8,2},{10,0},{12,6},{14,4},{1,11},{3,9}... | collective-permute-start | bytes 442376 | tf_op jit(solution)/shard_map/ppermute | solution.py:261
  68.9 21.3 %collective-permute-start.31 = (bf16[6,96,128]{2,1,0:T(8,128)(2,1)S(1)}, bf16[6,96,128]{2,1,0:T(8,128)(2,1)S(1)}, u32[]{:S(2)}, u32[]{:S(2)}) collective-permute-start(bf16[6,96,128]{2,1,0:T(8,128)(2,1)S(1)} %get-tuple-element.72), channel_id=1, source_target_pairs={{0,12},{2,14},{4,8},{6,10},{8,4},{10,6},{12,0},{14,2},{1,13},{3,15... | collective-permute-start | bytes 442376 | tf_op jit(solution)/shard_map/ppermute | solution.py:261
  69.8 20.4 %collective-permute-start.32 = (bf16[6,96,128]{2,1,0:T(8,128)(2,1)S(1)}, bf16[6,96,128]{2,1,0:T(8,128)(2,1)S(1)}, u32[]{:S(2)}, u32[]{:S(2)}) collective-permute-start(bf16[6,96,128]{2,1,0:T(8,128)(2,1)S(1)} %get-tuple-element.73), channel_id=1, source_target_pairs={{0,14},{2,12},{4,10},{6,8},{8,6},{10,4},{12,2},{14,0},{1,15},{3,13... | collective-permute-start | bytes 442376 | tf_op jit(solution)/shard_map/ppermute | solution.py:261
  74.6 22.2 %collective-permute-start.21 = (bf16[6,96,128]{2,1,0:T(8,128)(2,1)S(1)}, bf16[6,96,128]{2,1,0:T(8,128)(2,1)S(1)}, u32[]{:S(2)}, u32[]{:S(2)}) collective-permute-start(bf16[6,96,128]{2,1,0:T(8,128)(2,1)S(1)} %get-tuple-element.61), channel_id=1, source_target_pairs={{0,6},{2,4},{4,2},{6,0},{8,14},{10,12},{12,10},{14,8},{1,7},{3,5},... | collective-permute-start | bytes 442376 | tf_op jit(solution)/shard_map/ppermute | solution.py:261
  85.6 22.9 %collective-permute-start.22 = (bf16[6,96,128]{2,1,0:T(8,128)(2,1)S(1)}, bf16[6,96,128]{2,1,0:T(8,128)(2,1)S(1)}, u32[]{:S(2)}, u32[]{:S(2)}) collective-permute-start(bf16[6,96,128]{2,1,0:T(8,128)(2,1)S(1)} %get-tuple-element.62), channel_id=1, source_target_pairs={{0,8},{2,10},{4,12},{6,14},{8,0},{10,2},{12,4},{14,6},{1,9},{3,11}... | collective-permute-start | bytes 442376 | tf_op jit(solution)/shard_map/ppermute | solution.py:261
  90.2 21.7 %collective-permute-start.23 = (bf16[6,96,128]{2,1,0:T(8,128)(2,1)S(1)}, bf16[6,96,128]{2,1,0:T(8,128)(2,1)S(1)}, u32[]{:S(2)}, u32[]{:S(2)}) collective-permute-start(bf16[6,96,128]{2,1,0:T(8,128)(2,1)S(1)} %get-tuple-element.63), channel_id=1, source_target_pairs={{0,10},{2,8},{4,14},{6,12},{8,2},{10,0},{12,6},{14,4},{1,11},{3,9}... | collective-permute-start | bytes 442376 | tf_op jit(solution)/shard_map/ppermute | solution.py:261
  90.2 23.2 %collective-permute-start.24 = (bf16[6,96,128]{2,1,0:T(8,128)(2,1)S(1)}, bf16[6,96,128]{2,1,0:T(8,128)(2,1)S(1)}, u32[]{:S(2)}, u32[]{:S(2)}) collective-permute-start(bf16[6,96,128]{2,1,0:T(8,128)(2,1)S(1)} %get-tuple-element.64), channel_id=1, source_target_pairs={{0,12},{2,14},{4,8},{6,10},{8,4},{10,6},{12,0},{14,2},{1,13},{3,15... | collective-permute-start | bytes 442376 | tf_op jit(solution)/shard_map/ppermute | solution.py:261
  90.2 23.2 %collective-permute-start.25 = (bf16[6,96,128]{2,1,0:T(8,128)(2,1)S(1)}, bf16[6,96,128]{2,1,0:T(8,128)(2,1)S(1)}, u32[]{:S(2)}, u32[]{:S(2)}) collective-permute-start(bf16[6,96,128]{2,1,0:T(8,128)(2,1)S(1)} %get-tuple-element.65), channel_id=1, source_target_pairs={{0,14},{2,12},{4,10},{6,8},{8,6},{10,4},{12,2},{14,0},{1,15},{3,13... | collective-permute-start | bytes 442376 | tf_op jit(solution)/shard_map/ppermute | solution.py:261
  96.8 22.0 %collective-permute-start.14 = (bf16[4,96,128]{2,1,0:T(8,128)(2,1)S(1)}, bf16[4,96,128]{2,1,0:T(8,128)(2,1)S(1)}, u32[]{:S(2)}, u32[]{:S(2)}) collective-permute-start(bf16[4,96,128]{2,1,0:T(8,128)(2,1)S(1)} %get-tuple-element.53), channel_id=1, source_target_pairs={{0,6},{2,4},{4,2},{6,0},{8,14},{10,12},{12,10},{14,8},{1,7},{3,5},... | collective-permute-start | bytes 294920 | tf_op jit(solution)/shard_map/ppermute | solution.py:261
  108.5 14.4 %collective-permute-start.15 = (bf16[4,96,128]{2,1,0:T(8,128)(2,1)S(1)}, bf16[4,96,128]{2,1,0:T(8,128)(2,1)S(1)}, u32[]{:S(2)}, u32[]{:S(2)}) collective-permute-start(bf16[4,96,128]{2,1,0:T(8,128)(2,1)S(1)} %get-tuple-element.54), channel_id=1, source_target_pairs={{0,8},{2,10},{4,12},{6,14},{8,0},{10,2},{12,4},{14,6},{1,9},{3,11}... | collective-permute-start | bytes 294920 | tf_op jit(solution)/shard_map/ppermute | solution.py:261
  111.9 11.7 %collective-permute-start.16 = (bf16[4,96,128]{2,1,0:T(8,128)(2,1)S(1)}, bf16[4,96,128]{2,1,0:T(8,128)(2,1)S(1)}, u32[]{:S(2)}, u32[]{:S(2)}) collective-permute-start(bf16[4,96,128]{2,1,0:T(8,128)(2,1)S(1)} %get-tuple-element.55), channel_id=1, source_target_pairs={{0,10},{2,8},{4,14},{6,12},{8,2},{10,0},{12,6},{14,4},{1,11},{3,9}... | collective-permute-start | bytes 294920 | tf_op jit(solution)/shard_map/ppermute | solution.py:261
  113.5 10.2 %collective-permute-start.17 = (bf16[4,96,128]{2,1,0:T(8,128)(2,1)S(1)}, bf16[4,96,128]{2,1,0:T(8,128)(2,1)S(1)}, u32[]{:S(2)}, u32[]{:S(2)}) collective-permute-start(bf16[4,96,128]{2,1,0:T(8,128)(2,1)S(1)} %get-tuple-element.56), channel_id=1, source_target_pairs={{0,12},{2,14},{4,8},{6,10},{8,4},{10,6},{12,0},{14,2},{1,13},{3,15... | collective-permute-start | bytes 294920 | tf_op jit(solution)/shard_map/ppermute | solution.py:261
  113.5 10.1 %collective-permute-start.18 = (bf16[4,96,128]{2,1,0:T(8,128)(2,1)S(1)}, bf16[4,96,128]{2,1,0:T(8,128)(2,1)S(1)}, u32[]{:S(2)}, u32[]{:S(2)}) collective-permute-start(bf16[4,96,128]{2,1,0:T(8,128)(2,1)S(1)} %get-tuple-element.57), channel_id=1, source_target_pairs={{0,14},{2,12},{4,10},{6,8},{8,6},{10,4},{12,2},{14,0},{1,15},{3,13... | collective-permute-start | bytes 294920 | tf_op jit(solution)/shard_map/ppermute | solution.py:261
  125.6 1.4 collective-permute-start.33
  127.0 4.3 %collective-permute-start.34 = (f32[4,32,128]{2,1,0:T(8,128)S(1)}, f32[4,32,128]{2,1,0:T(8,128)S(1)}, u32[]{:S(2)}, u32[]{:S(2)}) collective-permute-start(f32[4,32,128]{2,1,0:T(8,128)S(1)} %slice_add_fusion), channel_id=1, source_target_pairs={{0,2},{2,0},{4,6},{6,4},{8,10},{10,8},{12,14},{14,12},{1,3},{3,1},... | collective-permute-start | bytes 196616 | tf_op jit(solution)/shard_map/ppermute | solution.py:261
  132.0 5.5 %collective-permute-start.37 = (f32[32,128]{1,0:T(8,128)S(1)}, f32[32,128]{1,0:T(8,128)S(1)}, u32[]{:S(2)}, u32[]{:S(2)}) collective-permute-start(f32[32,128]{1,0:T(8,128)S(1)} %get-tuple-element.77), channel_id=1, source_target_pairs={{0,12},{2,14},{4,8},{6,10},{8,4},{10,6},{12,0},{14,2},{1,13},{3,15... | collective-permute-start | bytes 49160 | tf_op jit(solution)/shard_map/ppermute | solution.py:261
  134.7 4.6 %collective-permute-start.36 = (f32[32,128]{1,0:T(8,128)S(1)}, f32[32,128]{1,0:T(8,128)S(1)}, u32[]{:S(2)}, u32[]{:S(2)}) collective-permute-start(f32[32,128]{1,0:T(8,128)S(1)} %get-tuple-element.78), channel_id=1, source_target_pairs={{0,8},{2,10},{4,12},{6,14},{8,0},{10,2},{12,4},{14,6},{1,9},{3,11}... | collective-permute-start | bytes 49160 | tf_op jit(solution)/shard_map/ppermute | solution.py:261
  137.4 3.7 %collective-permute-start.35 = (f32[32,128]{1,0:T(8,128)S(1)}, f32[32,128]{1,0:T(8,128)S(1)}, u32[]{:S(2)}, u32[]{:S(2)}) collective-permute-start(f32[32,128]{1,0:T(8,128)S(1)} %get-tuple-element.79), channel_id=1, source_target_pairs={{0,4},{2,6},{4,0},{6,2},{8,12},{10,14},{12,8},{14,10},{1,5},{3,7},... | collective-permute-start | bytes 49160 | tf_op jit(solution)/shard_map/ppermute | solution.py:261
  137.6 3.6 %copy-start.4 = (f32[32,128]{1,0:T(8,128)}, f32[32,128]{1,0:T(8,128)S(1)}, u32[]{:S(2)}) copy-start(f32[32,128]{1,0:T(8,128)S(1)} %collective-permute-done.37.refs_3_) | copy-start | bytes 49156
  139.3 1.8 %copy-start.5 = (f32[32,128]{1,0:T(8,128)}, f32[32,128]{1,0:T(8,128)S(1)}, u32[]{:S(2)}) copy-start(f32[32,128]{1,0:T(8,128)S(1)} %collective-permute-done.36.refs_2_) | copy-start | bytes 49156
  141.2 0.6 copy-start.6

commit v2 on v1

--- a/solution.py
+++ b/solution.py
@@ -10,6 +10,7 @@
 F32 = jnp.float32
 BF16 = jnp.bfloat16
 ROWS = 16
+WINDOW = 5
 WHOLE = pl.BlockSpec(memory_space=pltpu.VMEM)
 
 
@@ -75,8 +76,8 @@
         outs[k][...] = value[k * share : (k + 1) * share]
 
 
-def first_products(chips, where, own, other, moved):
-    first, depth, width = moved.shape
+def first_products(chips, where, own, other, moved, first):
+    _, depth, width = moved.shape
     orbitals = own.shape[1]
     share = orbitals // chips
     whole = lambda shape: pl.BlockSpec(shape, lambda j, w: (0,) * len(shape))
@@ -102,35 +103,35 @@
     )(where, own, other, moved)
 
 
-def rest_kernel(chips, groups, x_ref, table_ref, *outs):
+def rest_kernel(chips, spans, x_ref, table_ref, _, *outs):
     slots, depth, rows, width = x_ref.shape
     block = jnp.swapaxes(x_ref[...].reshape(slots * depth, rows, width), 0, 1)
     value = products(table_ref[...], block)
     share = table_ref.shape[0] // chips
-    for g, (lo, hi) in enumerate(groups):
-        for k in range(chips):
-            outs[g * chips + k][...] = value[k * share + lo : k * share + hi]
-
-
-def rest_products(chips, groups, integrals, table, first):
+    for (k, lo, hi), out in zip(spans, outs):
+        out[...] = value[k * share + lo : k * share + hi]
+
+
+def rest_products(chips, spans, integrals, table, first, after):
     slots, depth, total, width = integrals.shape
     orbitals = table.shape[0]
     rest = total - first
     skip = first // ROWS
-    shapes = [(hi - lo) for lo, hi in groups for _ in range(chips)]
-    return pl.pallas_call(
-        functools.partial(rest_kernel, chips, groups),
+    shapes = [hi - lo for _, lo, hi in spans]
+    return pl.pallas_call(
+        functools.partial(rest_kernel, chips, spans),
         grid=(rest // ROWS,),
         in_specs=[
             pl.BlockSpec((slots, depth, ROWS, width), lambda j: (0, 0, j + skip, 0)),
             pl.BlockSpec(table.shape, lambda j: (0, 0)),
+            pl.BlockSpec(memory_space=pl.ANY),
         ],
         out_specs=[pl.BlockSpec((n, ROWS, width), lambda j: (0, j, 0)) for n in shapes],
         out_shape=[jax.ShapeDtypeStruct((n, rest, width), BF16) for n in shapes],
         compiler_params=params(),
         cost_estimate=cost(orbitals * table.shape[1] * rest * width, integrals.size * 2),
         name="rest_products",
-    )(integrals, table)
+    )(integrals, table, after)
 
 
 def metric_kernel(where, own_ref, near_ref, far_ref, o_ref):
@@ -158,12 +159,12 @@
     )(where, own, near, far)
 
 
-def add_group(aux, bas, lo, hi, metric, early, late, total):
+def add_group(aux, bas, lo, hi, starts, metric, early, late, total):
     chips = aux * bas
     for i in range(lo, hi):
         columns = []
         for k in range(chips):
-            columns.append(jnp.concatenate([early[k][i], late[k][i - lo]], axis=0))
+            columns.append(jnp.concatenate([early[k][i], late[k][starts[k] + i - lo]], axis=0))
         stacked = jnp.concatenate(
             [jnp.concatenate(columns[kz * bas : (kz + 1) * bas], axis=1) for kz in range(aux)],
             axis=0,
@@ -175,7 +176,7 @@
     return total
 
 
-def group_kernel(aux, bas, lo, hi, started, last, *refs):
+def group_kernel(aux, bas, lo, hi, starts, started, last, *refs):
     chips = aux * bas
     refs = list(refs)
     where = refs.pop(0) if last else None
@@ -184,7 +185,7 @@
     late = [refs.pop(0) for _ in range(chips)]
     side = bas * late[0].shape[2]
     total = refs.pop(0)[...] if started else jnp.zeros((side, side), F32)
-    total = add_group(aux, bas, lo, hi, metric, early, late, total)
+    total = add_group(aux, bas, lo, hi, starts, metric, early, late, total)
     if not last:
         refs[0][...] = total
         return
@@ -207,6 +208,8 @@
 
 
 def group(aux, bas, lo, hi, metric, early, late, total, where=None):
+    starts = tuple(start for _, start in late)
+    late = [value for value, _ in late]
     last, started = where is not None, total is not None
     width = late[0].shape[2]
     side = bas * width
@@ -225,7 +228,7 @@
     rows = metric.shape[0]
     macs = (hi - lo) * (rows * rows * side + rows * side * side)
     return pl.pallas_call(
-        functools.partial(group_kernel, aux, bas, lo, hi, started, last),
+        functools.partial(group_kernel, aux, bas, lo, hi, starts, started, last),
         in_specs=specs,
         out_specs=[WHOLE] * 3 if last else WHOLE,
         out_shape=out,
@@ -234,13 +237,6 @@
         cost_estimate=cost(macs, (hi - lo) * rows * side * 2),
         name="group",
     )(*args)
-
-
-def turn_kernel(*refs):
-    total = refs[0][...]
-    for ref in refs[1:-1]:
-        total = total + ref[...]
-    refs[-1][...] = total.T
 
 
 def per_device(integrals, screening, coefficients, metric, aux_owner):
@@ -253,6 +249,7 @@
     a, b, o = (lax.axis_index(name) for name in ("aux", "bas", "occ"))
     first = integrals.shape[2] // 4
     groups = ((0, 6), (6, 12), (12, share))
+    inner, outer = (1, 2, 3), (4, 5, 6, 7)
 
     def swap(value, kz=0, kx=0):
         pairs = [
@@ -263,48 +260,66 @@
     def across(value):
         return lax.ppermute(value, "occ", [(0, 1), (1, 0)])
 
+    def after(value, *earlier):
+        return lax.optimization_barrier((value, *earlier))[0]
+
+    integrals = pltpu.with_memory_space_constraint(integrals, pltpu.HBM)
     other = swap(coefficients, kx=1)
-    rows = metric.shape[0] // 2
-    half = lax.dynamic_slice_in_dim(metric, o * rows, rows, axis=0)
-    near = jnp.concatenate([swap(half, kz=kz) for kz in range(1, aux)], axis=0)
+    moved = relayout(integrals, first)
+
+    rows = metric.shape[0] // 4
+    part = lax.dynamic_slice_in_dim(after(metric, moved), (b * 2 + o) * rows, rows, axis=0)
+    pieces = [swap(part, kz=kz) for kz in range(1, aux)]
+    where = jnp.concatenate([jnp.stack([a * bas + b, b]), screening[0, 0]]).astype(jnp.int32)
+    *early, table = first_products(
+        chips, where, after(coefficients, *pieces), other, moved, first
+    )
+
+    sent = []
+
+    def send(k, value):
+        if len(sent) >= WINDOW:
+            value = after(value, sent[-WINDOW])
+        sent.append(swap(value, k // bas, k % bas))
+        return sent[-1]
+
+    spans = [(k, lo, hi) for lo, hi in groups for k in outer]
+    spans += [(k, 0, share) for k in (0, *inner)]
+    got = {k: send(k, early[k]) for k in (4, 5, 1, 6, 7)}
+    late = rest_products(chips, tuple(spans), integrals, table, first, got[1])
+    for k in (2, 3):
+        got[k] = send(k, after(early[k], late[0]))
+    got[0] = early[0]
+    made = dict(zip(spans, late))
+    here = {(0, 0, share): made[0, 0, share]}
+    for g, (lo, hi) in enumerate(groups):
+        for at, k in enumerate(outer):
+            here[k, lo, hi] = send(k, made[k, lo, hi])
+            if g == 0 and at:
+                here[at, 0, share] = send(at, made[at, 0, share])
+
+    near = jnp.concatenate(pieces, axis=0)
+    near = jnp.concatenate([near, swap(near, kx=1)], axis=0)
     far = across(near)
     ordered = ordered_metric(
         jnp.concatenate([aux_owner, a[None]]).astype(jnp.int32), metric, near, far
     )
-
-    moved = relayout(integrals, first)
-    where = jnp.concatenate([jnp.stack([a * bas + b, b]), screening[0, 0]]).astype(jnp.int32)
-    *early, table = first_products(chips, where, coefficients, other, moved)
-    late = rest_products(chips, groups, integrals, table, first)
-
-    order = sorted(range(1, chips), key=lambda k: -(k // bas in (2, 3)))
-
-    def spread(values):
-        got = {0: values[0]}
-        for k in order:
-            got[k] = swap(values[k], k // bas, k % bas)
-        return [got[k] for k in range(chips)]
-
-    early = spread(early)
+    early = [got[k] for k in range(chips)]
     total = None
     for g, (lo, hi) in enumerate(groups):
-        part = spread(late[g * chips : (g + 1) * chips])
-        here = jnp.stack([a, b, o]).astype(jnp.int32) if g == len(groups) - 1 else None
-        total = group(aux, bas, lo, hi, ordered, early, part, total, here)
+        part = [(here[k, 0, share], lo) if k < 4 else (here[k, lo, hi], 0) for k in range(chips)]
+        place = jnp.stack([a, b, o]).astype(jnp.int32) if g == len(groups) - 1 else None
+        total = group(aux, bas, lo, hi, ordered, early, part, total, place)
     kept, near, away = total
     away = across(away)
     width = kept.shape[2]
     kept = kept + away[:, :, :width]
     near = near + away[:, :, width:]
     kept = kept + swap(near, kx=1)
-    pieces = [kept[0]] + [swap(kept[kz], kz=kz) for kz in range(1, aux)]
-    return pl.pallas_call(
-        turn_kernel,
-        in_specs=[WHOLE] * aux,
-        out_specs=WHOLE,
-        out_shape=jax.ShapeDtypeStruct((width, kept.shape[1]), F32),
-        name="turn",
-    )(*pieces)
+    value = kept[0]
+    for kz in range(1, aux):
+        value = value + swap(kept[kz], kz=kz)
+    return value.T
 
 
 def plain_device(integrals, screening, coefficients, metric, aux_owner):

time: 145 us -> 126 us (0.87)
  starting transfers between devices: 70.4 us -> 56.6 us
  local copies, waits for them, and re-layouts: 10.4 us -> 0.05 us
  waiting for transfers between devices: 46.8 us -> 50.4 us
    ppermute x36 -> x31, starting transfers between devices: 70.3 us -> 56.4 us  [swap(): return lax.ppermute(value, ('aux', 'bas'), pairs)]
    unnamed x20 -> x11, local copies, waits for them, and re-layouts: 7.39 us -> 0.03 us
    ppermute x36 -> x31, waiting for transfers between devices: 45.5 us -> 49.1 us  [swap(): return lax.ppermute(value, ('aux', 'bas'), pairs)]
    pallas_call x1 -> x0, local copies, waits for them, and re-layouts: 1.52 us -> none  [per_device(): pl.pallas_call(turn_kernel, in_specs=[WHOLE] * aux, out_specs=WHOLE, out_...]
    pallas_call x5 -> x4, Pallas kernels: 13.3 us -> 13.1 us  [the longest x1 7.03 us: rest_products(): pl.pallas_call(functools.partial(rest_kernel, chips, spans), grid=(rest /...]
  transfers between devices with their start and end apart: 38 -> 33, of which waited for: 16 -> 15; matrix products, arithmetic and copies ran while one was open for 0% -> 0% of each run, Pallas kernels for 9% -> 11%
where the time goes in v2:
time: 126 us
  starting transfers between devices  56.6 us (45%)
  waiting for transfers between devices  50.4 us (40%)
  Pallas kernels  17.4 us (14%)
    ppermute x31, starting transfers between devices, swap(): return lax.ppermute(value, ('aux', 'bas'), pairs)  56.4 us
    ppermute x31, waiting for transfers between devices, swap(): return lax.ppermute(value, ('aux', 'bas'), pairs)  49.1 us
    pallas_call x1, Pallas kernels, rest_products(): pl.pallas_call(functools.partial(rest_kernel, chips, spans), grid=(rest /...  7.03 us
    pallas_call x3, Pallas kernels, group(): pl.pallas_call(functools.partial(group_kernel, aux, bas, lo, hi, starts,...  6.03 us
  transfers between devices with their start and end apart: 33, of which 15 were waited for; matrix products, arithmetic and copies ran while one was open for 0% of the time, Pallas kernels for 11%

profile of v2, /device:TPU:0, one launch (start us, length us, event | category | flops | bytes accessed | tf_op | source)
XLA Modules:
  0.0 125.6 jit_solution(1248543785356837506)
XLA Ops:
  0.0 3.0 %collective-permute-start.5 = (bf16[1024,128]{1,0:T(8,128)(2,1)}, bf16[1024,128]{1,0:T(8,128)(2,1)S(1)}, u32[]{:S(2)}, u32[]{:S(2)}) collective-permute-start(bf16[1024,128]{1,0:T(8,128)(2,1)} %own_ref.2), channel_id=1, source_target_pairs={{0,2},{2,0},{4,6},{6,4},{8,10},{10,8},{12,14},{14,12},{1,3},{3,1},... | collective-permute-start | bytes 786440 | tf_op jit(solution)/shard_map/ppermute | solution.py:258
  3.0 2.0 %relayout.1.x_ref = bf16[32,256,128]{2,1,0:T(8,128)(2,1)S(1)} custom-call(bf16[2,128,128,128]{3,2,1,0:T(8,128)(2,1)} %bitcast.24), custom_call_target="tpu_custom_call" | custom-call | bytes 4194304 | tf_op jit(solution)/shard_map/relayout/pallas_call | solution.py:32
  5.1 1.6 %collective-permute-start = (bf16[32,512]{1,0:T(8,128)(2,1)S(1)}, bf16[32,512]{1,0:T(8,128)(2,1)S(1)}, u32[]{:S(2)}, u32[]{:S(2)}) collective-permute-start(bf16[32,512]{1,0:T(8,128)(2,1)S(1)} %constant_dynamic-slice_fusion), channel_id=1, source_target_pairs={{0,4},{2,6},{4,0},{6,2},{8,12},{10,14},{12,8},{14,10},{1,5},{3,7},... | collective-permute-start | bytes 98312 | tf_op jit(solution)/shard_map/ppermute | solution.py:258
  6.7 2.6 %collective-permute-start.1 = (bf16[32,512]{1,0:T(8,128)(2,1)S(1)}, bf16[32,512]{1,0:T(8,128)(2,1)S(1)}, u32[]{:S(2)}, u32[]{:S(2)}) collective-permute-start(bf16[32,512]{1,0:T(8,128)(2,1)S(1)} %constant_dynamic-slice_fusion), channel_id=1, source_target_pairs={{0,8},{2,10},{4,12},{6,14},{8,0},{10,2},{12,4},{14,6},{1,9},{3,11}... | collective-permute-start | bytes 98312 | tf_op jit(solution)/shard_map/ppermute | solution.py:258
  9.3 0.2 collective-permute-start.2
  9.6 2.2 %collective-permute-done.1 = bf16[32,512]{1,0:T(8,128)(2,1)S(1)} collective-permute-done((bf16[32,512]{1,0:T(8,128)(2,1)S(1)}, bf16[32,512]{1,0:T(8,128)(2,1)S(1)}, u32[]{:S(2)}, u32[]{:S(2)}) %collective-permute-start.1) | collective-permute-done | bytes 32800 | tf_op jit(solution)/shard_map/ppermute | solution.py:258
  11.8 3.2 %collective-permute-done.2 = bf16[32,512]{1,0:T(8,128)(2,1)S(1)} collective-permute-done((bf16[32,512]{1,0:T(8,128)(2,1)S(1)}, bf16[32,512]{1,0:T(8,128)(2,1)S(1)}, u32[]{:S(2)}, u32[]{:S(2)}) %collective-permute-start.2) | collective-permute-done | bytes 32800 | tf_op jit(solution)/shard_map/ppermute | solution.py:258
  15.0 1.7 %first_products.1 = (bf16[16,32,128]{2,1,0:T(8,128)(2,1)S(1)}, bf16[16,32,128]{2,1,0:T(8,128)(2,1)S(1)}, bf16[16,32,128]{2,1,0:T(8,128)(2,1)S(1)}, bf16[16,32,12...) custom-call(s32[4]{0:T(128)S(1)} %pad_add_fusion.2.where, ...), custom_call_target="tpu_custom_call" | custom-call | flops 268435456 | bytes 2097152 | tf_op jit(solution)/shard_map/first_products/pallas_call | solution.py:84
  16.7 0.6 collective-permute-start.6
  17.4 3.8 %collective-permute-start.9 = (bf16[16,32,128]{2,1,0:T(8,128)(2,1)S(1)}, bf16[16,32,128]{2,1,0:T(8,128)(2,1)S(1)}, u32[]{:S(2)}, u32[]{:S(2)}) collective-permute-start(bf16[16,32,128]{2,1,0:T(8,128)(2,1)S(1)} %get-tuple-element.66), channel_id=1, source_target_pairs={{0,10},{2,8},{4,14},{6,12},{8,2},{10,0},{12,6},{14,4},{1,11},{3,9}... | collective-permute-start | bytes 393224 | tf_op jit(solution)/shard_map/ppermute | solution.py:258
  21.2 0.4 collective-permute-start.11
  21.6 3.4 %collective-permute-start.12 = (bf16[16,32,128]{2,1,0:T(8,128)(2,1)S(1)}, bf16[16,32,128]{2,1,0:T(8,128)(2,1)S(1)}, u32[]{:S(2)}, u32[]{:S(2)}) collective-permute-start(bf16[16,32,128]{2,1,0:T(8,128)(2,1)S(1)} %get-tuple-element.69), channel_id=1, source_target_pairs={{0,14},{2,12},{4,10},{6,8},{8,6},{10,4},{12,2},{14,0},{1,15},{3,13... | collective-permute-start | bytes 393224 | tf_op jit(solution)/shard_map/ppermute | solution.py:258
  25.1 7.0 %rest_products.1 = (bf16[6,96,128]{2,1,0:T(8,128)(2,1)S(1)}, bf16[6,96,128]{2,1,0:T(8,128)(2,1)S(1)}, bf16[6,96,128]{2,1,0:T(8,128)(2,1)S(1)}, bf16[6,96,128]{2,...) custom-call(bf16[2,128,128,128]{3,2,1,0:T(8,128)(2,1)} %bitcast.25, ...), custom_call_target="tpu_custom_call" | custom-call | flops 805306368 | bytes 8388608 | tf_op jit(solution)/shard_map/rest_products/pallas_call | solution.py:121
  32.2 2.0 %collective-permute-done.7.refs_5_.refs_6_ = bf16[16,32,128]{2,1,0:T(8,128)(2,1)S(1)} collective-permute-done((bf16[16,32,128]{2,1,0:T(8,128)(2,1)S(1)}, bf16[16,32,128]{2,1,0:T(8,128)(2,1)S(1)}, u32[]{:S(2)}, u32[]{:S(2)}) %collective-permute-start.7) | collective-permute-done | bytes 131104 | tf_op jit(solution)/shard_map/ppermute | solution.py:258
  34.2 4.4 %collective-permute-done.9.refs_6_.refs_7_ = bf16[16,32,128]{2,1,0:T(8,128)(2,1)S(1)} collective-permute-done((bf16[16,32,128]{2,1,0:T(8,128)(2,1)S(1)}, bf16[16,32,128]{2,1,0:T(8,128)(2,1)S(1)}, u32[]{:S(2)}, u32[]{:S(2)}) %collective-permute-start.9) | collective-permute-done | bytes 131104 | tf_op jit(solution)/shard_map/ppermute | solution.py:258
  38.5 5.0 %collective-permute-start.15 = (bf16[6,96,128]{2,1,0:T(8,128)(2,1)S(1)}, bf16[6,96,128]{2,1,0:T(8,128)(2,1)S(1)}, u32[]{:S(2)}, u32[]{:S(2)}) collective-permute-start(bf16[6,96,128]{2,1,0:T(8,128)(2,1)S(1)} %get-tuple-element.77), channel_id=1, source_target_pairs={{0,10},{2,8},{4,14},{6,12},{8,2},{10,0},{12,6},{14,4},{1,11},{3,9}... | collective-permute-start | bytes 442376 | tf_op jit(solution)/shard_map/ppermute | solution.py:258
  43.6 0.7 collective-permute-start.13
  44.2 1.4 %collective-permute-start.3 = (bf16[96,512]{1,0:T(8,128)(2,1)S(1)}, bf16[96,512]{1,0:T(8,128)(2,1)S(1)}, u32[]{:S(2)}, u32[]{:S(2)}) collective-permute-start(bf16[96,512]{1,0:T(8,128)(2,1)S(1)} %pad_maximum_fusion), channel_id=1, source_target_pairs={{0,2},{2,0},{4,6},{6,4},{8,10},{10,8},{12,14},{14,12},{1,3},{3,1},... | collective-permute-start | bytes 294920 | tf_op jit(solution)/shard_map/ppermute | solution.py:258
  45.6 2.5 %collective-permute-start.20 = (bf16[6,96,128]{2,1,0:T(8,128)(2,1)S(1)}, bf16[6,96,128]{2,1,0:T(8,128)(2,1)S(1)}, u32[]{:S(2)}, u32[]{:S(2)}) collective-permute-start(bf16[6,96,128]{2,1,0:T(8,128)(2,1)S(1)} %get-tuple-element.88), channel_id=1, source_target_pairs={{0,12},{2,14},{4,8},{6,10},{8,4},{10,6},{12,0},{14,2},{1,13},{3,15... | collective-permute-start | bytes 442376 | tf_op jit(solution)/shard_map/ppermute | solution.py:258
  48.1 6.3 %collective-permute-done.25.refs_13_ = bf16[6,96,128]{2,1,0:T(8,128)(2,1)S(1)} collective-permute-done((bf16[6,96,128]{2,1,0:T(8,128)(2,1)S(1)}, bf16[6,96,128]{2,1,0:T(8,128)(2,1)S(1)}, u32[]{:S(2)}, u32[]{:S(2)}) %collective-permute-start.25) | collective-permute-done | bytes 147488 | tf_op jit(solution)/shard_map/ppermute | solution.py:258
  54.4 2.9 %collective-permute-done.15.refs_14_ = bf16[6,96,128]{2,1,0:T(8,128)(2,1)S(1)} collective-permute-done((bf16[6,96,128]{2,1,0:T(8,128)(2,1)S(1)}, bf16[6,96,128]{2,1,0:T(8,128)(2,1)S(1)}, u32[]{:S(2)}, u32[]{:S(2)}) %collective-permute-start.15) | collective-permute-done | bytes 147488 | tf_op jit(solution)/shard_map/ppermute | solution.py:258
  57.3 3.1 %collective-permute-start.26 = (bf16[6,96,128]{2,1,0:T(8,128)(2,1)S(1)}, bf16[6,96,128]{2,1,0:T(8,128)(2,1)S(1)}, u32[]{:S(2)}, u32[]{:S(2)}) collective-permute-start(bf16[6,96,128]{2,1,0:T(8,128)(2,1)S(1)} %get-tuple-element.98), channel_id=1, source_target_pairs={{0,14},{2,12},{4,10},{6,8},{8,6},{10,4},{12,2},{14,0},{1,15},{3,13... | collective-permute-start | bytes 442376 | tf_op jit(solution)/shard_map/ppermute | solution.py:258
  60.4 0.2 collective-permute-start.16
  60.7 3.2 %collective-permute-start.21 = (bf16[6,96,128]{2,1,0:T(8,128)(2,1)S(1)}, bf16[6,96,128]{2,1,0:T(8,128)(2,1)S(1)}, u32[]{:S(2)}, u32[]{:S(2)}) collective-permute-start(bf16[6,96,128]{2,1,0:T(8,128)(2,1)S(1)} %get-tuple-element.89), channel_id=1, source_target_pairs={{0,10},{2,8},{4,14},{6,12},{8,2},{10,0},{12,6},{14,4},{1,11},{3,9}... | collective-permute-start | bytes 442376 | tf_op jit(solution)/shard_map/ppermute | solution.py:258
  63.9 3.1 %collective-permute-done.26.refs_16_ = bf16[6,96,128]{2,1,0:T(8,128)(2,1)S(1)} collective-permute-done((bf16[6,96,128]{2,1,0:T(8,128)(2,1)S(1)}, bf16[6,96,128]{2,1,0:T(8,128)(2,1)S(1)}, u32[]{:S(2)}, u32[]{:S(2)}) %collective-permute-start.26) | collective-permute-done | bytes 147488 | tf_op jit(solution)/shard_map/ppermute | solution.py:258
  67.0 8.9 %collective-permute-done.14.refs_11_.refs_12_ = bf16[16,96,128]{2,1,0:T(8,128)(2,1)S(1)} collective-permute-done((bf16[16,96,128]{2,1,0:T(8,128)(2,1)S(1)}, bf16[16,96,128]{2,1,0:T(8,128)(2,1)S(1)}, u32[]{:S(2)}, u32[]{:S(2)}) %collective-permute-start.14) | collective-permute-done | bytes 393248 | tf_op jit(solution)/shard_map/ppermute | solution.py:258
  75.9 2.2 %collective-permute-start.27 = (bf16[6,96,128]{2,1,0:T(8,128)(2,1)S(1)}, bf16[6,96,128]{2,1,0:T(8,128)(2,1)S(1)}, u32[]{:S(2)}, u32[]{:S(2)}) collective-permute-start(bf16[6,96,128]{2,1,0:T(8,128)(2,1)S(1)} %get-tuple-element.99), channel_id=1, source_target_pairs={{0,14},{2,12},{4,10},{6,8},{8,6},{10,4},{12,2},{14,0},{1,15},{3,13... | collective-permute-start | bytes 442376 | tf_op jit(solution)/shard_map/ppermute | solution.py:258
  78.2 0.5 collective-permute-start.23
  78.8 0.6 ordered_metric.1.refs_0_.refs_1_
  79.5 3.4 %collective-permute-start.22 = (bf16[4,96,128]{2,1,0:T(8,128)(2,1)S(1)}, bf16[4,96,128]{2,1,0:T(8,128)(2,1)S(1)}, u32[]{:S(2)}, u32[]{:S(2)}) collective-permute-start(bf16[4,96,128]{2,1,0:T(8,128)(2,1)S(1)} %get-tuple-element.90), channel_id=1, source_target_pairs={{0,12},{2,14},{4,8},{6,10},{8,4},{10,6},{12,0},{14,2},{1,13},{3,15... | collective-permute-start | bytes 294920 | tf_op jit(solution)/shard_map/ppermute | solution.py:258
  82.8 4.2 %collective-permute-start.19 = (bf16[4,96,128]{2,1,0:T(8,128)(2,1)S(1)}, bf16[4,96,128]{2,1,0:T(8,128)(2,1)S(1)}, u32[]{:S(2)}, u32[]{:S(2)}) collective-permute-start(bf16[4,96,128]{2,1,0:T(8,128)(2,1)S(1)} %get-tuple-element.84), channel_id=1, source_target_pairs={{0,10},{2,8},{4,14},{6,12},{8,2},{10,0},{12,6},{14,4},{1,11},{3,9}... | collective-permute-start | bytes 294920 | tf_op jit(solution)/shard_map/ppermute | solution.py:258
  87.0 4.4 %collective-permute-done.16.refs_12_.refs_13_ = bf16[16,96,128]{2,1,0:T(8,128)(2,1)S(1)} collective-permute-done((bf16[16,96,128]{2,1,0:T(8,128)(2,1)S(1)}, bf16[16,96,128]{2,1,0:T(8,128)(2,1)S(1)}, u32[]{:S(2)}, u32[]{:S(2)}) %collective-permute-start.16) | collective-permute-done | bytes 393248 | tf_op jit(solution)/shard_map/ppermute | solution.py:258
  91.4 4.1 %collective-permute-start.17 = (bf16[4,96,128]{2,1,0:T(8,128)(2,1)S(1)}, bf16[4,96,128]{2,1,0:T(8,128)(2,1)S(1)}, u32[]{:S(2)}, u32[]{:S(2)}) collective-permute-start(bf16[4,96,128]{2,1,0:T(8,128)(2,1)S(1)} %get-tuple-element.80), channel_id=1, source_target_pairs={{0,8},{2,10},{4,12},{6,14},{8,0},{10,2},{12,4},{14,6},{1,9},{3,11}... | collective-permute-start | bytes 294920 | tf_op jit(solution)/shard_map/ppermute | solution.py:258
  95.5 2.0 %group.3.refs_17_ = f32[256,256]{1,0:T(8,128)S(1)} custom-call(bf16[512,512]{1,0:T(8,128)(2,1)S(1)} %ordered_metric.1.refs_0_.refs_1_, bf16[16,32,128]{2,1,0:T(8,128)(2,1)S(1)} %get-tuple-element.56.refs_1_.refs_2_, bf16[16,32,128]{2,1,0:T(8,128)(2,1)S(1)} %collective-permute-done.6._.refs_2_.refs_3_, ...), custom_call_target="tpu_custom_call" | custom-call | flops 1207959552 | bytes 1572864 | tf_op jit(solution)/shard_map/group/pallas_call | solution.py:230
  97.5 4.0 %collective-permute-start.24 = (bf16[4,96,128]{2,1,0:T(8,128)(2,1)S(1)}, bf16[4,96,128]{2,1,0:T(8,128)(2,1)S(1)}, u32[]{:S(2)}, u32[]{:S(2)}) collective-permute-start(bf16[4,96,128]{2,1,0:T(8,128)(2,1)S(1)} %get-tuple-element.94), channel_id=1, source_target_pairs={{0,14},{2,12},{4,10},{6,8},{8,6},{10,4},{12,2},{14,0},{1,15},{3,13... | collective-permute-start | bytes 294920 | tf_op jit(solution)/shard_map/ppermute | solution.py:258
  101.5 2.1 %group.4.refs_18_ = f32[256,256]{1,0:T(8,128)S(1)} custom-call(bf16[512,512]{1,0:T(8,128)(2,1)S(1)} %ordered_metric.1.refs_0_.refs_1_, bf16[16,32,128]{2,1,0:T(8,128)(2,1)S(1)} %get-tuple-element.56.refs_1_.refs_2_, bf16[16,32,128]{2,1,0:T(8,128)(2,1)S(1)} %collective-permute-done.6._.refs_2_.refs_3_, ...), custom_call_target="tpu_custom_call" | custom-call | flops 1207959552 | bytes 1572864 | tf_op jit(solution)/shard_map/group/pallas_call | solution.py:230
  103.6 3.2 %collective-permute-done.19.refs_15_ = bf16[4,96,128]{2,1,0:T(8,128)(2,1)S(1)} collective-permute-done((bf16[4,96,128]{2,1,0:T(8,128)(2,1)S(1)}, bf16[4,96,128]{2,1,0:T(8,128)(2,1)S(1)}, u32[]{:S(2)}, u32[]{:S(2)}) %collective-permute-start.19) | collective-permute-done | bytes 98336 | tf_op jit(solution)/shard_map/ppermute | solution.py:258
  106.8 0.9 collective-permute-done.17.refs_14_
  107.7 2.0 %group.5 = (f32[4,32,128]{2,1,0:T(8,128)S(1)}, f32[4,32,128]{2,1,0:T(8,128)S(1)}, f32[4,32,256]{2,1,0:T(8,128)S(1)}) custom-call(s32[3]{0:T(128)S(1)} %pad_add_fusion.refs_0_, bf16[512,512]{1,0:T(8,128)(2,1)S(1)} %ordered_metric.1.refs_0_.refs_1_, bf16[16,32,128]{2,1,0:T(8,128)(2,1)S(1)} %get-tuple-element.56.refs_1_.refs_2_, ...), custom_call_target="tpu_custom_call" | custom-call | flops 805306368 | bytes 1048576 | tf_op jit(solution)/shard_map/group/pallas_call | solution.py:230
  109.7 1.3 %collective-permute-done.28 = f32[4,32,256]{2,1,0:T(8,128)S(1)} collective-permute-done((f32[4,32,256]{2,1,0:T(8,128)S(1)}, f32[4,32,256]{2,1,0:T(8,128)S(1)}, u32[]{:S(2)}, u32[]{:S(2)}) %collective-permute-start.28) | collective-permute-done | bytes 131104 | tf_op jit(solution)/shard_map/ppermute | solution.py:261
  111.1 0.8 collective-permute-start.29
  111.9 3.5 %collective-permute-done.29 = f32[4,32,128]{2,1,0:T(8,128)S(1)} collective-permute-done((f32[4,32,128]{2,1,0:T(8,128)S(1)}, f32[4,32,128]{2,1,0:T(8,128)S(1)}, u32[]{:S(2)}, u32[]{:S(2)}) %collective-permute-start.29) | collective-permute-done | bytes 65568 | tf_op jit(solution)/shard_map/ppermute | solution.py:258
  115.4 1.9 %collective-permute-start.30 = (f32[32,128]{1,0:T(8,128)S(1)}, f32[32,128]{1,0:T(8,128)S(1)}, u32[]{:S(2)}, u32[]{:S(2)}) collective-permute-start(f32[32,128]{1,0:T(8,128)S(1)} %get-tuple-element.103), channel_id=1, source_target_pairs={{0,4},{2,6},{4,0},{6,2},{8,12},{10,14},{12,8},{14,10},{1,5},{3,7},... | collective-permute-start | bytes 49160 | tf_op jit(solution)/shard_map/ppermute | solution.py:258
  117.3 2.1 %collective-permute-start.31 = (f32[32,128]{1,0:T(8,128)S(1)}, f32[32,128]{1,0:T(8,128)S(1)}, u32[]{:S(2)}, u32[]{:S(2)}) collective-permute-start(f32[32,128]{1,0:T(8,128)S(1)} %get-tuple-element.105), channel_id=1, source_target_pairs={{0,8},{2,10},{4,12},{6,14},{8,0},{10,2},{12,4},{14,6},{1,9},{3,11}... | collective-permute-start | bytes 49160 | tf_op jit(solution)/shard_map/ppermute | solution.py:258
  119.4 1.4 %collective-permute-start.32 = (f32[32,128]{1,0:T(8,128)S(1)}, f32[32,128]{1,0:T(8,128)S(1)}, u32[]{:S(2)}, u32[]{:S(2)}) collective-permute-start(f32[32,128]{1,0:T(8,128)S(1)} %get-tuple-element.104), channel_id=1, source_target_pairs={{0,12},{2,14},{4,8},{6,10},{8,4},{10,6},{12,0},{14,2},{1,13},{3,15... | collective-permute-start | bytes 49160 | tf_op jit(solution)/shard_map/ppermute | solution.py:258
  120.8 1.2 collective-permute-done.31
  122.0 2.9 %collective-permute-done.32 = f32[32,128]{1,0:T(8,128)S(1)} collective-permute-done((f32[32,128]{1,0:T(8,128)S(1)}, f32[32,128]{1,0:T(8,128)S(1)}, u32[]{:S(2)}, u32[]{:S(2)}) %collective-permute-start.32) | collective-permute-done | bytes 16416 | tf_op jit(solution)/shard_map/ppermute | solution.py:258
  124.9 0.6 fusion.4
  (46 shorter events, 0.6 us)
Async XLA Ops:
  0.0 15.0 %copy-start = (bf16[1024,128]{1,0:T(8,128)(2,1)S(1)}, bf16[1024,128]{1,0:T(8,128)(2,1)}, u32[]{:S(2)}) copy-start(bf16[1024,128]{1,0:T(8,128)(2,1)} %own_ref.2) | copy-start | bytes 786436
  0.0 5.1 %copy-start.1 = (bf16[128,512]{1,0:T(8,128)(2,1)S(1)}, bf16[128,512]{1,0:T(8,128)(2,1)}, u32[]{:S(2)}) copy-start(bf16[128,512]{1,0:T(8,128)(2,1)} %own_ref.1) | copy-start | bytes 393220
  0.0 9.5 %copy-start.2 = (s32[1,1,2]{2,1,0:T(1,128)S(1)}, s32[1,1,2]{2,1,0:T(1,128)}, u32[]{:S(2)}) copy-start(s32[1,1,2]{2,1,0:T(1,128)} %param.6) | copy-start | bytes 28
  0.0 15.0 %collective-permute-start.5 = (bf16[1024,128]{1,0:T(8,128)(2,1)}, bf16[1024,128]{1,0:T(8,128)(2,1)S(1)}, u32[]{:S(2)}, u32[]{:S(2)}) collective-permute-start(bf16[1024,128]{1,0:T(8,128)(2,1)} %own_ref.2), channel_id=1, source_target_pairs={{0,2},{2,0},{4,6},{6,4},{8,10},{10,8},{12,14},{14,12},{1,3},{3,1},... | collective-permute-start | bytes 786440 | tf_op jit(solution)/shard_map/ppermute | solution.py:258
  5.0 61.9 %copy-start.3 = (s32[4]{0:T(128)S(1)}, s32[4]{0:T(128)}, u32[]{:S(2)}) copy-start(s32[4]{0:T(128)} %param.9) | copy-start | bytes 52
  5.1 4.5 %collective-permute-start = (bf16[32,512]{1,0:T(8,128)(2,1)S(1)}, bf16[32,512]{1,0:T(8,128)(2,1)S(1)}, u32[]{:S(2)}, u32[]{:S(2)}) collective-permute-start(bf16[32,512]{1,0:T(8,128)(2,1)S(1)} %constant_dynamic-slice_fusion), channel_id=1, source_target_pairs={{0,4},{2,6},{4,0},{6,2},{8,12},{10,14},{12,8},{14,10},{1,5},{3,7},... | collective-permute-start | bytes 98312 | tf_op jit(solution)/shard_map/ppermute | solution.py:258
  6.7 5.1 %collective-permute-start.1 = (bf16[32,512]{1,0:T(8,128)(2,1)S(1)}, bf16[32,512]{1,0:T(8,128)(2,1)S(1)}, u32[]{:S(2)}, u32[]{:S(2)}) collective-permute-start(bf16[32,512]{1,0:T(8,128)(2,1)S(1)} %constant_dynamic-slice_fusion), channel_id=1, source_target_pairs={{0,8},{2,10},{4,12},{6,14},{8,0},{10,2},{12,4},{14,6},{1,9},{3,11}... | collective-permute-start | bytes 98312 | tf_op jit(solution)/shard_map/ppermute | solution.py:258
  9.3 5.7 %collective-permute-start.2 = (bf16[32,512]{1,0:T(8,128)(2,1)S(1)}, bf16[32,512]{1,0:T(8,128)(2,1)S(1)}, u32[]{:S(2)}, u32[]{:S(2)}) collective-permute-start(bf16[32,512]{1,0:T(8,128)(2,1)S(1)} %constant_dynamic-slice_fusion), channel_id=1, source_target_pairs={{0,12},{2,14},{4,8},{6,10},{8,4},{10,6},{12,0},{14,2},{1,13},{3,15... | collective-permute-start | bytes 98312 | tf_op jit(solution)/shard_map/ppermute | solution.py:258
  16.7 8.3 %collective-permute-start.6 = (bf16[16,32,128]{2,1,0:T(8,128)(2,1)S(1)}, bf16[16,32,128]{2,1,0:T(8,128)(2,1)S(1)}, u32[]{:S(2)}, u32[]{:S(2)}) collective-permute-start(bf16[16,32,128]{2,1,0:T(8,128)(2,1)S(1)} %get-tuple-element.57), channel_id=1, source_target_pairs={{0,2},{2,0},{4,6},{6,4},{8,10},{10,8},{12,14},{14,12},{1,3},{3,1},... | collective-permute-start | bytes 393224 | tf_op jit(solution)/shard_map/ppermute | solution.py:258
  17.4 16.8 %collective-permute-start.7 = (bf16[16,32,128]{2,1,0:T(8,128)(2,1)S(1)}, bf16[16,32,128]{2,1,0:T(8,128)(2,1)S(1)}, u32[]{:S(2)}, u32[]{:S(2)}) collective-permute-start(bf16[16,32,128]{2,1,0:T(8,128)(2,1)S(1)} %get-tuple-element.62), channel_id=1, source_target_pairs={{0,8},{2,10},{4,12},{6,14},{8,0},{10,2},{12,4},{14,6},{1,9},{3,11}... | collective-permute-start | bytes 393224 | tf_op jit(solution)/shard_map/ppermute | solution.py:258
  17.4 21.2 %collective-permute-start.9 = (bf16[16,32,128]{2,1,0:T(8,128)(2,1)S(1)}, bf16[16,32,128]{2,1,0:T(8,128)(2,1)S(1)}, u32[]{:S(2)}, u32[]{:S(2)}) collective-permute-start(bf16[16,32,128]{2,1,0:T(8,128)(2,1)S(1)} %get-tuple-element.66), channel_id=1, source_target_pairs={{0,10},{2,8},{4,14},{6,12},{8,2},{10,0},{12,6},{14,4},{1,11},{3,9}... | collective-permute-start | bytes 393224 | tf_op jit(solution)/shard_map/ppermute | solution.py:258
  21.2 17.3 %collective-permute-start.11 = (bf16[16,32,128]{2,1,0:T(8,128)(2,1)S(1)}, bf16[16,32,128]{2,1,0:T(8,128)(2,1)S(1)}, u32[]{:S(2)}, u32[]{:S(2)}) collective-permute-start(bf16[16,32,128]{2,1,0:T(8,128)(2,1)S(1)} %get-tuple-element.68), channel_id=1, source_target_pairs={{0,12},{2,14},{4,8},{6,10},{8,4},{10,6},{12,0},{14,2},{1,13},{3,15... | collective-permute-start | bytes 393224 | tf_op jit(solution)/shard_map/ppermute | solution.py:258
  21.6 21.9 %collective-permute-start.12 = (bf16[16,32,128]{2,1,0:T(8,128)(2,1)S(1)}, bf16[16,32,128]{2,1,0:T(8,128)(2,1)S(1)}, u32[]{:S(2)}, u32[]{:S(2)}) collective-permute-start(bf16[16,32,128]{2,1,0:T(8,128)(2,1)S(1)} %get-tuple-element.69), channel_id=1, source_target_pairs={{0,14},{2,12},{4,10},{6,8},{8,6},{10,4},{12,2},{14,0},{1,15},{3,13... | collective-permute-start | bytes 393224 | tf_op jit(solution)/shard_map/ppermute | solution.py:258
  32.1 22.3 %collective-permute-start.25 = (bf16[6,96,128]{2,1,0:T(8,128)(2,1)S(1)}, bf16[6,96,128]{2,1,0:T(8,128)(2,1)S(1)}, u32[]{:S(2)}, u32[]{:S(2)}) collective-permute-start(bf16[6,96,128]{2,1,0:T(8,128)(2,1)S(1)} %get-tuple-element.97), channel_id=1, source_target_pairs={{0,8},{2,10},{4,12},{6,14},{8,0},{10,2},{12,4},{14,6},{1,9},{3,11}... | collective-permute-start | bytes 442376 | tf_op jit(solution)/shard_map/ppermute | solution.py:258
  34.2 10.1 %collective-permute-start.8 = (bf16[16,32,128]{2,1,0:T(8,128)(2,1)S(1)}, bf16[16,32,128]{2,1,0:T(8,128)(2,1)S(1)}, u32[]{:S(2)}, u32[]{:S(2)}) collective-permute-start(bf16[16,32,128]{2,1,0:T(8,128)(2,1)S(1)} %get-tuple-element.63), channel_id=1, source_target_pairs={{0,4},{2,6},{4,0},{6,2},{8,12},{10,14},{12,8},{14,10},{1,5},{3,7},... | collective-permute-start | bytes 393224 | tf_op jit(solution)/shard_map/ppermute | solution.py:258
  38.5 7.1 %collective-permute-start.10 = (bf16[16,32,128]{2,1,0:T(8,128)(2,1)S(1)}, bf16[16,32,128]{2,1,0:T(8,128)(2,1)S(1)}, u32[]{:S(2)}, u32[]{:S(2)}) collective-permute-start(bf16[16,32,128]{2,1,0:T(8,128)(2,1)S(1)} %get-tuple-element.67), channel_id=1, source_target_pairs={{0,6},{2,4},{4,2},{6,0},{8,14},{10,12},{12,10},{14,8},{1,7},{3,5},... | collective-permute-start | bytes 393224 | tf_op jit(solution)/shard_map/ppermute | solution.py:258
  38.5 18.8 %collective-permute-start.15 = (bf16[6,96,128]{2,1,0:T(8,128)(2,1)S(1)}, bf16[6,96,128]{2,1,0:T(8,128)(2,1)S(1)}, u32[]{:S(2)}, u32[]{:S(2)}) collective-permute-start(bf16[6,96,128]{2,1,0:T(8,128)(2,1)S(1)} %get-tuple-element.77), channel_id=1, source_target_pairs={{0,10},{2,8},{4,14},{6,12},{8,2},{10,0},{12,6},{14,4},{1,11},{3,9}... | collective-permute-start | bytes 442376 | tf_op jit(solution)/shard_map/ppermute | solution.py:258
  43.6 17.1 %collective-permute-start.13 = (bf16[16,96,128]{2,1,0:T(8,128)(2,1)S(1)}, bf16[16,96,128]{2,1,0:T(8,128)(2,1)S(1)}, u32[]{:S(2)}, u32[]{:S(2)}) collective-permute-start(bf16[16,96,128]{2,1,0:T(8,128)(2,1)S(1)} %get-tuple-element.72), channel_id=1, source_target_pairs={{0,2},{2,0},{4,6},{6,4},{8,10},{10,8},{12,14},{14,12},{1,3},{3,1},... | collective-permute-start | bytes 1179656 | tf_op jit(solution)/shard_map/ppermute | solution.py:258
  44.2 16.2 %collective-permute-start.3 = (bf16[96,512]{1,0:T(8,128)(2,1)S(1)}, bf16[96,512]{1,0:T(8,128)(2,1)S(1)}, u32[]{:S(2)}, u32[]{:S(2)}) collective-permute-start(bf16[96,512]{1,0:T(8,128)(2,1)S(1)} %pad_maximum_fusion), channel_id=1, source_target_pairs={{0,2},{2,0},{4,6},{6,4},{8,10},{10,8},{12,14},{14,12},{1,3},{3,1},... | collective-permute-start | bytes 294920 | tf_op jit(solution)/shard_map/ppermute | solution.py:258
  45.6 15.0 %collective-permute-start.20 = (bf16[6,96,128]{2,1,0:T(8,128)(2,1)S(1)}, bf16[6,96,128]{2,1,0:T(8,128)(2,1)S(1)}, u32[]{:S(2)}, u32[]{:S(2)}) collective-permute-start(bf16[6,96,128]{2,1,0:T(8,128)(2,1)S(1)} %get-tuple-element.88), channel_id=1, source_target_pairs={{0,12},{2,14},{4,8},{6,10},{8,4},{10,6},{12,0},{14,2},{1,13},{3,15... | collective-permute-start | bytes 442376 | tf_op jit(solution)/shard_map/ppermute | solution.py:258
  54.4 21.5 %collective-permute-start.14 = (bf16[16,96,128]{2,1,0:T(8,128)(2,1)S(1)}, bf16[16,96,128]{2,1,0:T(8,128)(2,1)S(1)}, u32[]{:S(2)}, u32[]{:S(2)}) collective-permute-start(bf16[16,96,128]{2,1,0:T(8,128)(2,1)S(1)} %get-tuple-element.74), channel_id=1, source_target_pairs={{0,4},{2,6},{4,0},{6,2},{8,12},{10,14},{12,8},{14,10},{1,5},{3,7},... | collective-permute-start | bytes 1179656 | tf_op jit(solution)/shard_map/ppermute | solution.py:258
  57.3 9.6 %collective-permute-start.26 = (bf16[6,96,128]{2,1,0:T(8,128)(2,1)S(1)}, bf16[6,96,128]{2,1,0:T(8,128)(2,1)S(1)}, u32[]{:S(2)}, u32[]{:S(2)}) collective-permute-start(bf16[6,96,128]{2,1,0:T(8,128)(2,1)S(1)} %get-tuple-element.98), channel_id=1, source_target_pairs={{0,14},{2,12},{4,10},{6,8},{8,6},{10,4},{12,2},{14,0},{1,15},{3,13... | collective-permute-start | bytes 442376 | tf_op jit(solution)/shard_map/ppermute | solution.py:258
  60.4 31.0 %collective-permute-start.16 = (bf16[16,96,128]{2,1,0:T(8,128)(2,1)S(1)}, bf16[16,96,128]{2,1,0:T(8,128)(2,1)S(1)}, u32[]{:S(2)}, u32[]{:S(2)}) collective-permute-start(bf16[16,96,128]{2,1,0:T(8,128)(2,1)S(1)} %get-tuple-element.78), channel_id=1, source_target_pairs={{0,6},{2,4},{4,2},{6,0},{8,14},{10,12},{12,10},{14,8},{1,7},{3,5},... | collective-permute-start | bytes 1179656 | tf_op jit(solution)/shard_map/ppermute | solution.py:258
  60.6 17.6 %collective-permute-start.4 = (bf16[192,512]{1,0:T(8,128)(2,1)S(1)}, bf16[192,512]{1,0:T(8,128)(2,1)S(1)}, u32[]{:S(2)}, u32[]{:S(2)}) collective-permute-start(bf16[192,512]{1,0:T(8,128)(2,1)S(1)} %constant_dynamic-update-slice_fusion.near_ref), channel_id=1, source_target_pairs={{0,1},{1,0},{2,3},{3,2},{4,5},{5,4},{6,7},{7,6},{8,9},{9,8},{10,11... | collective-permute-start | bytes 589832 | tf_op jit(solution)/shard_map/ppermute | solution.py:261
  60.7 18.8 %collective-permute-start.21 = (bf16[6,96,128]{2,1,0:T(8,128)(2,1)S(1)}, bf16[6,96,128]{2,1,0:T(8,128)(2,1)S(1)}, u32[]{:S(2)}, u32[]{:S(2)}) collective-permute-start(bf16[6,96,128]{2,1,0:T(8,128)(2,1)S(1)} %get-tuple-element.89), channel_id=1, source_target_pairs={{0,10},{2,8},{4,14},{6,12},{8,2},{10,0},{12,6},{14,4},{1,11},{3,9}... | collective-permute-start | bytes 442376 | tf_op jit(solution)/shard_map/ppermute | solution.py:258
  66.9 15.9 %collective-permute-start.18 = (bf16[6,96,128]{2,1,0:T(8,128)(2,1)S(1)}, bf16[6,96,128]{2,1,0:T(8,128)(2,1)S(1)}, u32[]{:S(2)}, u32[]{:S(2)}) collective-permute-start(bf16[6,96,128]{2,1,0:T(8,128)(2,1)S(1)} %get-tuple-element.83), channel_id=1, source_target_pairs={{0,8},{2,10},{4,12},{6,14},{8,0},{10,2},{12,4},{14,6},{1,9},{3,11}... | collective-permute-start | bytes 442376 | tf_op jit(solution)/shard_map/ppermute | solution.py:258
  75.9 25.6 %collective-permute-start.27 = (bf16[6,96,128]{2,1,0:T(8,128)(2,1)S(1)}, bf16[6,96,128]{2,1,0:T(8,128)(2,1)S(1)}, u32[]{:S(2)}, u32[]{:S(2)}) collective-permute-start(bf16[6,96,128]{2,1,0:T(8,128)(2,1)S(1)} %get-tuple-element.99), channel_id=1, source_target_pairs={{0,14},{2,12},{4,10},{6,8},{8,6},{10,4},{12,2},{14,0},{1,15},{3,13... | collective-permute-start | bytes 442376 | tf_op jit(solution)/shard_map/ppermute | solution.py:258
  78.2 19.3 %collective-permute-start.23 = (bf16[6,96,128]{2,1,0:T(8,128)(2,1)S(1)}, bf16[6,96,128]{2,1,0:T(8,128)(2,1)S(1)}, u32[]{:S(2)}, u32[]{:S(2)}) collective-permute-start(bf16[6,96,128]{2,1,0:T(8,128)(2,1)S(1)} %get-tuple-element.93), channel_id=1, source_target_pairs={{0,12},{2,14},{4,8},{6,10},{8,4},{10,6},{12,0},{14,2},{1,13},{3,15... | collective-permute-start | bytes 442376 | tf_op jit(solution)/shard_map/ppermute | solution.py:258
  79.5 24.1 %collective-permute-start.22 = (bf16[4,96,128]{2,1,0:T(8,128)(2,1)S(1)}, bf16[4,96,128]{2,1,0:T(8,128)(2,1)S(1)}, u32[]{:S(2)}, u32[]{:S(2)}) collective-permute-start(bf16[4,96,128]{2,1,0:T(8,128)(2,1)S(1)} %get-tuple-element.90), channel_id=1, source_target_pairs={{0,12},{2,14},{4,8},{6,10},{8,4},{10,6},{12,0},{14,2},{1,13},{3,15... | collective-permute-start | bytes 294920 | tf_op jit(solution)/shard_map/ppermute | solution.py:258
  82.8 24.0 %collective-permute-start.19 = (bf16[4,96,128]{2,1,0:T(8,128)(2,1)S(1)}, bf16[4,96,128]{2,1,0:T(8,128)(2,1)S(1)}, u32[]{:S(2)}, u32[]{:S(2)}) collective-permute-start(bf16[4,96,128]{2,1,0:T(8,128)(2,1)S(1)} %get-tuple-element.84), channel_id=1, source_target_pairs={{0,10},{2,8},{4,14},{6,12},{8,2},{10,0},{12,6},{14,4},{1,11},{3,9}... | collective-permute-start | bytes 294920 | tf_op jit(solution)/shard_map/ppermute | solution.py:258
  91.4 16.3 %collective-permute-start.17 = (bf16[4,96,128]{2,1,0:T(8,128)(2,1)S(1)}, bf16[4,96,128]{2,1,0:T(8,128)(2,1)S(1)}, u32[]{:S(2)}, u32[]{:S(2)}) collective-permute-start(bf16[4,96,128]{2,1,0:T(8,128)(2,1)S(1)} %get-tuple-element.80), channel_id=1, source_target_pairs={{0,8},{2,10},{4,12},{6,14},{8,0},{10,2},{12,4},{14,6},{1,9},{3,11}... | collective-permute-start | bytes 294920 | tf_op jit(solution)/shard_map/ppermute | solution.py:258
  97.5 10.2 %collective-permute-start.24 = (bf16[4,96,128]{2,1,0:T(8,128)(2,1)S(1)}, bf16[4,96,128]{2,1,0:T(8,128)(2,1)S(1)}, u32[]{:S(2)}, u32[]{:S(2)}) collective-permute-start(bf16[4,96,128]{2,1,0:T(8,128)(2,1)S(1)} %get-tuple-element.94), channel_id=1, source_target_pairs={{0,14},{2,12},{4,10},{6,8},{8,6},{10,4},{12,2},{14,0},{1,15},{3,13... | collective-permute-start | bytes 294920 | tf_op jit(solution)/shard_map/ppermute | solution.py:258
  109.6 1.4 %collective-permute-start.28 = (f32[4,32,256]{2,1,0:T(8,128)S(1)}, f32[4,32,256]{2,1,0:T(8,128)S(1)}, u32[]{:S(2)}, u32[]{:S(2)}) collective-permute-start(f32[4,32,256]{2,1,0:T(8,128)S(1)} %get-tuple-element.101), channel_id=1, source_target_pairs={{0,1},{1,0},{2,3},{3,2},{4,5},{5,4},{6,7},{7,6},{8,9},{9,8},{10,11... | collective-permute-start | bytes 393224 | tf_op jit(solution)/shard_map/ppermute | solution.py:261
  111.1 4.3 %collective-permute-start.29 = (f32[4,32,128]{2,1,0:T(8,128)S(1)}, f32[4,32,128]{2,1,0:T(8,128)S(1)}, u32[]{:S(2)}, u32[]{:S(2)}) collective-permute-start(f32[4,32,128]{2,1,0:T(8,128)S(1)} %slice_add_fusion), channel_id=1, source_target_pairs={{0,2},{2,0},{4,6},{6,4},{8,10},{10,8},{12,14},{14,12},{1,3},{3,1},... | collective-permute-start | bytes 196616 | tf_op jit(solution)/shard_map/ppermute | solution.py:258
  115.4 5.4 %collective-permute-start.30 = (f32[32,128]{1,0:T(8,128)S(1)}, f32[32,128]{1,0:T(8,128)S(1)}, u32[]{:S(2)}, u32[]{:S(2)}) collective-permute-start(f32[32,128]{1,0:T(8,128)S(1)} %get-tuple-element.103), channel_id=1, source_target_pairs={{0,4},{2,6},{4,0},{6,2},{8,12},{10,14},{12,8},{14,10},{1,5},{3,7},... | collective-permute-start | bytes 49160 | tf_op jit(solution)/shard_map/ppermute | solution.py:258
  117.3 4.7 %collective-permute-start.31 = (f32[32,128]{1,0:T(8,128)S(1)}, f32[32,128]{1,0:T(8,128)S(1)}, u32[]{:S(2)}, u32[]{:S(2)}) collective-permute-start(f32[32,128]{1,0:T(8,128)S(1)} %get-tuple-element.105), channel_id=1, source_target_pairs={{0,8},{2,10},{4,12},{6,14},{8,0},{10,2},{12,4},{14,6},{1,9},{3,11}... | collective-permute-start | bytes 49160 | tf_op jit(solution)/shard_map/ppermute | solution.py:258
  119.4 5.5 %collective-permute-start.32 = (f32[32,128]{1,0:T(8,128)S(1)}, f32[32,128]{1,0:T(8,128)S(1)}, u32[]{:S(2)}, u32[]{:S(2)}) collective-permute-start(f32[32,128]{1,0:T(8,128)S(1)} %get-tuple-element.104), channel_id=1, source_target_pairs={{0,12},{2,14},{4,8},{6,10},{8,4},{10,6},{12,0},{14,2},{1,13},{3,15... | collective-permute-start | bytes 49160 | tf_op jit(solution)/shard_map/ppermute | solution.py:258

commit v3 on v2

--- a/solution.py
+++ b/solution.py
@@ -11,6 +11,12 @@
 BF16 = jnp.bfloat16
 ROWS = 16
 WINDOW = 5
+GROUPS = ((0, 7), (7, 13), (13, 16))
+FIRST = 32
+OPEN = (4, 1, 5, 3, 6, 7)
+ORDER = ((2, -1), (4, 0), (5, 0), (1, 0), (6, 0), (2, 0), (7, 0), (3, 0), (4, 1), (5, 1), (7, 1), (6, 1), (4, 2), (5, 2), (6, 2), (7, 2))
+RESTDEP = 1
+LAST = (2, 3, 1)
 WHOLE = pl.BlockSpec(memory_space=pltpu.VMEM)
 
 
@@ -134,33 +140,36 @@
     )(integrals, table, after)
 
 
-def metric_kernel(where, own_ref, near_ref, far_ref, o_ref):
+def metric_kernel(where, *refs):
+    o_ref = refs[-1]
     aux = where.shape[0] - 1
     width = o_ref.shape[1] // aux
     for kz in range(aux):
         start = pl.multiple_of(where[where[aux] ^ kz] * width, width)
         at = 0
-        for ref in (own_ref, near_ref, far_ref):
+        for ref in refs[:-1]:
             size = ref.shape[0]
             o_ref[at : at + size, kz * width : (kz + 1) * width] = ref[:, pl.ds(start, width)]
             at += size
 
 
-def ordered_metric(where, own, near, far):
-    total = own.shape[0] + near.shape[0] + far.shape[0]
+def ordered_metric(where, pieces):
+    total = sum(piece.shape[0] for piece in pieces)
+    columns = pieces[0].shape[1]
     return pl.pallas_call(
         metric_kernel,
-        in_specs=[pl.BlockSpec(memory_space=pltpu.SMEM)] + [WHOLE] * 3,
+        in_specs=[pl.BlockSpec(memory_space=pltpu.SMEM)] + [WHOLE] * len(pieces),
         out_specs=WHOLE,
-        out_shape=jax.ShapeDtypeStruct((total, own.shape[1]), BF16),
-        compiler_params=params(),
-        cost_estimate=cost(0, total * own.shape[1] * 4),
+        out_shape=jax.ShapeDtypeStruct((total, columns), BF16),
+        compiler_params=params(),
+        cost_estimate=cost(0, total * columns * 4),
         name="ordered_metric",
-    )(where, own, near, far)
+    )(where, *pieces)
 
 
 def add_group(aux, bas, lo, hi, starts, metric, early, late, total):
     chips = aux * bas
+    fitted = []
     for i in range(lo, hi):
         columns = []
         for k in range(chips):
@@ -169,11 +178,11 @@
             [jnp.concatenate(columns[kz * bas : (kz + 1) * bas], axis=1) for kz in range(aux)],
             axis=0,
         )
-        fitted = jnp.dot(metric, stacked, preferred_element_type=F32).astype(BF16)
-        total = total + lax.dot_general(
-            fitted, fitted, (((0,), (0,)), ((), ())), preferred_element_type=F32
-        )
-    return total
+        fitted.append(jnp.dot(metric, stacked, preferred_element_type=F32).astype(BF16))
+    fitted = jnp.concatenate(fitted, axis=0)
+    return total + lax.dot_general(
+        fitted, fitted, (((0,), (0,)), ((), ())), preferred_element_type=F32
+    )
 
 
 def group_kernel(aux, bas, lo, hi, starts, started, last, *refs):
@@ -247,8 +256,8 @@
     orbitals = coefficients.shape[1]
     share = orbitals // chips
     a, b, o = (lax.axis_index(name) for name in ("aux", "bas", "occ"))
-    first = integrals.shape[2] // 4
-    groups = ((0, 6), (6, 12), (12, share))
+    first = FIRST
+    groups = GROUPS
     inner, outer = (1, 2, 3), (4, 5, 6, 7)
 
     def swap(value, kz=0, kx=0):
@@ -266,48 +275,46 @@
     integrals = pltpu.with_memory_space_constraint(integrals, pltpu.HBM)
     other = swap(coefficients, kx=1)
     moved = relayout(integrals, first)
-
+    where = jnp.concatenate([jnp.stack([a * bas + b, b]), screening[0, 0]]).astype(jnp.int32)
     rows = metric.shape[0] // 4
-    part = lax.dynamic_slice_in_dim(after(metric, moved), (b * 2 + o) * rows, rows, axis=0)
-    pieces = [swap(part, kz=kz) for kz in range(1, aux)]
-    where = jnp.concatenate([jnp.stack([a * bas + b, b]), screening[0, 0]]).astype(jnp.int32)
+    held = lax.dynamic_slice_in_dim(metric, (b * 2 + o) * rows, rows, axis=0)
+    held = [held, swap(held, kz=2)]
     *early, table = first_products(
-        chips, where, after(coefficients, *pieces), other, moved, first
-    )
-
+        chips, where, after(coefficients, *held), other, moved, first
+    )
+    held = jnp.concatenate(held, axis=0)
     sent = []
 
-    def send(k, value):
+    def send(value, kz, kx):
         if len(sent) >= WINDOW:
             value = after(value, sent[-WINDOW])
-        sent.append(swap(value, k // bas, k % bas))
+        sent.append(swap(value, kz, kx))
         return sent[-1]
 
+    got = {(k, -1): send(early[k], k // bas, k % bas) for k in OPEN}
+    got[0, -1] = early[0]
     spans = [(k, lo, hi) for lo, hi in groups for k in outer]
     spans += [(k, 0, share) for k in (0, *inner)]
-    got = {k: send(k, early[k]) for k in (4, 5, 1, 6, 7)}
-    late = rest_products(chips, tuple(spans), integrals, table, first, got[1])
-    for k in (2, 3):
-        got[k] = send(k, after(early[k], late[0]))
-    got[0] = early[0]
+    late = rest_products(chips, tuple(spans), integrals, table, first, got[RESTDEP, -1])
     made = dict(zip(spans, late))
-    here = {(0, 0, share): made[0, 0, share]}
-    for g, (lo, hi) in enumerate(groups):
-        for at, k in enumerate(outer):
-            here[k, lo, hi] = send(k, made[k, lo, hi])
-            if g == 0 and at:
-                here[at, 0, share] = send(at, made[at, 0, share])
-
-    near = jnp.concatenate(pieces, axis=0)
-    near = jnp.concatenate([near, swap(near, kx=1)], axis=0)
-    far = across(near)
+    got[0, 0] = made[0, 0, share]
+    for k, g in ORDER:
+        if g < 0:
+            value = after(early[k], late[0])
+        else:
+            value = made[(k, *groups[g])] if k in outer else made[k, 0, share]
+        got[k, g] = send(value, k // bas, k % bas)
+    held = jnp.concatenate([held, swap(held, kz=1)], axis=0)
+    held = jnp.concatenate([held, swap(held, kx=1)], axis=0)
     ordered = ordered_metric(
-        jnp.concatenate([aux_owner, a[None]]).astype(jnp.int32), metric, near, far
-    )
-    early = [got[k] for k in range(chips)]
+        jnp.concatenate([aux_owner, a[None]]).astype(jnp.int32), [held, across(held)]
+    )
+    early = [got[k, -1] for k in range(chips)]
     total = None
     for g, (lo, hi) in enumerate(groups):
-        part = [(here[k, 0, share], lo) if k < 4 else (here[k, lo, hi], 0) for k in range(chips)]
+        part = [
+            (got[k, g], 0) if k in outer else (got[k, 0], lo) for k in range(chips)
+        ]
         place = jnp.stack([a, b, o]).astype(jnp.int32) if g == len(groups) - 1 else None
         total = group(aux, bas, lo, hi, ordered, early, part, total, place)
     kept, near, away = total
@@ -317,7 +324,7 @@
     near = near + away[:, :, width:]
     kept = kept + swap(near, kx=1)
     value = kept[0]
-    for kz in range(1, aux):
+    for kz in LAST:
         value = value + swap(kept[kz], kz=kz)
     return value.T
 

time: 126 us -> 122 us (0.968)
  starting transfers between devices: 56.6 us -> 54.6 us
  waiting for transfers between devices: 50.4 us -> 48.7 us
    ppermute x31 -> x30, starting transfers between devices: 56.4 us -> 54.4 us  [swap(): return lax.ppermute(value, ('aux', 'bas'), pairs)]
    ppermute x31 -> x30, waiting for transfers between devices: 49.1 us -> 47.4 us  [swap(): return lax.ppermute(value, ('aux', 'bas'), pairs)]
  transfers between devices with their start and end apart: 33 -> 32, of which waited for: 15 -> 14; matrix products, arithmetic and copies ran while one was open for 0% -> 1% of each run, Pallas kernels for 11% -> 11%
where the time goes in v3:
time: 122 us; the launch traced here: 121 us
  starting transfers between devices  54.6 us (45%)
  waiting for transfers between devices  48.7 us (40%)
  Pallas kernels  16.4 us (13%)
  other arithmetic  1.55 us (1%)
    ppermute x30, starting transfers between devices, swap(): return lax.ppermute(value, ('aux', 'bas'), pairs)  54.4 us
    ppermute x30, waiting for transfers between devices, swap(): return lax.ppermute(value, ('aux', 'bas'), pairs)  47.4 us
    pallas_call x1, Pallas kernels, rest_products(): pl.pallas_call(functools.partial(rest_kernel, chips, spans), grid=(rest /...  7.03 us
    pallas_call x3, Pallas kernels, group(): pl.pallas_call(functools.partial(group_kernel, aux, bas, lo, hi, starts,...  5 us
  transfers between devices with their start and end apart: 32, of which 14 were waited for; matrix products, arithmetic and copies ran while one was open for 1% of the time, Pallas kernels for 11%

profile of v3, /device:TPU:0, one launch (start us, length us, event | category | flops | bytes accessed | tf_op | source)
XLA Modules:
  0.0 121.5 jit_solution(2223769532628259991)
XLA Ops:
  0.0 2.9 %collective-permute-start.4 = (bf16[1024,128]{1,0:T(8,128)(2,1)}, bf16[1024,128]{1,0:T(8,128)(2,1)S(1)}, u32[]{:S(2)}, u32[]{:S(2)}) collective-permute-start(bf16[1024,128]{1,0:T(8,128)(2,1)} %own_ref), channel_id=1, source_target_pairs={{0,2},{2,0},{4,6},{6,4},{8,10},{10,8},{12,14},{14,12},{1,3},{3,1},... | collective-permute-start | bytes 786440 | tf_op jit(solution)/shard_map/ppermute | solution.py:267
  3.0 2.6 %collective-permute-start = (bf16[32,512]{1,0:T(8,128)(2,1)S(1)}, bf16[32,512]{1,0:T(8,128)(2,1)S(1)}, u32[]{:S(2)}, u32[]{:S(2)}) collective-permute-start(bf16[32,512]{1,0:T(8,128)(2,1)S(1)} %constant_dynamic-slice_fusion), channel_id=1, source_target_pairs={{0,8},{2,10},{4,12},{6,14},{8,0},{10,2},{12,4},{14,6},{1,9},{3,11}... | collective-permute-start | bytes 98312 | tf_op jit(solution)/shard_map/ppermute | solution.py:267
  5.5 0.7 pad_add_fusion.2.where
  6.3 2.0 %relayout.1.x_ref = bf16[32,256,128]{2,1,0:T(8,128)(2,1)S(1)} custom-call(bf16[2,128,128,128]{3,2,1,0:T(8,128)(2,1)} %bitcast.24), custom_call_target="tpu_custom_call" | custom-call | bytes 4194304 | tf_op jit(solution)/shard_map/relayout/pallas_call | solution.py:38
  8.3 1.2 collective-permute-done.4.other_ref
  9.5 1.7 %first_products.1 = (bf16[16,32,128]{2,1,0:T(8,128)(2,1)S(1)}, bf16[16,32,128]{2,1,0:T(8,128)(2,1)S(1)}, bf16[16,32,128]{2,1,0:T(8,128)(2,1)S(1)}, bf16[16,32,12...) custom-call(s32[4]{0:T(128)S(1)} %pad_add_fusion.2.where, ...), custom_call_target="tpu_custom_call" | custom-call | flops 268435456 | bytes 2097152 | tf_op jit(solution)/shard_map/first_products/pallas_call | solution.py:90
  11.2 2.9 %collective-permute-start.8 = (bf16[16,32,128]{2,1,0:T(8,128)(2,1)S(1)}, bf16[16,32,128]{2,1,0:T(8,128)(2,1)S(1)}, u32[]{:S(2)}, u32[]{:S(2)}) collective-permute-start(bf16[16,32,128]{2,1,0:T(8,128)(2,1)S(1)} %get-tuple-element.61), channel_id=1, source_target_pairs={{0,8},{2,10},{4,12},{6,14},{8,0},{10,2},{12,4},{14,6},{1,9},{3,11}... | collective-permute-start | bytes 393224 | tf_op jit(solution)/shard_map/ppermute | solution.py:267
  14.1 1.5 %collective-permute-start.5 = (bf16[16,32,128]{2,1,0:T(8,128)(2,1)S(1)}, bf16[16,32,128]{2,1,0:T(8,128)(2,1)S(1)}, u32[]{:S(2)}, u32[]{:S(2)}) collective-permute-start(bf16[16,32,128]{2,1,0:T(8,128)(2,1)S(1)} %get-tuple-element.54), channel_id=1, source_target_pairs={{0,2},{2,0},{4,6},{6,4},{8,10},{10,8},{12,14},{14,12},{1,3},{3,1},... | collective-permute-start | bytes 393224 | tf_op jit(solution)/shard_map/ppermute | solution.py:267
  15.6 1.5 %collective-permute-start.7 = (bf16[16,32,128]{2,1,0:T(8,128)(2,1)S(1)}, bf16[16,32,128]{2,1,0:T(8,128)(2,1)S(1)}, u32[]{:S(2)}, u32[]{:S(2)}) collective-permute-start(bf16[16,32,128]{2,1,0:T(8,128)(2,1)S(1)} %get-tuple-element.60), channel_id=1, source_target_pairs={{0,6},{2,4},{4,2},{6,0},{8,14},{10,12},{12,10},{14,8},{1,7},{3,5},... | collective-permute-start | bytes 393224 | tf_op jit(solution)/shard_map/ppermute | solution.py:267
  17.1 1.3 %collective-permute-start.9 = (bf16[16,32,128]{2,1,0:T(8,128)(2,1)S(1)}, bf16[16,32,128]{2,1,0:T(8,128)(2,1)S(1)}, u32[]{:S(2)}, u32[]{:S(2)}) collective-permute-start(bf16[16,32,128]{2,1,0:T(8,128)(2,1)S(1)} %get-tuple-element.62), channel_id=1, source_target_pairs={{0,10},{2,8},{4,14},{6,12},{8,2},{10,0},{12,6},{14,4},{1,11},{3,9}... | collective-permute-start | bytes 393224 | tf_op jit(solution)/shard_map/ppermute | solution.py:267
  18.4 0.4 collective-permute-start.1
  18.8 0.9 collective-permute-done.8.refs_5_.refs_6_
  19.8 5.5 %collective-permute-start.10 = (bf16[16,32,128]{2,1,0:T(8,128)(2,1)S(1)}, bf16[16,32,128]{2,1,0:T(8,128)(2,1)S(1)}, u32[]{:S(2)}, u32[]{:S(2)}) collective-permute-start(bf16[16,32,128]{2,1,0:T(8,128)(2,1)S(1)} %get-tuple-element.63), channel_id=1, source_target_pairs={{0,12},{2,14},{4,8},{6,10},{8,4},{10,6},{12,0},{14,2},{1,13},{3,15... | collective-permute-start | bytes 393224 | tf_op jit(solution)/shard_map/ppermute | solution.py:267
  25.3 0.9 collective-permute-start.11
  26.2 7.0 %rest_products.1 = (bf16[7,96,128]{2,1,0:T(8,128)(2,1)S(1)}, bf16[7,96,128]{2,1,0:T(8,128)(2,1)S(1)}, bf16[7,96,128]{2,1,0:T(8,128)(2,1)S(1)}, bf16[7,96,128]{2,...) custom-call(bf16[2,128,128,128]{3,2,1,0:T(8,128)(2,1)} %bitcast.25, ...), custom_call_target="tpu_custom_call" | custom-call | flops 805306368 | bytes 8388608 | tf_op jit(solution)/shard_map/rest_products/pallas_call | solution.py:127
  33.3 4.4 %collective-permute-start.24 = (bf16[7,96,128]{2,1,0:T(8,128)(2,1)S(1)}, bf16[7,96,128]{2,1,0:T(8,128)(2,1)S(1)}, u32[]{:S(2)}, u32[]{:S(2)}) collective-permute-start(bf16[7,96,128]{2,1,0:T(8,128)(2,1)S(1)} %get-tuple-element.93), channel_id=1, source_target_pairs={{0,8},{2,10},{4,12},{6,14},{8,0},{10,2},{12,4},{14,6},{1,9},{3,11}... | collective-permute-start | bytes 516104 | tf_op jit(solution)/shard_map/ppermute | solution.py:267
  37.8 1.5 %collective-permute-start.2 = (bf16[128,512]{1,0:T(8,128)(2,1)S(1)}, bf16[128,512]{1,0:T(8,128)(2,1)S(1)}, u32[]{:S(2)}, u32[]{:S(2)}) collective-permute-start(bf16[128,512]{1,0:T(8,128)(2,1)S(1)} %pad_maximum_fusion.1), channel_id=1, source_target_pairs={{0,2},{2,0},{4,6},{6,4},{8,10},{10,8},{12,14},{14,12},{1,3},{3,1},... | collective-permute-start | bytes 393224 | tf_op jit(solution)/shard_map/ppermute | solution.py:267
  39.3 0.6 collective-permute-start.12
  39.9 2.5 %collective-permute-start.19 = (bf16[7,96,128]{2,1,0:T(8,128)(2,1)S(1)}, bf16[7,96,128]{2,1,0:T(8,128)(2,1)S(1)}, u32[]{:S(2)}, u32[]{:S(2)}) collective-permute-start(bf16[7,96,128]{2,1,0:T(8,128)(2,1)S(1)} %get-tuple-element.84), channel_id=1, source_target_pairs={{0,12},{2,14},{4,8},{6,10},{8,4},{10,6},{12,0},{14,2},{1,13},{3,15... | collective-permute-start | bytes 516104 | tf_op jit(solution)/shard_map/ppermute | solution.py:267
  42.4 10.1 %collective-permute-done.24.refs_13_ = bf16[7,96,128]{2,1,0:T(8,128)(2,1)S(1)} collective-permute-done((bf16[7,96,128]{2,1,0:T(8,128)(2,1)S(1)}, bf16[7,96,128]{2,1,0:T(8,128)(2,1)S(1)}, u32[]{:S(2)}, u32[]{:S(2)}) %collective-permute-start.24) | collective-permute-done | bytes 172064 | tf_op jit(solution)/shard_map/ppermute | solution.py:267
  52.5 0.4 collective-permute-start.13
  52.9 3.6 %collective-permute-done.14.refs_14_ = bf16[7,96,128]{2,1,0:T(8,128)(2,1)S(1)} collective-permute-done((bf16[7,96,128]{2,1,0:T(8,128)(2,1)S(1)}, bf16[7,96,128]{2,1,0:T(8,128)(2,1)S(1)}, u32[]{:S(2)}, u32[]{:S(2)}) %collective-permute-start.14) | collective-permute-done | bytes 172064 | tf_op jit(solution)/shard_map/ppermute | solution.py:267
  56.5 3.5 %collective-permute-start.25 = (bf16[7,96,128]{2,1,0:T(8,128)(2,1)S(1)}, bf16[7,96,128]{2,1,0:T(8,128)(2,1)S(1)}, u32[]{:S(2)}, u32[]{:S(2)}) collective-permute-start(bf16[7,96,128]{2,1,0:T(8,128)(2,1)S(1)} %get-tuple-element.94), channel_id=1, source_target_pairs={{0,14},{2,12},{4,10},{6,8},{8,6},{10,4},{12,2},{14,0},{1,15},{3,13... | collective-permute-start | bytes 516104 | tf_op jit(solution)/shard_map/ppermute | solution.py:267
  60.2 2.7 %collective-permute-start.20 = (bf16[6,96,128]{2,1,0:T(8,128)(2,1)S(1)}, bf16[6,96,128]{2,1,0:T(8,128)(2,1)S(1)}, u32[]{:S(2)}, u32[]{:S(2)}) collective-permute-start(bf16[6,96,128]{2,1,0:T(8,128)(2,1)S(1)} %get-tuple-element.85), channel_id=1, source_target_pairs={{0,10},{2,8},{4,14},{6,12},{8,2},{10,0},{12,6},{14,4},{1,11},{3,9}... | collective-permute-start | bytes 442376 | tf_op jit(solution)/shard_map/ppermute | solution.py:267
  62.9 7.3 %collective-permute-done.25.refs_16_ = bf16[7,96,128]{2,1,0:T(8,128)(2,1)S(1)} collective-permute-done((bf16[7,96,128]{2,1,0:T(8,128)(2,1)S(1)}, bf16[7,96,128]{2,1,0:T(8,128)(2,1)S(1)}, u32[]{:S(2)}, u32[]{:S(2)}) %collective-permute-start.25) | collective-permute-done | bytes 172064 | tf_op jit(solution)/shard_map/ppermute | solution.py:267
  70.4 2.7 %collective-permute-done.13.refs_11_.refs_12_ = bf16[16,96,128]{2,1,0:T(8,128)(2,1)S(1)} collective-permute-done((bf16[16,96,128]{2,1,0:T(8,128)(2,1)S(1)}, bf16[16,96,128]{2,1,0:T(8,128)(2,1)S(1)}, u32[]{:S(2)}, u32[]{:S(2)}) %collective-permute-start.13) | collective-permute-done | bytes 393248 | tf_op jit(solution)/shard_map/ppermute | solution.py:267
  73.0 3.4 %collective-permute-start.26 = (bf16[6,96,128]{2,1,0:T(8,128)(2,1)S(1)}, bf16[6,96,128]{2,1,0:T(8,128)(2,1)S(1)}, u32[]{:S(2)}, u32[]{:S(2)}) collective-permute-start(bf16[6,96,128]{2,1,0:T(8,128)(2,1)S(1)} %get-tuple-element.95), channel_id=1, source_target_pairs={{0,12},{2,14},{4,8},{6,10},{8,4},{10,6},{12,0},{14,2},{1,13},{3,15... | collective-permute-start | bytes 442376 | tf_op jit(solution)/shard_map/ppermute | solution.py:267
  76.5 1.7 %collective-permute-start.22 = (bf16[6,96,128]{2,1,0:T(8,128)(2,1)S(1)}, bf16[6,96,128]{2,1,0:T(8,128)(2,1)S(1)}, u32[]{:S(2)}, u32[]{:S(2)}) collective-permute-start(bf16[6,96,128]{2,1,0:T(8,128)(2,1)S(1)} %get-tuple-element.89), channel_id=1, source_target_pairs={{0,14},{2,12},{4,10},{6,8},{8,6},{10,4},{12,2},{14,0},{1,15},{3,13... | collective-permute-start | bytes 442376 | tf_op jit(solution)/shard_map/ppermute | solution.py:267
  78.2 0.6 ordered_metric.1.refs_0_.refs_1_
  78.9 3.9 %collective-permute-start.21 = (bf16[3,96,128]{2,1,0:T(8,128)(2,1)S(1)}, bf16[3,96,128]{2,1,0:T(8,128)(2,1)S(1)}, u32[]{:S(2)}, u32[]{:S(2)}) collective-permute-start(bf16[3,96,128]{2,1,0:T(8,128)(2,1)S(1)} %get-tuple-element.86), channel_id=1, source_target_pairs={{0,12},{2,14},{4,8},{6,10},{8,4},{10,6},{12,0},{14,2},{1,13},{3,15... | collective-permute-start | bytes 221192 | tf_op jit(solution)/shard_map/ppermute | solution.py:267
  82.8 10.0 %collective-permute-done.17.refs_13_ = bf16[6,96,128]{2,1,0:T(8,128)(2,1)S(1)} collective-permute-done((bf16[6,96,128]{2,1,0:T(8,128)(2,1)S(1)}, bf16[6,96,128]{2,1,0:T(8,128)(2,1)S(1)}, u32[]{:S(2)}, u32[]{:S(2)}) %collective-permute-start.17) | collective-permute-done | bytes 147488 | tf_op jit(solution)/shard_map/ppermute | solution.py:267
  92.9 3.4 %collective-permute-start.16 = (bf16[3,96,128]{2,1,0:T(8,128)(2,1)S(1)}, bf16[3,96,128]{2,1,0:T(8,128)(2,1)S(1)}, u32[]{:S(2)}, u32[]{:S(2)}) collective-permute-start(bf16[3,96,128]{2,1,0:T(8,128)(2,1)S(1)} %get-tuple-element.76), channel_id=1, source_target_pairs={{0,8},{2,10},{4,12},{6,14},{8,0},{10,2},{12,4},{14,6},{1,9},{3,11}... | collective-permute-start | bytes 221192 | tf_op jit(solution)/shard_map/ppermute | solution.py:267
  96.3 1.8 %group.3.refs_17_ = f32[256,256]{1,0:T(8,128)S(1)} custom-call(bf16[512,512]{1,0:T(8,128)(2,1)S(1)} %ordered_metric.1.refs_0_.refs_1_, bf16[16,32,128]{2,1,0:T(8,128)(2,1)S(1)} %get-tuple-element.53.refs_1_.refs_2_, bf16[16,32,128]{2,1,0:T(8,128)(2,1)S(1)} %collective-permute-done.5._.refs_2_.refs_3_, ...), custom_call_target="tpu_custom_call" | custom-call | flops 1409286144 | bytes 1835008 | tf_op jit(solution)/shard_map/group/pallas_call | solution.py:239
  98.1 0.5 collective-permute-start.23
  98.6 1.6 %group.4.refs_18_ = f32[256,256]{1,0:T(8,128)S(1)} custom-call(bf16[512,512]{1,0:T(8,128)(2,1)S(1)} %ordered_metric.1.refs_0_.refs_1_, bf16[16,32,128]{2,1,0:T(8,128)(2,1)S(1)} %get-tuple-element.53.refs_1_.refs_2_, bf16[16,32,128]{2,1,0:T(8,128)(2,1)S(1)} %collective-permute-done.5._.refs_2_.refs_3_, ...), custom_call_target="tpu_custom_call" | custom-call | flops 1207959552 | bytes 1572864 | tf_op jit(solution)/shard_map/group/pallas_call | solution.py:239
  100.3 3.3 %collective-permute-done.18.refs_15_ = bf16[3,96,128]{2,1,0:T(8,128)(2,1)S(1)} collective-permute-done((bf16[3,96,128]{2,1,0:T(8,128)(2,1)S(1)}, bf16[3,96,128]{2,1,0:T(8,128)(2,1)S(1)}, u32[]{:S(2)}, u32[]{:S(2)}) %collective-permute-start.18) | collective-permute-done | bytes 73760 | tf_op jit(solution)/shard_map/ppermute | solution.py:267
  103.6 0.3 collective-permute-done.16.refs_14_
  103.9 1.3 %collective-permute-done.23.refs_17_ = bf16[3,96,128]{2,1,0:T(8,128)(2,1)S(1)} collective-permute-done((bf16[3,96,128]{2,1,0:T(8,128)(2,1)S(1)}, bf16[3,96,128]{2,1,0:T(8,128)(2,1)S(1)}, u32[]{:S(2)}, u32[]{:S(2)}) %collective-permute-start.23) | collective-permute-done | bytes 73760 | tf_op jit(solution)/shard_map/ppermute | solution.py:267
  105.2 1.6 %group.5 = (f32[4,32,128]{2,1,0:T(8,128)S(1)}, f32[4,32,128]{2,1,0:T(8,128)S(1)}, f32[4,32,256]{2,1,0:T(8,128)S(1)}) custom-call(s32[3]{0:T(128)S(1)} %pad_add_fusion.refs_0_, bf16[512,512]{1,0:T(8,128)(2,1)S(1)} %ordered_metric.1.refs_0_.refs_1_, bf16[16,32,128]{2,1,0:T(8,128)(2,1)S(1)} %get-tuple-element.53.refs_1_.refs_2_, ...), custom_call_target="tpu_custom_call" | custom-call | flops 603979776 | bytes 786432 | tf_op jit(solution)/shard_map/group/pallas_call | solution.py:239
  106.9 1.3 %collective-permute-done.27 = f32[4,32,256]{2,1,0:T(8,128)S(1)} collective-permute-done((f32[4,32,256]{2,1,0:T(8,128)S(1)}, f32[4,32,256]{2,1,0:T(8,128)S(1)}, u32[]{:S(2)}, u32[]{:S(2)}) %collective-permute-start.27) | collective-permute-done | bytes 131104 | tf_op jit(solution)/shard_map/ppermute | solution.py:270
  108.2 1.0 collective-permute-start.28
  109.2 3.3 %collective-permute-done.28 = f32[4,32,128]{2,1,0:T(8,128)S(1)} collective-permute-done((f32[4,32,128]{2,1,0:T(8,128)S(1)}, f32[4,32,128]{2,1,0:T(8,128)S(1)}, u32[]{:S(2)}, u32[]{:S(2)}) %collective-permute-start.28) | collective-permute-done | bytes 65568 | tf_op jit(solution)/shard_map/ppermute | solution.py:267
  112.6 2.3 %collective-permute-start.29 = (f32[32,128]{1,0:T(8,128)S(1)}, f32[32,128]{1,0:T(8,128)S(1)}, u32[]{:S(2)}, u32[]{:S(2)}) collective-permute-start(f32[32,128]{1,0:T(8,128)S(1)} %get-tuple-element.99), channel_id=1, source_target_pairs={{0,8},{2,10},{4,12},{6,14},{8,0},{10,2},{12,4},{14,6},{1,9},{3,11}... | collective-permute-start | bytes 49160 | tf_op jit(solution)/shard_map/ppermute | solution.py:267
  114.9 0.4 collective-permute-start.31
  115.3 2.3 %collective-permute-start.30 = (f32[32,128]{1,0:T(8,128)S(1)}, f32[32,128]{1,0:T(8,128)S(1)}, u32[]{:S(2)}, u32[]{:S(2)}) collective-permute-start(f32[32,128]{1,0:T(8,128)S(1)} %get-tuple-element.101), channel_id=1, source_target_pairs={{0,12},{2,14},{4,8},{6,10},{8,4},{10,6},{12,0},{14,2},{1,13},{3,15... | collective-permute-start | bytes 49160 | tf_op jit(solution)/shard_map/ppermute | solution.py:267
  117.6 1.2 collective-permute-done.31
  118.8 2.1 %collective-permute-done.30 = f32[32,128]{1,0:T(8,128)S(1)} collective-permute-done((f32[32,128]{1,0:T(8,128)S(1)}, f32[32,128]{1,0:T(8,128)S(1)}, u32[]{:S(2)}, u32[]{:S(2)}) %collective-permute-start.30) | collective-permute-done | bytes 16416 | tf_op jit(solution)/shard_map/ppermute | solution.py:267
  120.8 0.6 fusion.4
  (40 shorter events, 0.7 us)
Async XLA Ops:
  0.0 2.9 %copy-start = (bf16[128,512]{1,0:T(8,128)(2,1)S(1)}, bf16[128,512]{1,0:T(8,128)(2,1)}, u32[]{:S(2)}) copy-start(bf16[128,512]{1,0:T(8,128)(2,1)} %param.8) | copy-start | bytes 393220
  0.0 9.5 %copy-start.1 = (bf16[1024,128]{1,0:T(8,128)(2,1)S(1)}, bf16[1024,128]{1,0:T(8,128)(2,1)}, u32[]{:S(2)}) copy-start(bf16[1024,128]{1,0:T(8,128)(2,1)} %own_ref) | copy-start | bytes 786436
  0.0 9.5 %collective-permute-start.4 = (bf16[1024,128]{1,0:T(8,128)(2,1)}, bf16[1024,128]{1,0:T(8,128)(2,1)S(1)}, u32[]{:S(2)}, u32[]{:S(2)}) collective-permute-start(bf16[1024,128]{1,0:T(8,128)(2,1)} %own_ref), channel_id=1, source_target_pairs={{0,2},{2,0},{4,6},{6,4},{8,10},{10,8},{12,14},{14,12},{1,3},{3,1},... | collective-permute-start | bytes 786440 | tf_op jit(solution)/shard_map/ppermute | solution.py:267
  3.0 5.4 %collective-permute-start = (bf16[32,512]{1,0:T(8,128)(2,1)S(1)}, bf16[32,512]{1,0:T(8,128)(2,1)S(1)}, u32[]{:S(2)}, u32[]{:S(2)}) collective-permute-start(bf16[32,512]{1,0:T(8,128)(2,1)S(1)} %constant_dynamic-slice_fusion), channel_id=1, source_target_pairs={{0,8},{2,10},{4,12},{6,14},{8,0},{10,2},{12,4},{14,6},{1,9},{3,11}... | collective-permute-start | bytes 98312 | tf_op jit(solution)/shard_map/ppermute | solution.py:267
  8.3 69.8 %copy-start.2 = (s32[4]{0:T(128)S(1)}, s32[4]{0:T(128)}, u32[]{:S(2)}) copy-start(s32[4]{0:T(128)} %param.9) | copy-start | bytes 52
  11.2 8.6 %collective-permute-start.8 = (bf16[16,32,128]{2,1,0:T(8,128)(2,1)S(1)}, bf16[16,32,128]{2,1,0:T(8,128)(2,1)S(1)}, u32[]{:S(2)}, u32[]{:S(2)}) collective-permute-start(bf16[16,32,128]{2,1,0:T(8,128)(2,1)S(1)} %get-tuple-element.61), channel_id=1, source_target_pairs={{0,8},{2,10},{4,12},{6,14},{8,0},{10,2},{12,4},{14,6},{1,9},{3,11}... | collective-permute-start | bytes 393224 | tf_op jit(solution)/shard_map/ppermute | solution.py:267
  14.1 11.2 %collective-permute-start.5 = (bf16[16,32,128]{2,1,0:T(8,128)(2,1)S(1)}, bf16[16,32,128]{2,1,0:T(8,128)(2,1)S(1)}, u32[]{:S(2)}, u32[]{:S(2)}) collective-permute-start(bf16[16,32,128]{2,1,0:T(8,128)(2,1)S(1)} %get-tuple-element.54), channel_id=1, source_target_pairs={{0,2},{2,0},{4,6},{6,4},{8,10},{10,8},{12,14},{14,12},{1,3},{3,1},... | collective-permute-start | bytes 393224 | tf_op jit(solution)/shard_map/ppermute | solution.py:267
  15.6 17.7 %collective-permute-start.7 = (bf16[16,32,128]{2,1,0:T(8,128)(2,1)S(1)}, bf16[16,32,128]{2,1,0:T(8,128)(2,1)S(1)}, u32[]{:S(2)}, u32[]{:S(2)}) collective-permute-start(bf16[16,32,128]{2,1,0:T(8,128)(2,1)S(1)} %get-tuple-element.60), channel_id=1, source_target_pairs={{0,6},{2,4},{4,2},{6,0},{8,14},{10,12},{12,10},{14,8},{1,7},{3,5},... | collective-permute-start | bytes 393224 | tf_op jit(solution)/shard_map/ppermute | solution.py:267
  17.1 16.1 %collective-permute-start.9 = (bf16[16,32,128]{2,1,0:T(8,128)(2,1)S(1)}, bf16[16,32,128]{2,1,0:T(8,128)(2,1)S(1)}, u32[]{:S(2)}, u32[]{:S(2)}) collective-permute-start(bf16[16,32,128]{2,1,0:T(8,128)(2,1)S(1)} %get-tuple-element.62), channel_id=1, source_target_pairs={{0,10},{2,8},{4,14},{6,12},{8,2},{10,0},{12,6},{14,4},{1,11},{3,9}... | collective-permute-start | bytes 393224 | tf_op jit(solution)/shard_map/ppermute | solution.py:267
  18.4 19.3 %collective-permute-start.1 = (bf16[64,512]{1,0:T(8,128)(2,1)S(1)}, bf16[64,512]{1,0:T(8,128)(2,1)S(1)}, u32[]{:S(2)}, u32[]{:S(2)}) collective-permute-start(bf16[64,512]{1,0:T(8,128)(2,1)S(1)} %pad_maximum_fusion.2), channel_id=1, source_target_pairs={{0,4},{2,6},{4,0},{6,2},{8,12},{10,14},{12,8},{14,10},{1,5},{3,7},... | collective-permute-start | bytes 196616 | tf_op jit(solution)/shard_map/ppermute | solution.py:267
  19.8 18.0 %collective-permute-start.10 = (bf16[16,32,128]{2,1,0:T(8,128)(2,1)S(1)}, bf16[16,32,128]{2,1,0:T(8,128)(2,1)S(1)}, u32[]{:S(2)}, u32[]{:S(2)}) collective-permute-start(bf16[16,32,128]{2,1,0:T(8,128)(2,1)S(1)} %get-tuple-element.63), channel_id=1, source_target_pairs={{0,12},{2,14},{4,8},{6,10},{8,4},{10,6},{12,0},{14,2},{1,13},{3,15... | collective-permute-start | bytes 393224 | tf_op jit(solution)/shard_map/ppermute | solution.py:267
  25.3 14.0 %collective-permute-start.11 = (bf16[16,32,128]{2,1,0:T(8,128)(2,1)S(1)}, bf16[16,32,128]{2,1,0:T(8,128)(2,1)S(1)}, u32[]{:S(2)}, u32[]{:S(2)}) collective-permute-start(bf16[16,32,128]{2,1,0:T(8,128)(2,1)S(1)} %get-tuple-element.65), channel_id=1, source_target_pairs={{0,14},{2,12},{4,10},{6,8},{8,6},{10,4},{12,2},{14,0},{1,15},{3,13... | collective-permute-start | bytes 393224 | tf_op jit(solution)/shard_map/ppermute | solution.py:267
  33.3 6.6 %collective-permute-start.6 = (bf16[16,32,128]{2,1,0:T(8,128)(2,1)S(1)}, bf16[16,32,128]{2,1,0:T(8,128)(2,1)S(1)}, u32[]{:S(2)}, u32[]{:S(2)}) collective-permute-start(bf16[16,32,128]{2,1,0:T(8,128)(2,1)S(1)} %get-tuple-element.59), channel_id=1, source_target_pairs={{0,4},{2,6},{4,0},{6,2},{8,12},{10,14},{12,8},{14,10},{1,5},{3,7},... | collective-permute-start | bytes 393224 | tf_op jit(solution)/shard_map/ppermute | solution.py:267
  33.3 19.2 %collective-permute-start.24 = (bf16[7,96,128]{2,1,0:T(8,128)(2,1)S(1)}, bf16[7,96,128]{2,1,0:T(8,128)(2,1)S(1)}, u32[]{:S(2)}, u32[]{:S(2)}) collective-permute-start(bf16[7,96,128]{2,1,0:T(8,128)(2,1)S(1)} %get-tuple-element.93), channel_id=1, source_target_pairs={{0,8},{2,10},{4,12},{6,14},{8,0},{10,2},{12,4},{14,6},{1,9},{3,11}... | collective-permute-start | bytes 516104 | tf_op jit(solution)/shard_map/ppermute | solution.py:267
  37.7 18.8 %collective-permute-start.14 = (bf16[7,96,128]{2,1,0:T(8,128)(2,1)S(1)}, bf16[7,96,128]{2,1,0:T(8,128)(2,1)S(1)}, u32[]{:S(2)}, u32[]{:S(2)}) collective-permute-start(bf16[7,96,128]{2,1,0:T(8,128)(2,1)S(1)} %get-tuple-element.73), channel_id=1, source_target_pairs={{0,10},{2,8},{4,14},{6,12},{8,2},{10,0},{12,6},{14,4},{1,11},{3,9}... | collective-permute-start | bytes 516104 | tf_op jit(solution)/shard_map/ppermute | solution.py:267
  37.8 22.3 %collective-permute-start.2 = (bf16[128,512]{1,0:T(8,128)(2,1)S(1)}, bf16[128,512]{1,0:T(8,128)(2,1)S(1)}, u32[]{:S(2)}, u32[]{:S(2)}) collective-permute-start(bf16[128,512]{1,0:T(8,128)(2,1)S(1)} %pad_maximum_fusion.1), channel_id=1, source_target_pairs={{0,2},{2,0},{4,6},{6,4},{8,10},{10,8},{12,14},{14,12},{1,3},{3,1},... | collective-permute-start | bytes 393224 | tf_op jit(solution)/shard_map/ppermute | solution.py:267
  39.3 20.9 %collective-permute-start.12 = (bf16[16,96,128]{2,1,0:T(8,128)(2,1)S(1)}, bf16[16,96,128]{2,1,0:T(8,128)(2,1)S(1)}, u32[]{:S(2)}, u32[]{:S(2)}) collective-permute-start(bf16[16,96,128]{2,1,0:T(8,128)(2,1)S(1)} %get-tuple-element.68), channel_id=1, source_target_pairs={{0,2},{2,0},{4,6},{6,4},{8,10},{10,8},{12,14},{14,12},{1,3},{3,1},... | collective-permute-start | bytes 1179656 | tf_op jit(solution)/shard_map/ppermute | solution.py:267
  39.9 20.2 %collective-permute-start.19 = (bf16[7,96,128]{2,1,0:T(8,128)(2,1)S(1)}, bf16[7,96,128]{2,1,0:T(8,128)(2,1)S(1)}, u32[]{:S(2)}, u32[]{:S(2)}) collective-permute-start(bf16[7,96,128]{2,1,0:T(8,128)(2,1)S(1)} %get-tuple-element.84), channel_id=1, source_target_pairs={{0,12},{2,14},{4,8},{6,10},{8,4},{10,6},{12,0},{14,2},{1,13},{3,15... | collective-permute-start | bytes 516104 | tf_op jit(solution)/shard_map/ppermute | solution.py:267
  52.5 20.5 %collective-permute-start.13 = (bf16[16,96,128]{2,1,0:T(8,128)(2,1)S(1)}, bf16[16,96,128]{2,1,0:T(8,128)(2,1)S(1)}, u32[]{:S(2)}, u32[]{:S(2)}) collective-permute-start(bf16[16,96,128]{2,1,0:T(8,128)(2,1)S(1)} %get-tuple-element.70), channel_id=1, source_target_pairs={{0,4},{2,6},{4,0},{6,2},{8,12},{10,14},{12,8},{14,10},{1,5},{3,7},... | collective-permute-start | bytes 1179656 | tf_op jit(solution)/shard_map/ppermute | solution.py:267
  56.5 13.7 %collective-permute-start.25 = (bf16[7,96,128]{2,1,0:T(8,128)(2,1)S(1)}, bf16[7,96,128]{2,1,0:T(8,128)(2,1)S(1)}, u32[]{:S(2)}, u32[]{:S(2)}) collective-permute-start(bf16[7,96,128]{2,1,0:T(8,128)(2,1)S(1)} %get-tuple-element.94), channel_id=1, source_target_pairs={{0,14},{2,12},{4,10},{6,8},{8,6},{10,4},{12,2},{14,0},{1,15},{3,13... | collective-permute-start | bytes 516104 | tf_op jit(solution)/shard_map/ppermute | solution.py:267
  60.0 32.9 %collective-permute-start.15 = (bf16[16,96,128]{2,1,0:T(8,128)(2,1)S(1)}, bf16[16,96,128]{2,1,0:T(8,128)(2,1)S(1)}, u32[]{:S(2)}, u32[]{:S(2)}) collective-permute-start(bf16[16,96,128]{2,1,0:T(8,128)(2,1)S(1)} %get-tuple-element.74), channel_id=1, source_target_pairs={{0,6},{2,4},{4,2},{6,0},{8,14},{10,12},{12,10},{14,8},{1,7},{3,5},... | collective-permute-start | bytes 1179656 | tf_op jit(solution)/shard_map/ppermute | solution.py:267
  60.1 16.4 %collective-permute-start.3 = (bf16[256,512]{1,0:T(8,128)(2,1)S(1)}, bf16[256,512]{1,0:T(8,128)(2,1)S(1)}, u32[]{:S(2)}, u32[]{:S(2)}) collective-permute-start(bf16[256,512]{1,0:T(8,128)(2,1)S(1)} %pad_maximum_fusion.refs_0_), channel_id=1, source_target_pairs={{0,1},{1,0},{2,3},{3,2},{4,5},{5,4},{6,7},{7,6},{8,9},{9,8},{10,11... | collective-permute-start | bytes 786440 | tf_op jit(solution)/shard_map/ppermute | solution.py:270
  60.2 18.7 %collective-permute-start.20 = (bf16[6,96,128]{2,1,0:T(8,128)(2,1)S(1)}, bf16[6,96,128]{2,1,0:T(8,128)(2,1)S(1)}, u32[]{:S(2)}, u32[]{:S(2)}) collective-permute-start(bf16[6,96,128]{2,1,0:T(8,128)(2,1)S(1)} %get-tuple-element.85), channel_id=1, source_target_pairs={{0,10},{2,8},{4,14},{6,12},{8,2},{10,0},{12,6},{14,4},{1,11},{3,9}... | collective-permute-start | bytes 442376 | tf_op jit(solution)/shard_map/ppermute | solution.py:267
  70.2 22.5 %collective-permute-start.17 = (bf16[6,96,128]{2,1,0:T(8,128)(2,1)S(1)}, bf16[6,96,128]{2,1,0:T(8,128)(2,1)S(1)}, u32[]{:S(2)}, u32[]{:S(2)}) collective-permute-start(bf16[6,96,128]{2,1,0:T(8,128)(2,1)S(1)} %get-tuple-element.79), channel_id=1, source_target_pairs={{0,8},{2,10},{4,12},{6,14},{8,0},{10,2},{12,4},{14,6},{1,9},{3,11}... | collective-permute-start | bytes 442376 | tf_op jit(solution)/shard_map/ppermute | solution.py:267
  73.0 25.6 %collective-permute-start.26 = (bf16[6,96,128]{2,1,0:T(8,128)(2,1)S(1)}, bf16[6,96,128]{2,1,0:T(8,128)(2,1)S(1)}, u32[]{:S(2)}, u32[]{:S(2)}) collective-permute-start(bf16[6,96,128]{2,1,0:T(8,128)(2,1)S(1)} %get-tuple-element.95), channel_id=1, source_target_pairs={{0,12},{2,14},{4,8},{6,10},{8,4},{10,6},{12,0},{14,2},{1,13},{3,15... | collective-permute-start | bytes 442376 | tf_op jit(solution)/shard_map/ppermute | solution.py:267
  76.5 21.7 %collective-permute-start.22 = (bf16[6,96,128]{2,1,0:T(8,128)(2,1)S(1)}, bf16[6,96,128]{2,1,0:T(8,128)(2,1)S(1)}, u32[]{:S(2)}, u32[]{:S(2)}) collective-permute-start(bf16[6,96,128]{2,1,0:T(8,128)(2,1)S(1)} %get-tuple-element.89), channel_id=1, source_target_pairs={{0,14},{2,12},{4,10},{6,8},{8,6},{10,4},{12,2},{14,0},{1,15},{3,13... | collective-permute-start | bytes 442376 | tf_op jit(solution)/shard_map/ppermute | solution.py:267
  78.9 21.4 %collective-permute-start.21 = (bf16[3,96,128]{2,1,0:T(8,128)(2,1)S(1)}, bf16[3,96,128]{2,1,0:T(8,128)(2,1)S(1)}, u32[]{:S(2)}, u32[]{:S(2)}) collective-permute-start(bf16[3,96,128]{2,1,0:T(8,128)(2,1)S(1)} %get-tuple-element.86), channel_id=1, source_target_pairs={{0,12},{2,14},{4,8},{6,10},{8,4},{10,6},{12,0},{14,2},{1,13},{3,15... | collective-permute-start | bytes 221192 | tf_op jit(solution)/shard_map/ppermute | solution.py:267
  92.7 10.8 %collective-permute-start.18 = (bf16[3,96,128]{2,1,0:T(8,128)(2,1)S(1)}, bf16[3,96,128]{2,1,0:T(8,128)(2,1)S(1)}, u32[]{:S(2)}, u32[]{:S(2)}) collective-permute-start(bf16[3,96,128]{2,1,0:T(8,128)(2,1)S(1)} %get-tuple-element.80), channel_id=1, source_target_pairs={{0,10},{2,8},{4,14},{6,12},{8,2},{10,0},{12,6},{14,4},{1,11},{3,9}... | collective-permute-start | bytes 221192 | tf_op jit(solution)/shard_map/ppermute | solution.py:267
  92.9 11.0 %collective-permute-start.16 = (bf16[3,96,128]{2,1,0:T(8,128)(2,1)S(1)}, bf16[3,96,128]{2,1,0:T(8,128)(2,1)S(1)}, u32[]{:S(2)}, u32[]{:S(2)}) collective-permute-start(bf16[3,96,128]{2,1,0:T(8,128)(2,1)S(1)} %get-tuple-element.76), channel_id=1, source_target_pairs={{0,8},{2,10},{4,12},{6,14},{8,0},{10,2},{12,4},{14,6},{1,9},{3,11}... | collective-permute-start | bytes 221192 | tf_op jit(solution)/shard_map/ppermute | solution.py:267
  98.1 7.1 %collective-permute-start.23 = (bf16[3,96,128]{2,1,0:T(8,128)(2,1)S(1)}, bf16[3,96,128]{2,1,0:T(8,128)(2,1)S(1)}, u32[]{:S(2)}, u32[]{:S(2)}) collective-permute-start(bf16[3,96,128]{2,1,0:T(8,128)(2,1)S(1)} %get-tuple-element.90), channel_id=1, source_target_pairs={{0,14},{2,12},{4,10},{6,8},{8,6},{10,4},{12,2},{14,0},{1,15},{3,13... | collective-permute-start | bytes 221192 | tf_op jit(solution)/shard_map/ppermute | solution.py:267
  106.8 1.4 %collective-permute-start.27 = (f32[4,32,256]{2,1,0:T(8,128)S(1)}, f32[4,32,256]{2,1,0:T(8,128)S(1)}, u32[]{:S(2)}, u32[]{:S(2)}) collective-permute-start(f32[4,32,256]{2,1,0:T(8,128)S(1)} %get-tuple-element.97), channel_id=1, source_target_pairs={{0,1},{1,0},{2,3},{3,2},{4,5},{5,4},{6,7},{7,6},{8,9},{9,8},{10,11... | collective-permute-start | bytes 393224 | tf_op jit(solution)/shard_map/ppermute | solution.py:270
  108.2 4.3 %collective-permute-start.28 = (f32[4,32,128]{2,1,0:T(8,128)S(1)}, f32[4,32,128]{2,1,0:T(8,128)S(1)}, u32[]{:S(2)}, u32[]{:S(2)}) collective-permute-start(f32[4,32,128]{2,1,0:T(8,128)S(1)} %slice_add_fusion), channel_id=1, source_target_pairs={{0,2},{2,0},{4,6},{6,4},{8,10},{10,8},{12,14},{14,12},{1,3},{3,1},... | collective-permute-start | bytes 196616 | tf_op jit(solution)/shard_map/ppermute | solution.py:267
  112.6 5.0 %collective-permute-start.29 = (f32[32,128]{1,0:T(8,128)S(1)}, f32[32,128]{1,0:T(8,128)S(1)}, u32[]{:S(2)}, u32[]{:S(2)}) collective-permute-start(f32[32,128]{1,0:T(8,128)S(1)} %get-tuple-element.99), channel_id=1, source_target_pairs={{0,8},{2,10},{4,12},{6,14},{8,0},{10,2},{12,4},{14,6},{1,9},{3,11}... | collective-permute-start | bytes 49160 | tf_op jit(solution)/shard_map/ppermute | solution.py:267
  114.9 3.9 %collective-permute-start.31 = (f32[32,128]{1,0:T(8,128)S(1)}, f32[32,128]{1,0:T(8,128)S(1)}, u32[]{:S(2)}, u32[]{:S(2)}) collective-permute-start(f32[32,128]{1,0:T(8,128)S(1)} %get-tuple-element.100), channel_id=1, source_target_pairs={{0,4},{2,6},{4,0},{6,2},{8,12},{10,14},{12,8},{14,10},{1,5},{3,7},... | collective-permute-start | bytes 49160 | tf_op jit(solution)/shard_map/ppermute | solution.py:267
  115.3 5.5 %collective-permute-start.30 = (f32[32,128]{1,0:T(8,128)S(1)}, f32[32,128]{1,0:T(8,128)S(1)}, u32[]{:S(2)}, u32[]{:S(2)}) collective-permute-start(f32[32,128]{1,0:T(8,128)S(1)} %get-tuple-element.101), channel_id=1, source_target_pairs={{0,12},{2,14},{4,8},{6,10},{8,4},{10,6},{12,0},{14,2},{1,13},{3,15... | collective-permute-start | bytes 49160 | tf_op jit(solution)/shard_map/ppermute | solution.py:267

commit v4 on v3

--- a/solution.py
+++ b/solution.py
@@ -14,9 +14,13 @@
 GROUPS = ((0, 7), (7, 13), (13, 16))
 FIRST = 32
 OPEN = (4, 1, 5, 3, 6, 7)
-ORDER = ((2, -1), (4, 0), (5, 0), (1, 0), (6, 0), (2, 0), (7, 0), (3, 0), (4, 1), (5, 1), (7, 1), (6, 1), (4, 2), (5, 2), (6, 2), (7, 2))
+ORDER = (
+    ((2, -1), (4, 0), (5, 0), (1, 0), (6, 0), (2, 0), (7, 0), (3, 0))
+    + ((4, 1), (5, 1), (7, 1), (6, 1))
+    + ((7, 2), (4, 2), (5, 2), (6, 2))
+)
 RESTDEP = 1
-LAST = (2, 3, 1)
+LAST = (3, 2, 1)
 WHOLE = pl.BlockSpec(memory_space=pltpu.VMEM)
 
 
@@ -60,49 +64,36 @@
 def first_kernel(chips, where, own_ref, other_ref, x_ref, *rest):
     outs, table_ref, plain = rest[:chips], rest[chips], rest[chips + 1]
     share = table_ref.shape[0] // chips
-
-    @pl.when(pl.program_id(0) == 0)
-    def _():
-        block = plain.shape[0]
-        held = own_ref.shape[0] // block
-        for s in range(plain.shape[1] // block):
-            name = where[2 + s]
-            away = lax.div(name, held) != where[1]
-            start = pl.multiple_of(lax.rem(name, held) * block, block)
-            mine = own_ref[pl.ds(start, block), :].astype(F32)
-            theirs = other_ref[pl.ds(start, block), :].astype(F32)
-            picked = jnp.where(away, theirs, mine)
-            plain[:, s * block : (s + 1) * block] = picked.T.astype(BF16)
+    block = plain.shape[0]
+    held = own_ref.shape[0] // block
+    for s in range(plain.shape[1] // block):
+        name = where[2 + s]
+        away = lax.div(name, held) != where[1]
+        start = pl.multiple_of(lax.rem(name, held) * block, block)
+        mine = own_ref[pl.ds(start, block), :].astype(F32)
+        theirs = other_ref[pl.ds(start, block), :].astype(F32)
+        picked = jnp.where(away, theirs, mine)
+        plain[:, s * block : (s + 1) * block] = picked.T.astype(BF16)
+    for k in range(chips):
+        start = pl.multiple_of((where[0] ^ k) * share, share)
+        table_ref[k * share : (k + 1) * share, :] = plain[pl.ds(start, share), :]
+    for at in range(0, x_ref.shape[0], ROWS):
+        value = products(table_ref[...], x_ref[at : at + ROWS])
         for k in range(chips):
-            start = pl.multiple_of((where[0] ^ k) * share, share)
-            table_ref[k * share : (k + 1) * share, :] = plain[pl.ds(start, share), :]
-
-    value = products(table_ref[...], x_ref[...])
-    for k in range(chips):
-        outs[k][...] = value[k * share : (k + 1) * share]
+            outs[k][:, at : at + ROWS, :] = value[k * share : (k + 1) * share]
 
 
 def first_products(chips, where, own, other, moved, first):
     _, depth, width = moved.shape
     orbitals = own.shape[1]
     share = orbitals // chips
-    whole = lambda shape: pl.BlockSpec(shape, lambda j, w: (0,) * len(shape))
     return pl.pallas_call(
         functools.partial(first_kernel, chips),
-        grid_spec=pltpu.PrefetchScalarGridSpec(
-            num_scalar_prefetch=1,
-            grid=(first // ROWS,),
-            in_specs=[
-                whole(own.shape),
-                whole(other.shape),
-                pl.BlockSpec((ROWS, depth, width), lambda j, w: (j, 0, 0)),
-            ],
-            out_specs=[pl.BlockSpec((share, ROWS, width), lambda j, w: (0, j, 0))] * chips
-            + [whole((orbitals, depth))],
-            scratch_shapes=[pltpu.VMEM((orbitals, depth), BF16)],
-        ),
+        in_specs=[pl.BlockSpec(memory_space=pltpu.SMEM)] + [WHOLE] * 3,
+        out_specs=[WHOLE] * (chips + 1),
         out_shape=[jax.ShapeDtypeStruct((share, first, width), BF16)] * chips
         + [jax.ShapeDtypeStruct((orbitals, depth), BF16)],
+        scratch_shapes=[pltpu.VMEM((orbitals, depth), BF16)],
         compiler_params=params(),
         cost_estimate=cost(orbitals * depth * first * width, moved.size * 2),
         name="first_products",

time: 122 us -> 120 us (0.984)
  starting transfers between devices: 54.6 us -> 53.3 us
    ppermute x30, starting transfers between devices: 54.4 us -> 53.1 us  [swap(): return lax.ppermute(value, ('aux', 'bas'), pairs)]
where the time goes in v4:
time: 120 us
  starting transfers between devices  53.3 us (44%)
  waiting for transfers between devices  49 us (41%)
  Pallas kernels  16 us (13%)
  other arithmetic  1.55 us (1%)
    ppermute x30, starting transfers between devices, swap(): return lax.ppermute(value, ('aux', 'bas'), pairs)  53.1 us
    ppermute x30, waiting for transfers between devices, swap(): return lax.ppermute(value, ('aux', 'bas'), pairs)  47.6 us
    pallas_call x1, Pallas kernels, rest_products(): pl.pallas_call(functools.partial(rest_kernel, chips, spans), grid=(rest /...  7.04 us
    pallas_call x3, Pallas kernels, group(): pl.pallas_call(functools.partial(group_kernel, aux, bas, lo, hi, starts,...  5.01 us
  transfers between devices with their start and end apart: 32, of which 14 were waited for; matrix products, arithmetic and copies ran while one was open for 1% of the time, Pallas kernels for 11%

profile of v4, /device:TPU:0, one launch (start us, length us, event | category | flops | bytes accessed | tf_op | source)
XLA Modules:
  0.0 120.0 jit_solution(5549369550090801457)
XLA Ops:
  0.0 2.9 %collective-permute-start.4 = (bf16[1024,128]{1,0:T(8,128)(2,1)}, bf16[1024,128]{1,0:T(8,128)(2,1)S(1)}, u32[]{:S(2)}, u32[]{:S(2)}) collective-permute-start(bf16[1024,128]{1,0:T(8,128)(2,1)} %own_ref), channel_id=1, source_target_pairs={{0,2},{2,0},{4,6},{6,4},{8,10},{10,8},{12,14},{14,12},{1,3},{3,1},... | collective-permute-start | bytes 786440 | tf_op jit(solution)/shard_map/ppermute | solution.py:258
  3.0 2.6 %collective-permute-start = (bf16[32,512]{1,0:T(8,128)(2,1)S(1)}, bf16[32,512]{1,0:T(8,128)(2,1)S(1)}, u32[]{:S(2)}, u32[]{:S(2)}) collective-permute-start(bf16[32,512]{1,0:T(8,128)(2,1)S(1)} %constant_dynamic-slice_fusion), channel_id=1, source_target_pairs={{0,8},{2,10},{4,12},{6,14},{8,0},{10,2},{12,4},{14,6},{1,9},{3,11}... | collective-permute-start | bytes 98312 | tf_op jit(solution)/shard_map/ppermute | solution.py:258
  5.5 0.7 pad_add_fusion.2.where
  6.3 2.0 %relayout.1.x_ref = bf16[32,256,128]{2,1,0:T(8,128)(2,1)S(1)} custom-call(bf16[2,128,128,128]{3,2,1,0:T(8,128)(2,1)} %bitcast.24), custom_call_target="tpu_custom_call" | custom-call | bytes 4194304 | tf_op jit(solution)/shard_map/relayout/pallas_call | solution.py:42
  8.3 1.2 collective-permute-done.4.other_ref
  9.5 1.2 %first_products.1 = (bf16[16,32,128]{2,1,0:T(8,128)(2,1)S(1)}, bf16[16,32,128]{2,1,0:T(8,128)(2,1)S(1)}, bf16[16,32,128]{2,1,0:T(8,128)(2,1)S(1)}, bf16[16,32,12...) custom-call(s32[4]{0:T(128)S(1)} %pad_add_fusion.2.where, ...), custom_call_target="tpu_custom_call" | custom-call | flops 268435456 | bytes 2097152 | tf_op jit(solution)/shard_map/first_products/pallas_call | solution.py:90
  10.7 2.9 %collective-permute-start.8 = (bf16[16,32,128]{2,1,0:T(8,128)(2,1)S(1)}, bf16[16,32,128]{2,1,0:T(8,128)(2,1)S(1)}, u32[]{:S(2)}, u32[]{:S(2)}) collective-permute-start(bf16[16,32,128]{2,1,0:T(8,128)(2,1)S(1)} %get-tuple-element.61), channel_id=1, source_target_pairs={{0,8},{2,10},{4,12},{6,14},{8,0},{10,2},{12,4},{14,6},{1,9},{3,11}... | collective-permute-start | bytes 393224 | tf_op jit(solution)/shard_map/ppermute | solution.py:258
  13.6 1.5 %collective-permute-start.5 = (bf16[16,32,128]{2,1,0:T(8,128)(2,1)S(1)}, bf16[16,32,128]{2,1,0:T(8,128)(2,1)S(1)}, u32[]{:S(2)}, u32[]{:S(2)}) collective-permute-start(bf16[16,32,128]{2,1,0:T(8,128)(2,1)S(1)} %get-tuple-element.54), channel_id=1, source_target_pairs={{0,2},{2,0},{4,6},{6,4},{8,10},{10,8},{12,14},{14,12},{1,3},{3,1},... | collective-permute-start | bytes 393224 | tf_op jit(solution)/shard_map/ppermute | solution.py:258
  15.1 1.5 %collective-permute-start.7 = (bf16[16,32,128]{2,1,0:T(8,128)(2,1)S(1)}, bf16[16,32,128]{2,1,0:T(8,128)(2,1)S(1)}, u32[]{:S(2)}, u32[]{:S(2)}) collective-permute-start(bf16[16,32,128]{2,1,0:T(8,128)(2,1)S(1)} %get-tuple-element.60), channel_id=1, source_target_pairs={{0,6},{2,4},{4,2},{6,0},{8,14},{10,12},{12,10},{14,8},{1,7},{3,5},... | collective-permute-start | bytes 393224 | tf_op jit(solution)/shard_map/ppermute | solution.py:258
  16.7 1.3 %collective-permute-start.9 = (bf16[16,32,128]{2,1,0:T(8,128)(2,1)S(1)}, bf16[16,32,128]{2,1,0:T(8,128)(2,1)S(1)}, u32[]{:S(2)}, u32[]{:S(2)}) collective-permute-start(bf16[16,32,128]{2,1,0:T(8,128)(2,1)S(1)} %get-tuple-element.62), channel_id=1, source_target_pairs={{0,10},{2,8},{4,14},{6,12},{8,2},{10,0},{12,6},{14,4},{1,11},{3,9}... | collective-permute-start | bytes 393224 | tf_op jit(solution)/shard_map/ppermute | solution.py:258
  17.9 0.4 collective-permute-start.1
  18.4 0.9 collective-permute-done.8.refs_5_.refs_6_
  19.3 5.5 %collective-permute-start.10 = (bf16[16,32,128]{2,1,0:T(8,128)(2,1)S(1)}, bf16[16,32,128]{2,1,0:T(8,128)(2,1)S(1)}, u32[]{:S(2)}, u32[]{:S(2)}) collective-permute-start(bf16[16,32,128]{2,1,0:T(8,128)(2,1)S(1)} %get-tuple-element.63), channel_id=1, source_target_pairs={{0,12},{2,14},{4,8},{6,10},{8,4},{10,6},{12,0},{14,2},{1,13},{3,15... | collective-permute-start | bytes 393224 | tf_op jit(solution)/shard_map/ppermute | solution.py:258
  24.8 0.9 collective-permute-start.11
  25.8 7.0 %rest_products.1 = (bf16[7,96,128]{2,1,0:T(8,128)(2,1)S(1)}, bf16[7,96,128]{2,1,0:T(8,128)(2,1)S(1)}, bf16[7,96,128]{2,1,0:T(8,128)(2,1)S(1)}, bf16[7,96,128]{2,...) custom-call(bf16[2,128,128,128]{3,2,1,0:T(8,128)(2,1)} %bitcast.25, ...), custom_call_target="tpu_custom_call" | custom-call | flops 805306368 | bytes 8388608 | tf_op jit(solution)/shard_map/rest_products/pallas_call | solution.py:118
  32.9 4.4 %collective-permute-start.24 = (bf16[7,96,128]{2,1,0:T(8,128)(2,1)S(1)}, bf16[7,96,128]{2,1,0:T(8,128)(2,1)S(1)}, u32[]{:S(2)}, u32[]{:S(2)}) collective-permute-start(bf16[7,96,128]{2,1,0:T(8,128)(2,1)S(1)} %get-tuple-element.93), channel_id=1, source_target_pairs={{0,8},{2,10},{4,12},{6,14},{8,0},{10,2},{12,4},{14,6},{1,9},{3,11}... | collective-permute-start | bytes 516104 | tf_op jit(solution)/shard_map/ppermute | solution.py:258
  37.3 1.5 %collective-permute-start.2 = (bf16[128,512]{1,0:T(8,128)(2,1)S(1)}, bf16[128,512]{1,0:T(8,128)(2,1)S(1)}, u32[]{:S(2)}, u32[]{:S(2)}) collective-permute-start(bf16[128,512]{1,0:T(8,128)(2,1)S(1)} %pad_maximum_fusion.1), channel_id=1, source_target_pairs={{0,2},{2,0},{4,6},{6,4},{8,10},{10,8},{12,14},{14,12},{1,3},{3,1},... | collective-permute-start | bytes 393224 | tf_op jit(solution)/shard_map/ppermute | solution.py:258
  38.8 0.6 collective-permute-start.12
  39.4 2.5 %collective-permute-start.18 = (bf16[7,96,128]{2,1,0:T(8,128)(2,1)S(1)}, bf16[7,96,128]{2,1,0:T(8,128)(2,1)S(1)}, u32[]{:S(2)}, u32[]{:S(2)}) collective-permute-start(bf16[7,96,128]{2,1,0:T(8,128)(2,1)S(1)} %get-tuple-element.82), channel_id=1, source_target_pairs={{0,12},{2,14},{4,8},{6,10},{8,4},{10,6},{12,0},{14,2},{1,13},{3,15... | collective-permute-start | bytes 516104 | tf_op jit(solution)/shard_map/ppermute | solution.py:258
  41.9 10.2 %collective-permute-done.24.refs_13_ = bf16[7,96,128]{2,1,0:T(8,128)(2,1)S(1)} collective-permute-done((bf16[7,96,128]{2,1,0:T(8,128)(2,1)S(1)}, bf16[7,96,128]{2,1,0:T(8,128)(2,1)S(1)}, u32[]{:S(2)}, u32[]{:S(2)}) %collective-permute-start.24) | collective-permute-done | bytes 172064 | tf_op jit(solution)/shard_map/ppermute | solution.py:258
  52.1 0.3 collective-permute-start.13
  52.4 3.6 %collective-permute-done.14.refs_14_ = bf16[7,96,128]{2,1,0:T(8,128)(2,1)S(1)} collective-permute-done((bf16[7,96,128]{2,1,0:T(8,128)(2,1)S(1)}, bf16[7,96,128]{2,1,0:T(8,128)(2,1)S(1)}, u32[]{:S(2)}, u32[]{:S(2)}) %collective-permute-start.14) | collective-permute-done | bytes 172064 | tf_op jit(solution)/shard_map/ppermute | solution.py:258
  56.0 3.5 %collective-permute-start.25 = (bf16[7,96,128]{2,1,0:T(8,128)(2,1)S(1)}, bf16[7,96,128]{2,1,0:T(8,128)(2,1)S(1)}, u32[]{:S(2)}, u32[]{:S(2)}) collective-permute-start(bf16[7,96,128]{2,1,0:T(8,128)(2,1)S(1)} %get-tuple-element.94), channel_id=1, source_target_pairs={{0,14},{2,12},{4,10},{6,8},{8,6},{10,4},{12,2},{14,0},{1,15},{3,13... | collective-permute-start | bytes 516104 | tf_op jit(solution)/shard_map/ppermute | solution.py:258
  59.7 2.7 %collective-permute-start.19 = (bf16[6,96,128]{2,1,0:T(8,128)(2,1)S(1)}, bf16[6,96,128]{2,1,0:T(8,128)(2,1)S(1)}, u32[]{:S(2)}, u32[]{:S(2)}) collective-permute-start(bf16[6,96,128]{2,1,0:T(8,128)(2,1)S(1)} %get-tuple-element.83), channel_id=1, source_target_pairs={{0,10},{2,8},{4,14},{6,12},{8,2},{10,0},{12,6},{14,4},{1,11},{3,9}... | collective-permute-start | bytes 442376 | tf_op jit(solution)/shard_map/ppermute | solution.py:258
  62.5 7.3 %collective-permute-done.25.refs_16_ = bf16[7,96,128]{2,1,0:T(8,128)(2,1)S(1)} collective-permute-done((bf16[7,96,128]{2,1,0:T(8,128)(2,1)S(1)}, bf16[7,96,128]{2,1,0:T(8,128)(2,1)S(1)}, u32[]{:S(2)}, u32[]{:S(2)}) %collective-permute-start.25) | collective-permute-done | bytes 172064 | tf_op jit(solution)/shard_map/ppermute | solution.py:258
  69.7 0.1 collective-permute-start.16
  69.9 2.8 %collective-permute-done.13.refs_11_.refs_12_ = bf16[16,96,128]{2,1,0:T(8,128)(2,1)S(1)} collective-permute-done((bf16[16,96,128]{2,1,0:T(8,128)(2,1)S(1)}, bf16[16,96,128]{2,1,0:T(8,128)(2,1)S(1)}, u32[]{:S(2)}, u32[]{:S(2)}) %collective-permute-start.13) | collective-permute-done | bytes 393248 | tf_op jit(solution)/shard_map/ppermute | solution.py:258
  72.7 3.3 %collective-permute-start.26 = (bf16[6,96,128]{2,1,0:T(8,128)(2,1)S(1)}, bf16[6,96,128]{2,1,0:T(8,128)(2,1)S(1)}, u32[]{:S(2)}, u32[]{:S(2)}) collective-permute-start(bf16[6,96,128]{2,1,0:T(8,128)(2,1)S(1)} %get-tuple-element.95), channel_id=1, source_target_pairs={{0,12},{2,14},{4,8},{6,10},{8,4},{10,6},{12,0},{14,2},{1,13},{3,15... | collective-permute-start | bytes 442376 | tf_op jit(solution)/shard_map/ppermute | solution.py:258
  76.0 1.7 %collective-permute-start.21 = (bf16[6,96,128]{2,1,0:T(8,128)(2,1)S(1)}, bf16[6,96,128]{2,1,0:T(8,128)(2,1)S(1)}, u32[]{:S(2)}, u32[]{:S(2)}) collective-permute-start(bf16[6,96,128]{2,1,0:T(8,128)(2,1)S(1)} %get-tuple-element.87), channel_id=1, source_target_pairs={{0,14},{2,12},{4,10},{6,8},{8,6},{10,4},{12,2},{14,0},{1,15},{3,13... | collective-permute-start | bytes 442376 | tf_op jit(solution)/shard_map/ppermute | solution.py:258
  77.8 0.6 ordered_metric.1.refs_0_.refs_1_
  78.4 2.0 %collective-permute-start.20 = (bf16[3,96,128]{2,1,0:T(8,128)(2,1)S(1)}, bf16[3,96,128]{2,1,0:T(8,128)(2,1)S(1)}, u32[]{:S(2)}, u32[]{:S(2)}) collective-permute-start(bf16[3,96,128]{2,1,0:T(8,128)(2,1)S(1)} %get-tuple-element.84), channel_id=1, source_target_pairs={{0,10},{2,8},{4,14},{6,12},{8,2},{10,0},{12,6},{14,4},{1,11},{3,9}... | collective-permute-start | bytes 221192 | tf_op jit(solution)/shard_map/ppermute | solution.py:258
  80.4 12.7 %collective-permute-done.16.refs_13_ = bf16[6,96,128]{2,1,0:T(8,128)(2,1)S(1)} collective-permute-done((bf16[6,96,128]{2,1,0:T(8,128)(2,1)S(1)}, bf16[6,96,128]{2,1,0:T(8,128)(2,1)S(1)}, u32[]{:S(2)}, u32[]{:S(2)}) %collective-permute-start.16) | collective-permute-done | bytes 147488 | tf_op jit(solution)/shard_map/ppermute | solution.py:258
  93.1 1.8 %group.3.refs_17_ = f32[256,256]{1,0:T(8,128)S(1)} custom-call(bf16[512,512]{1,0:T(8,128)(2,1)S(1)} %ordered_metric.1.refs_0_.refs_1_, bf16[16,32,128]{2,1,0:T(8,128)(2,1)S(1)} %get-tuple-element.53.refs_1_.refs_2_, bf16[16,32,128]{2,1,0:T(8,128)(2,1)S(1)} %collective-permute-done.5._.refs_2_.refs_3_, ...), custom_call_target="tpu_custom_call" | custom-call | flops 1409286144 | bytes 1835008 | tf_op jit(solution)/shard_map/group/pallas_call | solution.py:230
  95.0 4.4 %collective-permute-start.22 = (bf16[3,96,128]{2,1,0:T(8,128)(2,1)S(1)}, bf16[3,96,128]{2,1,0:T(8,128)(2,1)S(1)}, u32[]{:S(2)}, u32[]{:S(2)}) collective-permute-start(bf16[3,96,128]{2,1,0:T(8,128)(2,1)S(1)} %get-tuple-element.88), channel_id=1, source_target_pairs={{0,12},{2,14},{4,8},{6,10},{8,4},{10,6},{12,0},{14,2},{1,13},{3,15... | collective-permute-start | bytes 221192 | tf_op jit(solution)/shard_map/ppermute | solution.py:258
  99.4 1.6 %group.4.refs_18_ = f32[256,256]{1,0:T(8,128)S(1)} custom-call(bf16[512,512]{1,0:T(8,128)(2,1)S(1)} %ordered_metric.1.refs_0_.refs_1_, bf16[16,32,128]{2,1,0:T(8,128)(2,1)S(1)} %get-tuple-element.53.refs_1_.refs_2_, bf16[16,32,128]{2,1,0:T(8,128)(2,1)S(1)} %collective-permute-done.5._.refs_2_.refs_3_, ...), custom_call_target="tpu_custom_call" | custom-call | flops 1207959552 | bytes 1572864 | tf_op jit(solution)/shard_map/group/pallas_call | solution.py:230
  101.0 2.1 %collective-permute-done.20.refs_15_ = bf16[3,96,128]{2,1,0:T(8,128)(2,1)S(1)} collective-permute-done((bf16[3,96,128]{2,1,0:T(8,128)(2,1)S(1)}, bf16[3,96,128]{2,1,0:T(8,128)(2,1)S(1)}, u32[]{:S(2)}, u32[]{:S(2)}) %collective-permute-start.20) | collective-permute-done | bytes 73760 | tf_op jit(solution)/shard_map/ppermute | solution.py:258
  103.1 0.4 collective-permute-done.17.refs_14_
  103.5 1.6 %group.5 = (f32[4,32,128]{2,1,0:T(8,128)S(1)}, f32[4,32,128]{2,1,0:T(8,128)S(1)}, f32[4,32,256]{2,1,0:T(8,128)S(1)}) custom-call(s32[3]{0:T(128)S(1)} %pad_add_fusion.refs_0_, bf16[512,512]{1,0:T(8,128)(2,1)S(1)} %ordered_metric.1.refs_0_.refs_1_, bf16[16,32,128]{2,1,0:T(8,128)(2,1)S(1)} %get-tuple-element.53.refs_1_.refs_2_, ...), custom_call_target="tpu_custom_call" | custom-call | flops 603979776 | bytes 786432 | tf_op jit(solution)/shard_map/group/pallas_call | solution.py:230
  105.1 1.3 %collective-permute-done.27 = f32[4,32,256]{2,1,0:T(8,128)S(1)} collective-permute-done((f32[4,32,256]{2,1,0:T(8,128)S(1)}, f32[4,32,256]{2,1,0:T(8,128)S(1)}, u32[]{:S(2)}, u32[]{:S(2)}) %collective-permute-start.27) | collective-permute-done | bytes 131104 | tf_op jit(solution)/shard_map/ppermute | solution.py:261
  106.5 1.0 collective-permute-start.28
  107.5 3.3 %collective-permute-done.28 = f32[4,32,128]{2,1,0:T(8,128)S(1)} collective-permute-done((f32[4,32,128]{2,1,0:T(8,128)S(1)}, f32[4,32,128]{2,1,0:T(8,128)S(1)}, u32[]{:S(2)}, u32[]{:S(2)}) %collective-permute-start.28) | collective-permute-done | bytes 65568 | tf_op jit(solution)/shard_map/ppermute | solution.py:258
  110.8 2.2 %collective-permute-start.29 = (f32[32,128]{1,0:T(8,128)S(1)}, f32[32,128]{1,0:T(8,128)S(1)}, u32[]{:S(2)}, u32[]{:S(2)}) collective-permute-start(f32[32,128]{1,0:T(8,128)S(1)} %get-tuple-element.99), channel_id=1, source_target_pairs={{0,12},{2,14},{4,8},{6,10},{8,4},{10,6},{12,0},{14,2},{1,13},{3,15... | collective-permute-start | bytes 49160 | tf_op jit(solution)/shard_map/ppermute | solution.py:258
  113.1 1.7 %collective-permute-start.31 = (f32[32,128]{1,0:T(8,128)S(1)}, f32[32,128]{1,0:T(8,128)S(1)}, u32[]{:S(2)}, u32[]{:S(2)}) collective-permute-start(f32[32,128]{1,0:T(8,128)S(1)} %get-tuple-element.100), channel_id=1, source_target_pairs={{0,4},{2,6},{4,0},{6,2},{8,12},{10,14},{12,8},{14,10},{1,5},{3,7},... | collective-permute-start | bytes 49160 | tf_op jit(solution)/shard_map/ppermute | solution.py:258
  114.7 1.4 %collective-permute-start.30 = (f32[32,128]{1,0:T(8,128)S(1)}, f32[32,128]{1,0:T(8,128)S(1)}, u32[]{:S(2)}, u32[]{:S(2)}) collective-permute-start(f32[32,128]{1,0:T(8,128)S(1)} %get-tuple-element.101), channel_id=1, source_target_pairs={{0,8},{2,10},{4,12},{6,14},{8,0},{10,2},{12,4},{14,6},{1,9},{3,11}... | collective-permute-start | bytes 49160 | tf_op jit(solution)/shard_map/ppermute | solution.py:258
  116.1 0.3 collective-permute-done.29
  116.4 0.4 collective-permute-done.31
  116.8 2.6 %collective-permute-done.30 = f32[32,128]{1,0:T(8,128)S(1)} collective-permute-done((f32[32,128]{1,0:T(8,128)S(1)}, f32[32,128]{1,0:T(8,128)S(1)}, u32[]{:S(2)}, u32[]{:S(2)}) %collective-permute-start.30) | collective-permute-done | bytes 16416 | tf_op jit(solution)/shard_map/ppermute | solution.py:258
  119.4 0.6 fusion.4
  (40 shorter events, 0.5 us)
Async XLA Ops:
  0.0 2.9 %copy-start = (bf16[128,512]{1,0:T(8,128)(2,1)S(1)}, bf16[128,512]{1,0:T(8,128)(2,1)}, u32[]{:S(2)}) copy-start(bf16[128,512]{1,0:T(8,128)(2,1)} %param.8) | copy-start | bytes 393220
  0.0 9.5 %copy-start.1 = (bf16[1024,128]{1,0:T(8,128)(2,1)S(1)}, bf16[1024,128]{1,0:T(8,128)(2,1)}, u32[]{:S(2)}) copy-start(bf16[1024,128]{1,0:T(8,128)(2,1)} %own_ref) | copy-start | bytes 786436
  0.0 9.5 %collective-permute-start.4 = (bf16[1024,128]{1,0:T(8,128)(2,1)}, bf16[1024,128]{1,0:T(8,128)(2,1)S(1)}, u32[]{:S(2)}, u32[]{:S(2)}) collective-permute-start(bf16[1024,128]{1,0:T(8,128)(2,1)} %own_ref), channel_id=1, source_target_pairs={{0,2},{2,0},{4,6},{6,4},{8,10},{10,8},{12,14},{14,12},{1,3},{3,1},... | collective-permute-start | bytes 786440 | tf_op jit(solution)/shard_map/ppermute | solution.py:258
  3.0 5.4 %collective-permute-start = (bf16[32,512]{1,0:T(8,128)(2,1)S(1)}, bf16[32,512]{1,0:T(8,128)(2,1)S(1)}, u32[]{:S(2)}, u32[]{:S(2)}) collective-permute-start(bf16[32,512]{1,0:T(8,128)(2,1)S(1)} %constant_dynamic-slice_fusion), channel_id=1, source_target_pairs={{0,8},{2,10},{4,12},{6,14},{8,0},{10,2},{12,4},{14,6},{1,9},{3,11}... | collective-permute-start | bytes 98312 | tf_op jit(solution)/shard_map/ppermute | solution.py:258
  8.3 69.4 %copy-start.2 = (s32[4]{0:T(128)S(1)}, s32[4]{0:T(128)}, u32[]{:S(2)}) copy-start(s32[4]{0:T(128)} %param.9) | copy-start | bytes 52
  10.7 8.6 %collective-permute-start.8 = (bf16[16,32,128]{2,1,0:T(8,128)(2,1)S(1)}, bf16[16,32,128]{2,1,0:T(8,128)(2,1)S(1)}, u32[]{:S(2)}, u32[]{:S(2)}) collective-permute-start(bf16[16,32,128]{2,1,0:T(8,128)(2,1)S(1)} %get-tuple-element.61), channel_id=1, source_target_pairs={{0,8},{2,10},{4,12},{6,14},{8,0},{10,2},{12,4},{14,6},{1,9},{3,11}... | collective-permute-start | bytes 393224 | tf_op jit(solution)/shard_map/ppermute | solution.py:258
  13.6 11.2 %collective-permute-start.5 = (bf16[16,32,128]{2,1,0:T(8,128)(2,1)S(1)}, bf16[16,32,128]{2,1,0:T(8,128)(2,1)S(1)}, u32[]{:S(2)}, u32[]{:S(2)}) collective-permute-start(bf16[16,32,128]{2,1,0:T(8,128)(2,1)S(1)} %get-tuple-element.54), channel_id=1, source_target_pairs={{0,2},{2,0},{4,6},{6,4},{8,10},{10,8},{12,14},{14,12},{1,3},{3,1},... | collective-permute-start | bytes 393224 | tf_op jit(solution)/shard_map/ppermute | solution.py:258
  15.1 17.7 %collective-permute-start.7 = (bf16[16,32,128]{2,1,0:T(8,128)(2,1)S(1)}, bf16[16,32,128]{2,1,0:T(8,128)(2,1)S(1)}, u32[]{:S(2)}, u32[]{:S(2)}) collective-permute-start(bf16[16,32,128]{2,1,0:T(8,128)(2,1)S(1)} %get-tuple-element.60), channel_id=1, source_target_pairs={{0,6},{2,4},{4,2},{6,0},{8,14},{10,12},{12,10},{14,8},{1,7},{3,5},... | collective-permute-start | bytes 393224 | tf_op jit(solution)/shard_map/ppermute | solution.py:258
  16.7 16.1 %collective-permute-start.9 = (bf16[16,32,128]{2,1,0:T(8,128)(2,1)S(1)}, bf16[16,32,128]{2,1,0:T(8,128)(2,1)S(1)}, u32[]{:S(2)}, u32[]{:S(2)}) collective-permute-start(bf16[16,32,128]{2,1,0:T(8,128)(2,1)S(1)} %get-tuple-element.62), channel_id=1, source_target_pairs={{0,10},{2,8},{4,14},{6,12},{8,2},{10,0},{12,6},{14,4},{1,11},{3,9}... | collective-permute-start | bytes 393224 | tf_op jit(solution)/shard_map/ppermute | solution.py:258
  17.9 19.3 %collective-permute-start.1 = (bf16[64,512]{1,0:T(8,128)(2,1)S(1)}, bf16[64,512]{1,0:T(8,128)(2,1)S(1)}, u32[]{:S(2)}, u32[]{:S(2)}) collective-permute-start(bf16[64,512]{1,0:T(8,128)(2,1)S(1)} %pad_maximum_fusion.2), channel_id=1, source_target_pairs={{0,4},{2,6},{4,0},{6,2},{8,12},{10,14},{12,8},{14,10},{1,5},{3,7},... | collective-permute-start | bytes 196616 | tf_op jit(solution)/shard_map/ppermute | solution.py:258
  19.3 18.0 %collective-permute-start.10 = (bf16[16,32,128]{2,1,0:T(8,128)(2,1)S(1)}, bf16[16,32,128]{2,1,0:T(8,128)(2,1)S(1)}, u32[]{:S(2)}, u32[]{:S(2)}) collective-permute-start(bf16[16,32,128]{2,1,0:T(8,128)(2,1)S(1)} %get-tuple-element.63), channel_id=1, source_target_pairs={{0,12},{2,14},{4,8},{6,10},{8,4},{10,6},{12,0},{14,2},{1,13},{3,15... | collective-permute-start | bytes 393224 | tf_op jit(solution)/shard_map/ppermute | solution.py:258
  24.8 14.0 %collective-permute-start.11 = (bf16[16,32,128]{2,1,0:T(8,128)(2,1)S(1)}, bf16[16,32,128]{2,1,0:T(8,128)(2,1)S(1)}, u32[]{:S(2)}, u32[]{:S(2)}) collective-permute-start(bf16[16,32,128]{2,1,0:T(8,128)(2,1)S(1)} %get-tuple-element.65), channel_id=1, source_target_pairs={{0,14},{2,12},{4,10},{6,8},{8,6},{10,4},{12,2},{14,0},{1,15},{3,13... | collective-permute-start | bytes 393224 | tf_op jit(solution)/shard_map/ppermute | solution.py:258
  32.8 6.6 %collective-permute-start.6 = (bf16[16,32,128]{2,1,0:T(8,128)(2,1)S(1)}, bf16[16,32,128]{2,1,0:T(8,128)(2,1)S(1)}, u32[]{:S(2)}, u32[]{:S(2)}) collective-permute-start(bf16[16,32,128]{2,1,0:T(8,128)(2,1)S(1)} %get-tuple-element.59), channel_id=1, source_target_pairs={{0,4},{2,6},{4,0},{6,2},{8,12},{10,14},{12,8},{14,10},{1,5},{3,7},... | collective-permute-start | bytes 393224 | tf_op jit(solution)/shard_map/ppermute | solution.py:258
  32.9 19.2 %collective-permute-start.24 = (bf16[7,96,128]{2,1,0:T(8,128)(2,1)S(1)}, bf16[7,96,128]{2,1,0:T(8,128)(2,1)S(1)}, u32[]{:S(2)}, u32[]{:S(2)}) collective-permute-start(bf16[7,96,128]{2,1,0:T(8,128)(2,1)S(1)} %get-tuple-element.93), channel_id=1, source_target_pairs={{0,8},{2,10},{4,12},{6,14},{8,0},{10,2},{12,4},{14,6},{1,9},{3,11}... | collective-permute-start | bytes 516104 | tf_op jit(solution)/shard_map/ppermute | solution.py:258
  37.3 18.8 %collective-permute-start.14 = (bf16[7,96,128]{2,1,0:T(8,128)(2,1)S(1)}, bf16[7,96,128]{2,1,0:T(8,128)(2,1)S(1)}, u32[]{:S(2)}, u32[]{:S(2)}) collective-permute-start(bf16[7,96,128]{2,1,0:T(8,128)(2,1)S(1)} %get-tuple-element.73), channel_id=1, source_target_pairs={{0,10},{2,8},{4,14},{6,12},{8,2},{10,0},{12,6},{14,4},{1,11},{3,9}... | collective-permute-start | bytes 516104 | tf_op jit(solution)/shard_map/ppermute | solution.py:258
  37.3 22.3 %collective-permute-start.2 = (bf16[128,512]{1,0:T(8,128)(2,1)S(1)}, bf16[128,512]{1,0:T(8,128)(2,1)S(1)}, u32[]{:S(2)}, u32[]{:S(2)}) collective-permute-start(bf16[128,512]{1,0:T(8,128)(2,1)S(1)} %pad_maximum_fusion.1), channel_id=1, source_target_pairs={{0,2},{2,0},{4,6},{6,4},{8,10},{10,8},{12,14},{14,12},{1,3},{3,1},... | collective-permute-start | bytes 393224 | tf_op jit(solution)/shard_map/ppermute | solution.py:258
  38.8 20.9 %collective-permute-start.12 = (bf16[16,96,128]{2,1,0:T(8,128)(2,1)S(1)}, bf16[16,96,128]{2,1,0:T(8,128)(2,1)S(1)}, u32[]{:S(2)}, u32[]{:S(2)}) collective-permute-start(bf16[16,96,128]{2,1,0:T(8,128)(2,1)S(1)} %get-tuple-element.68), channel_id=1, source_target_pairs={{0,2},{2,0},{4,6},{6,4},{8,10},{10,8},{12,14},{14,12},{1,3},{3,1},... | collective-permute-start | bytes 1179656 | tf_op jit(solution)/shard_map/ppermute | solution.py:258
  39.4 20.2 %collective-permute-start.18 = (bf16[7,96,128]{2,1,0:T(8,128)(2,1)S(1)}, bf16[7,96,128]{2,1,0:T(8,128)(2,1)S(1)}, u32[]{:S(2)}, u32[]{:S(2)}) collective-permute-start(bf16[7,96,128]{2,1,0:T(8,128)(2,1)S(1)} %get-tuple-element.82), channel_id=1, source_target_pairs={{0,12},{2,14},{4,8},{6,10},{8,4},{10,6},{12,0},{14,2},{1,13},{3,15... | collective-permute-start | bytes 516104 | tf_op jit(solution)/shard_map/ppermute | solution.py:258
  52.1 20.5 %collective-permute-start.13 = (bf16[16,96,128]{2,1,0:T(8,128)(2,1)S(1)}, bf16[16,96,128]{2,1,0:T(8,128)(2,1)S(1)}, u32[]{:S(2)}, u32[]{:S(2)}) collective-permute-start(bf16[16,96,128]{2,1,0:T(8,128)(2,1)S(1)} %get-tuple-element.70), channel_id=1, source_target_pairs={{0,4},{2,6},{4,0},{6,2},{8,12},{10,14},{12,8},{14,10},{1,5},{3,7},... | collective-permute-start | bytes 1179656 | tf_op jit(solution)/shard_map/ppermute | solution.py:258
  56.0 13.7 %collective-permute-start.25 = (bf16[7,96,128]{2,1,0:T(8,128)(2,1)S(1)}, bf16[7,96,128]{2,1,0:T(8,128)(2,1)S(1)}, u32[]{:S(2)}, u32[]{:S(2)}) collective-permute-start(bf16[7,96,128]{2,1,0:T(8,128)(2,1)S(1)} %get-tuple-element.94), channel_id=1, source_target_pairs={{0,14},{2,12},{4,10},{6,8},{8,6},{10,4},{12,2},{14,0},{1,15},{3,13... | collective-permute-start | bytes 516104 | tf_op jit(solution)/shard_map/ppermute | solution.py:258
  59.6 33.5 %collective-permute-start.15 = (bf16[16,96,128]{2,1,0:T(8,128)(2,1)S(1)}, bf16[16,96,128]{2,1,0:T(8,128)(2,1)S(1)}, u32[]{:S(2)}, u32[]{:S(2)}) collective-permute-start(bf16[16,96,128]{2,1,0:T(8,128)(2,1)S(1)} %get-tuple-element.74), channel_id=1, source_target_pairs={{0,6},{2,4},{4,2},{6,0},{8,14},{10,12},{12,10},{14,8},{1,7},{3,5},... | collective-permute-start | bytes 1179656 | tf_op jit(solution)/shard_map/ppermute | solution.py:258
  59.6 16.4 %collective-permute-start.3 = (bf16[256,512]{1,0:T(8,128)(2,1)S(1)}, bf16[256,512]{1,0:T(8,128)(2,1)S(1)}, u32[]{:S(2)}, u32[]{:S(2)}) collective-permute-start(bf16[256,512]{1,0:T(8,128)(2,1)S(1)} %pad_maximum_fusion.refs_0_), channel_id=1, source_target_pairs={{0,1},{1,0},{2,3},{3,2},{4,5},{5,4},{6,7},{7,6},{8,9},{9,8},{10,11... | collective-permute-start | bytes 786440 | tf_op jit(solution)/shard_map/ppermute | solution.py:261
  59.7 18.7 %collective-permute-start.19 = (bf16[6,96,128]{2,1,0:T(8,128)(2,1)S(1)}, bf16[6,96,128]{2,1,0:T(8,128)(2,1)S(1)}, u32[]{:S(2)}, u32[]{:S(2)}) collective-permute-start(bf16[6,96,128]{2,1,0:T(8,128)(2,1)S(1)} %get-tuple-element.83), channel_id=1, source_target_pairs={{0,10},{2,8},{4,14},{6,12},{8,2},{10,0},{12,6},{14,4},{1,11},{3,9}... | collective-permute-start | bytes 442376 | tf_op jit(solution)/shard_map/ppermute | solution.py:258
  69.7 23.4 %collective-permute-start.16 = (bf16[6,96,128]{2,1,0:T(8,128)(2,1)S(1)}, bf16[6,96,128]{2,1,0:T(8,128)(2,1)S(1)}, u32[]{:S(2)}, u32[]{:S(2)}) collective-permute-start(bf16[6,96,128]{2,1,0:T(8,128)(2,1)S(1)} %get-tuple-element.77), channel_id=1, source_target_pairs={{0,8},{2,10},{4,12},{6,14},{8,0},{10,2},{12,4},{14,6},{1,9},{3,11}... | collective-permute-start | bytes 442376 | tf_op jit(solution)/shard_map/ppermute | solution.py:258
  72.7 26.7 %collective-permute-start.26 = (bf16[6,96,128]{2,1,0:T(8,128)(2,1)S(1)}, bf16[6,96,128]{2,1,0:T(8,128)(2,1)S(1)}, u32[]{:S(2)}, u32[]{:S(2)}) collective-permute-start(bf16[6,96,128]{2,1,0:T(8,128)(2,1)S(1)} %get-tuple-element.95), channel_id=1, source_target_pairs={{0,12},{2,14},{4,8},{6,10},{8,4},{10,6},{12,0},{14,2},{1,13},{3,15... | collective-permute-start | bytes 442376 | tf_op jit(solution)/shard_map/ppermute | solution.py:258
  76.0 19.0 %collective-permute-start.21 = (bf16[6,96,128]{2,1,0:T(8,128)(2,1)S(1)}, bf16[6,96,128]{2,1,0:T(8,128)(2,1)S(1)}, u32[]{:S(2)}, u32[]{:S(2)}) collective-permute-start(bf16[6,96,128]{2,1,0:T(8,128)(2,1)S(1)} %get-tuple-element.87), channel_id=1, source_target_pairs={{0,14},{2,12},{4,10},{6,8},{8,6},{10,4},{12,2},{14,0},{1,15},{3,13... | collective-permute-start | bytes 442376 | tf_op jit(solution)/shard_map/ppermute | solution.py:258
  78.4 24.7 %collective-permute-start.20 = (bf16[3,96,128]{2,1,0:T(8,128)(2,1)S(1)}, bf16[3,96,128]{2,1,0:T(8,128)(2,1)S(1)}, u32[]{:S(2)}, u32[]{:S(2)}) collective-permute-start(bf16[3,96,128]{2,1,0:T(8,128)(2,1)S(1)} %get-tuple-element.84), channel_id=1, source_target_pairs={{0,10},{2,8},{4,14},{6,12},{8,2},{10,0},{12,6},{14,4},{1,11},{3,9}... | collective-permute-start | bytes 221192 | tf_op jit(solution)/shard_map/ppermute | solution.py:258
  93.1 10.4 %collective-permute-start.17 = (bf16[3,96,128]{2,1,0:T(8,128)(2,1)S(1)}, bf16[3,96,128]{2,1,0:T(8,128)(2,1)S(1)}, u32[]{:S(2)}, u32[]{:S(2)}) collective-permute-start(bf16[3,96,128]{2,1,0:T(8,128)(2,1)S(1)} %get-tuple-element.78), channel_id=1, source_target_pairs={{0,8},{2,10},{4,12},{6,14},{8,0},{10,2},{12,4},{14,6},{1,9},{3,11}... | collective-permute-start | bytes 221192 | tf_op jit(solution)/shard_map/ppermute | solution.py:258
  93.1 10.4 %collective-permute-start.23 = (bf16[3,96,128]{2,1,0:T(8,128)(2,1)S(1)}, bf16[3,96,128]{2,1,0:T(8,128)(2,1)S(1)}, u32[]{:S(2)}, u32[]{:S(2)}) collective-permute-start(bf16[3,96,128]{2,1,0:T(8,128)(2,1)S(1)} %get-tuple-element.90), channel_id=1, source_target_pairs={{0,14},{2,12},{4,10},{6,8},{8,6},{10,4},{12,2},{14,0},{1,15},{3,13... | collective-permute-start | bytes 221192 | tf_op jit(solution)/shard_map/ppermute | solution.py:258
  95.0 8.5 %collective-permute-start.22 = (bf16[3,96,128]{2,1,0:T(8,128)(2,1)S(1)}, bf16[3,96,128]{2,1,0:T(8,128)(2,1)S(1)}, u32[]{:S(2)}, u32[]{:S(2)}) collective-permute-start(bf16[3,96,128]{2,1,0:T(8,128)(2,1)S(1)} %get-tuple-element.88), channel_id=1, source_target_pairs={{0,12},{2,14},{4,8},{6,10},{8,4},{10,6},{12,0},{14,2},{1,13},{3,15... | collective-permute-start | bytes 221192 | tf_op jit(solution)/shard_map/ppermute | solution.py:258
  105.0 1.4 %collective-permute-start.27 = (f32[4,32,256]{2,1,0:T(8,128)S(1)}, f32[4,32,256]{2,1,0:T(8,128)S(1)}, u32[]{:S(2)}, u32[]{:S(2)}) collective-permute-start(f32[4,32,256]{2,1,0:T(8,128)S(1)} %get-tuple-element.97), channel_id=1, source_target_pairs={{0,1},{1,0},{2,3},{3,2},{4,5},{5,4},{6,7},{7,6},{8,9},{9,8},{10,11... | collective-permute-start | bytes 393224 | tf_op jit(solution)/shard_map/ppermute | solution.py:261
  106.5 4.3 %collective-permute-start.28 = (f32[4,32,128]{2,1,0:T(8,128)S(1)}, f32[4,32,128]{2,1,0:T(8,128)S(1)}, u32[]{:S(2)}, u32[]{:S(2)}) collective-permute-start(f32[4,32,128]{2,1,0:T(8,128)S(1)} %slice_add_fusion), channel_id=1, source_target_pairs={{0,2},{2,0},{4,6},{6,4},{8,10},{10,8},{12,14},{14,12},{1,3},{3,1},... | collective-permute-start | bytes 196616 | tf_op jit(solution)/shard_map/ppermute | solution.py:258
  110.8 5.6 %collective-permute-start.29 = (f32[32,128]{1,0:T(8,128)S(1)}, f32[32,128]{1,0:T(8,128)S(1)}, u32[]{:S(2)}, u32[]{:S(2)}) collective-permute-start(f32[32,128]{1,0:T(8,128)S(1)} %get-tuple-element.99), channel_id=1, source_target_pairs={{0,12},{2,14},{4,8},{6,10},{8,4},{10,6},{12,0},{14,2},{1,13},{3,15... | collective-permute-start | bytes 49160 | tf_op jit(solution)/shard_map/ppermute | solution.py:258
  113.1 3.7 %collective-permute-start.31 = (f32[32,128]{1,0:T(8,128)S(1)}, f32[32,128]{1,0:T(8,128)S(1)}, u32[]{:S(2)}, u32[]{:S(2)}) collective-permute-start(f32[32,128]{1,0:T(8,128)S(1)} %get-tuple-element.100), channel_id=1, source_target_pairs={{0,4},{2,6},{4,0},{6,2},{8,12},{10,14},{12,8},{14,10},{1,5},{3,7},... | collective-permute-start | bytes 49160 | tf_op jit(solution)/shard_map/ppermute | solution.py:258
  114.7 4.6 %collective-permute-start.30 = (f32[32,128]{1,0:T(8,128)S(1)}, f32[32,128]{1,0:T(8,128)S(1)}, u32[]{:S(2)}, u32[]{:S(2)}) collective-permute-start(f32[32,128]{1,0:T(8,128)S(1)} %get-tuple-element.101), channel_id=1, source_target_pairs={{0,8},{2,10},{4,12},{6,14},{8,0},{10,2},{12,4},{14,6},{1,9},{3,11}... | collective-permute-start | bytes 49160 | tf_op jit(solution)/shard_map/ppermute | solution.py:258

commit v5 on v4

--- a/solution.py
+++ b/solution.py
@@ -67,15 +67,16 @@
     block = plain.shape[0]
     held = own_ref.shape[0] // block
     for s in range(plain.shape[1] // block):
-        name = where[2 + s]
-        away = lax.div(name, held) != where[1]
+        name = where[0, 2 + s]
+        away = lax.div(name, held) != where[0, 1]
         start = pl.multiple_of(lax.rem(name, held) * block, block)
         mine = own_ref[pl.ds(start, block), :].astype(F32)
         theirs = other_ref[pl.ds(start, block), :].astype(F32)
         picked = jnp.where(away, theirs, mine)
         plain[:, s * block : (s + 1) * block] = picked.T.astype(BF16)
+    me = where[0, 0]
     for k in range(chips):
-        start = pl.multiple_of((where[0] ^ k) * share, share)
+        start = pl.multiple_of((me ^ k) * share, share)
         table_ref[k * share : (k + 1) * share, :] = plain[pl.ds(start, share), :]
     for at in range(0, x_ref.shape[0], ROWS):
         value = products(table_ref[...], x_ref[at : at + ROWS])
@@ -89,7 +90,7 @@
     share = orbitals // chips
     return pl.pallas_call(
         functools.partial(first_kernel, chips),
-        in_specs=[pl.BlockSpec(memory_space=pltpu.SMEM)] + [WHOLE] * 3,
+        in_specs=[WHOLE] * 4,
         out_specs=[WHOLE] * (chips + 1),
         out_shape=[jax.ShapeDtypeStruct((share, first, width), BF16)] * chips
         + [jax.ShapeDtypeStruct((orbitals, depth), BF16)],
@@ -97,7 +98,7 @@
         compiler_params=params(),
         cost_estimate=cost(orbitals * depth * first * width, moved.size * 2),
         name="first_products",
-    )(where, own, other, moved)
+    )(where[None], own, other, moved)
 
 
 def rest_kernel(chips, spans, x_ref, table_ref, _, *outs):
@@ -193,11 +194,12 @@
     scratch[...] = total
     width = side // bas
     piece = kept.shape[1]
+    a_here, b_here, o_here = (where[0, n] for n in range(3))
     for ka in range(aux):
-        a = where[0] ^ ka
+        a = a_here ^ ka
         for who in range(2):
-            row = (a * 2 + (where[2] ^ who)) * piece
-            block = lax.div(row, width) ^ where[1]
+            row = (a * 2 + (o_here ^ who)) * piece
+            block = lax.div(row, width) ^ b_here
             start = pl.multiple_of(block * width + lax.rem(row, width), piece)
             value = scratch[pl.ds(start, piece), :]
             if who:
@@ -213,10 +215,9 @@
     last, started = where is not None, total is not None
     width = late[0].shape[2]
     side = bas * width
-    args = ([where] if last else []) + [metric, *early, *late] + ([total] if started else [])
+    args = ([where[None]] if last else []) + [metric, *early, *late] + ([total] if started else [])
     specs = [WHOLE] * len(args)
     if last:
-        specs[0] = pl.BlockSpec(memory_space=pltpu.SMEM)
         piece = side // (aux * 2)
         out = [
             jax.ShapeDtypeStruct((aux, piece, width), F32),

time: 120 us -> 119 us (level)
  no operation moved by 1% of the time
where the time goes in v5:
time: 119 us
  starting transfers between devices  53.3 us (45%)
  waiting for transfers between devices  49 us (41%)
  Pallas kernels  15 us (13%)
  other arithmetic  1.55 us (1%)
    ppermute x30, starting transfers between devices, swap(): return lax.ppermute(value, ('aux', 'bas'), pairs)  53.2 us
    ppermute x30, waiting for transfers between devices, swap(): return lax.ppermute(value, ('aux', 'bas'), pairs)  47.6 us
    pallas_call x1, Pallas kernels, rest_products(): pl.pallas_call(functools.partial(rest_kernel, chips, spans), grid=(rest /...  7.03 us
    pallas_call x3, Pallas kernels, group(): pl.pallas_call(functools.partial(group_kernel, aux, bas, lo, hi, starts,...  4.48 us
  transfers between devices with their start and end apart: 32, of which 14 were waited for; matrix products, arithmetic and copies ran while one was open for 1% of the time, Pallas kernels for 11%

profile of v5, /device:TPU:0, one launch (start us, length us, event | category | flops | bytes accessed | tf_op | source)
XLA Modules:
  0.0 119.0 jit_solution(8067434340582370702)
XLA Ops:
  0.0 2.9 %collective-permute-start.4 = (bf16[1024,128]{1,0:T(8,128)(2,1)}, bf16[1024,128]{1,0:T(8,128)(2,1)S(1)}, u32[]{:S(2)}, u32[]{:S(2)}) collective-permute-start(bf16[1024,128]{1,0:T(8,128)(2,1)} %own_ref), channel_id=1, source_target_pairs={{0,2},{2,0},{4,6},{6,4},{8,10},{10,8},{12,14},{14,12},{1,3},{3,1},... | collective-permute-start | bytes 786440 | tf_op jit(solution)/shard_map/ppermute | solution.py:259
  3.0 2.6 %collective-permute-start = (bf16[32,512]{1,0:T(8,128)(2,1)S(1)}, bf16[32,512]{1,0:T(8,128)(2,1)S(1)}, u32[]{:S(2)}, u32[]{:S(2)}) collective-permute-start(bf16[32,512]{1,0:T(8,128)(2,1)S(1)} %constant_dynamic-slice_fusion), channel_id=1, source_target_pairs={{0,8},{2,10},{4,12},{6,14},{8,0},{10,2},{12,4},{14,6},{1,9},{3,11}... | collective-permute-start | bytes 98312 | tf_op jit(solution)/shard_map/ppermute | solution.py:259
  5.5 0.7 add_bitcast_fusion.1.where
  6.3 2.0 %relayout.1.x_ref = bf16[32,256,128]{2,1,0:T(8,128)(2,1)S(1)} custom-call(bf16[2,128,128,128]{3,2,1,0:T(8,128)(2,1)} %bitcast.28), custom_call_target="tpu_custom_call" | custom-call | bytes 4194304 | tf_op jit(solution)/shard_map/relayout/pallas_call | solution.py:42
  8.3 1.2 collective-permute-done.4.other_ref
  9.5 0.8 first_products.1
  10.3 2.9 %collective-permute-start.8 = (bf16[16,32,128]{2,1,0:T(8,128)(2,1)S(1)}, bf16[16,32,128]{2,1,0:T(8,128)(2,1)S(1)}, u32[]{:S(2)}, u32[]{:S(2)}) collective-permute-start(bf16[16,32,128]{2,1,0:T(8,128)(2,1)S(1)} %get-tuple-element.61), channel_id=1, source_target_pairs={{0,8},{2,10},{4,12},{6,14},{8,0},{10,2},{12,4},{14,6},{1,9},{3,11}... | collective-permute-start | bytes 393224 | tf_op jit(solution)/shard_map/ppermute | solution.py:259
  13.2 1.5 %collective-permute-start.5 = (bf16[16,32,128]{2,1,0:T(8,128)(2,1)S(1)}, bf16[16,32,128]{2,1,0:T(8,128)(2,1)S(1)}, u32[]{:S(2)}, u32[]{:S(2)}) collective-permute-start(bf16[16,32,128]{2,1,0:T(8,128)(2,1)S(1)} %get-tuple-element.54), channel_id=1, source_target_pairs={{0,2},{2,0},{4,6},{6,4},{8,10},{10,8},{12,14},{14,12},{1,3},{3,1},... | collective-permute-start | bytes 393224 | tf_op jit(solution)/shard_map/ppermute | solution.py:259
  14.7 1.5 %collective-permute-start.7 = (bf16[16,32,128]{2,1,0:T(8,128)(2,1)S(1)}, bf16[16,32,128]{2,1,0:T(8,128)(2,1)S(1)}, u32[]{:S(2)}, u32[]{:S(2)}) collective-permute-start(bf16[16,32,128]{2,1,0:T(8,128)(2,1)S(1)} %get-tuple-element.60), channel_id=1, source_target_pairs={{0,6},{2,4},{4,2},{6,0},{8,14},{10,12},{12,10},{14,8},{1,7},{3,5},... | collective-permute-start | bytes 393224 | tf_op jit(solution)/shard_map/ppermute | solution.py:259
  16.2 1.3 %collective-permute-start.9 = (bf16[16,32,128]{2,1,0:T(8,128)(2,1)S(1)}, bf16[16,32,128]{2,1,0:T(8,128)(2,1)S(1)}, u32[]{:S(2)}, u32[]{:S(2)}) collective-permute-start(bf16[16,32,128]{2,1,0:T(8,128)(2,1)S(1)} %get-tuple-element.62), channel_id=1, source_target_pairs={{0,10},{2,8},{4,14},{6,12},{8,2},{10,0},{12,6},{14,4},{1,11},{3,9}... | collective-permute-start | bytes 393224 | tf_op jit(solution)/shard_map/ppermute | solution.py:259
  17.5 0.4 collective-permute-start.1
  17.9 0.9 collective-permute-done.8.refs_5_.refs_6_
  18.9 5.5 %collective-permute-start.10 = (bf16[16,32,128]{2,1,0:T(8,128)(2,1)S(1)}, bf16[16,32,128]{2,1,0:T(8,128)(2,1)S(1)}, u32[]{:S(2)}, u32[]{:S(2)}) collective-permute-start(bf16[16,32,128]{2,1,0:T(8,128)(2,1)S(1)} %get-tuple-element.63), channel_id=1, source_target_pairs={{0,12},{2,14},{4,8},{6,10},{8,4},{10,6},{12,0},{14,2},{1,13},{3,15... | collective-permute-start | bytes 393224 | tf_op jit(solution)/shard_map/ppermute | solution.py:259
  24.4 0.9 collective-permute-start.11
  25.3 7.0 %rest_products.1 = (bf16[7,96,128]{2,1,0:T(8,128)(2,1)S(1)}, bf16[7,96,128]{2,1,0:T(8,128)(2,1)S(1)}, bf16[7,96,128]{2,1,0:T(8,128)(2,1)S(1)}, bf16[7,96,128]{2,...) custom-call(bf16[2,128,128,128]{3,2,1,0:T(8,128)(2,1)} %bitcast.29, ...), custom_call_target="tpu_custom_call" | custom-call | flops 805306368 | bytes 8388608 | tf_op jit(solution)/shard_map/rest_products/pallas_call | solution.py:119
  32.5 4.4 %collective-permute-start.24 = (bf16[7,96,128]{2,1,0:T(8,128)(2,1)S(1)}, bf16[7,96,128]{2,1,0:T(8,128)(2,1)S(1)}, u32[]{:S(2)}, u32[]{:S(2)}) collective-permute-start(bf16[7,96,128]{2,1,0:T(8,128)(2,1)S(1)} %get-tuple-element.93), channel_id=1, source_target_pairs={{0,8},{2,10},{4,12},{6,14},{8,0},{10,2},{12,4},{14,6},{1,9},{3,11}... | collective-permute-start | bytes 516104 | tf_op jit(solution)/shard_map/ppermute | solution.py:259
  36.9 1.5 %collective-permute-start.2 = (bf16[128,512]{1,0:T(8,128)(2,1)S(1)}, bf16[128,512]{1,0:T(8,128)(2,1)S(1)}, u32[]{:S(2)}, u32[]{:S(2)}) collective-permute-start(bf16[128,512]{1,0:T(8,128)(2,1)S(1)} %pad_maximum_fusion.1), channel_id=1, source_target_pairs={{0,2},{2,0},{4,6},{6,4},{8,10},{10,8},{12,14},{14,12},{1,3},{3,1},... | collective-permute-start | bytes 393224 | tf_op jit(solution)/shard_map/ppermute | solution.py:259
  38.4 0.6 collective-permute-start.12
  38.9 2.5 %collective-permute-start.18 = (bf16[7,96,128]{2,1,0:T(8,128)(2,1)S(1)}, bf16[7,96,128]{2,1,0:T(8,128)(2,1)S(1)}, u32[]{:S(2)}, u32[]{:S(2)}) collective-permute-start(bf16[7,96,128]{2,1,0:T(8,128)(2,1)S(1)} %get-tuple-element.82), channel_id=1, source_target_pairs={{0,12},{2,14},{4,8},{6,10},{8,4},{10,6},{12,0},{14,2},{1,13},{3,15... | collective-permute-start | bytes 516104 | tf_op jit(solution)/shard_map/ppermute | solution.py:259
  41.5 10.2 %collective-permute-done.24.refs_13_ = bf16[7,96,128]{2,1,0:T(8,128)(2,1)S(1)} collective-permute-done((bf16[7,96,128]{2,1,0:T(8,128)(2,1)S(1)}, bf16[7,96,128]{2,1,0:T(8,128)(2,1)S(1)}, u32[]{:S(2)}, u32[]{:S(2)}) %collective-permute-start.24) | collective-permute-done | bytes 172064 | tf_op jit(solution)/shard_map/ppermute | solution.py:259
  51.7 0.3 collective-permute-start.13
  52.0 3.6 %collective-permute-done.14.refs_14_ = bf16[7,96,128]{2,1,0:T(8,128)(2,1)S(1)} collective-permute-done((bf16[7,96,128]{2,1,0:T(8,128)(2,1)S(1)}, bf16[7,96,128]{2,1,0:T(8,128)(2,1)S(1)}, u32[]{:S(2)}, u32[]{:S(2)}) %collective-permute-start.14) | collective-permute-done | bytes 172064 | tf_op jit(solution)/shard_map/ppermute | solution.py:259
  55.6 3.5 %collective-permute-start.25 = (bf16[7,96,128]{2,1,0:T(8,128)(2,1)S(1)}, bf16[7,96,128]{2,1,0:T(8,128)(2,1)S(1)}, u32[]{:S(2)}, u32[]{:S(2)}) collective-permute-start(bf16[7,96,128]{2,1,0:T(8,128)(2,1)S(1)} %get-tuple-element.94), channel_id=1, source_target_pairs={{0,14},{2,12},{4,10},{6,8},{8,6},{10,4},{12,2},{14,0},{1,15},{3,13... | collective-permute-start | bytes 516104 | tf_op jit(solution)/shard_map/ppermute | solution.py:259
  59.3 2.7 %collective-permute-start.19 = (bf16[6,96,128]{2,1,0:T(8,128)(2,1)S(1)}, bf16[6,96,128]{2,1,0:T(8,128)(2,1)S(1)}, u32[]{:S(2)}, u32[]{:S(2)}) collective-permute-start(bf16[6,96,128]{2,1,0:T(8,128)(2,1)S(1)} %get-tuple-element.83), channel_id=1, source_target_pairs={{0,10},{2,8},{4,14},{6,12},{8,2},{10,0},{12,6},{14,4},{1,11},{3,9}... | collective-permute-start | bytes 442376 | tf_op jit(solution)/shard_map/ppermute | solution.py:259
  62.0 7.3 %collective-permute-done.25.refs_16_ = bf16[7,96,128]{2,1,0:T(8,128)(2,1)S(1)} collective-permute-done((bf16[7,96,128]{2,1,0:T(8,128)(2,1)S(1)}, bf16[7,96,128]{2,1,0:T(8,128)(2,1)S(1)}, u32[]{:S(2)}, u32[]{:S(2)}) %collective-permute-start.25) | collective-permute-done | bytes 172064 | tf_op jit(solution)/shard_map/ppermute | solution.py:259
  69.4 0.1 add_bitcast_fusion.refs_0_
  69.5 2.7 %collective-permute-done.13.refs_11_.refs_12_ = bf16[16,96,128]{2,1,0:T(8,128)(2,1)S(1)} collective-permute-done((bf16[16,96,128]{2,1,0:T(8,128)(2,1)S(1)}, bf16[16,96,128]{2,1,0:T(8,128)(2,1)S(1)}, u32[]{:S(2)}, u32[]{:S(2)}) %collective-permute-start.13) | collective-permute-done | bytes 393248 | tf_op jit(solution)/shard_map/ppermute | solution.py:259
  72.2 3.4 %collective-permute-start.26 = (bf16[6,96,128]{2,1,0:T(8,128)(2,1)S(1)}, bf16[6,96,128]{2,1,0:T(8,128)(2,1)S(1)}, u32[]{:S(2)}, u32[]{:S(2)}) collective-permute-start(bf16[6,96,128]{2,1,0:T(8,128)(2,1)S(1)} %get-tuple-element.95), channel_id=1, source_target_pairs={{0,12},{2,14},{4,8},{6,10},{8,4},{10,6},{12,0},{14,2},{1,13},{3,15... | collective-permute-start | bytes 442376 | tf_op jit(solution)/shard_map/ppermute | solution.py:259
  75.6 1.7 %collective-permute-start.21 = (bf16[6,96,128]{2,1,0:T(8,128)(2,1)S(1)}, bf16[6,96,128]{2,1,0:T(8,128)(2,1)S(1)}, u32[]{:S(2)}, u32[]{:S(2)}) collective-permute-start(bf16[6,96,128]{2,1,0:T(8,128)(2,1)S(1)} %get-tuple-element.87), channel_id=1, source_target_pairs={{0,14},{2,12},{4,10},{6,8},{8,6},{10,4},{12,2},{14,0},{1,15},{3,13... | collective-permute-start | bytes 442376 | tf_op jit(solution)/shard_map/ppermute | solution.py:259
  77.3 0.6 ordered_metric.1.refs_0_.refs_1_
  78.0 2.0 %collective-permute-start.20 = (bf16[3,96,128]{2,1,0:T(8,128)(2,1)S(1)}, bf16[3,96,128]{2,1,0:T(8,128)(2,1)S(1)}, u32[]{:S(2)}, u32[]{:S(2)}) collective-permute-start(bf16[3,96,128]{2,1,0:T(8,128)(2,1)S(1)} %get-tuple-element.84), channel_id=1, source_target_pairs={{0,10},{2,8},{4,14},{6,12},{8,2},{10,0},{12,6},{14,4},{1,11},{3,9}... | collective-permute-start | bytes 221192 | tf_op jit(solution)/shard_map/ppermute | solution.py:259
  80.0 12.7 %collective-permute-done.16.refs_13_ = bf16[6,96,128]{2,1,0:T(8,128)(2,1)S(1)} collective-permute-done((bf16[6,96,128]{2,1,0:T(8,128)(2,1)S(1)}, bf16[6,96,128]{2,1,0:T(8,128)(2,1)S(1)}, u32[]{:S(2)}, u32[]{:S(2)}) %collective-permute-start.16) | collective-permute-done | bytes 147488 | tf_op jit(solution)/shard_map/ppermute | solution.py:259
  92.7 1.8 %group.3.refs_17_ = f32[256,256]{1,0:T(8,128)S(1)} custom-call(bf16[512,512]{1,0:T(8,128)(2,1)S(1)} %ordered_metric.1.refs_0_.refs_1_, bf16[16,32,128]{2,1,0:T(8,128)(2,1)S(1)} %get-tuple-element.53.refs_1_.refs_2_, bf16[16,32,128]{2,1,0:T(8,128)(2,1)S(1)} %collective-permute-done.5._.refs_2_.refs_3_, ...), custom_call_target="tpu_custom_call" | custom-call | flops 1409286144 | bytes 1835008 | tf_op jit(solution)/shard_map/group/pallas_call | solution.py:231
  94.5 4.4 %collective-permute-start.22 = (bf16[3,96,128]{2,1,0:T(8,128)(2,1)S(1)}, bf16[3,96,128]{2,1,0:T(8,128)(2,1)S(1)}, u32[]{:S(2)}, u32[]{:S(2)}) collective-permute-start(bf16[3,96,128]{2,1,0:T(8,128)(2,1)S(1)} %get-tuple-element.88), channel_id=1, source_target_pairs={{0,12},{2,14},{4,8},{6,10},{8,4},{10,6},{12,0},{14,2},{1,13},{3,15... | collective-permute-start | bytes 221192 | tf_op jit(solution)/shard_map/ppermute | solution.py:259
  99.0 1.6 %group.4.refs_18_ = f32[256,256]{1,0:T(8,128)S(1)} custom-call(bf16[512,512]{1,0:T(8,128)(2,1)S(1)} %ordered_metric.1.refs_0_.refs_1_, bf16[16,32,128]{2,1,0:T(8,128)(2,1)S(1)} %get-tuple-element.53.refs_1_.refs_2_, bf16[16,32,128]{2,1,0:T(8,128)(2,1)S(1)} %collective-permute-done.5._.refs_2_.refs_3_, ...), custom_call_target="tpu_custom_call" | custom-call | flops 1207959552 | bytes 1572864 | tf_op jit(solution)/shard_map/group/pallas_call | solution.py:231
  100.6 2.1 %collective-permute-done.20.refs_15_ = bf16[3,96,128]{2,1,0:T(8,128)(2,1)S(1)} collective-permute-done((bf16[3,96,128]{2,1,0:T(8,128)(2,1)S(1)}, bf16[3,96,128]{2,1,0:T(8,128)(2,1)S(1)}, u32[]{:S(2)}, u32[]{:S(2)}) %collective-permute-start.20) | collective-permute-done | bytes 73760 | tf_op jit(solution)/shard_map/ppermute | solution.py:259
  102.7 0.4 collective-permute-done.17.refs_14_
  103.0 1.0 group.5
  104.2 1.3 %collective-permute-done.27 = f32[4,32,256]{2,1,0:T(8,128)S(1)} collective-permute-done((f32[4,32,256]{2,1,0:T(8,128)S(1)}, f32[4,32,256]{2,1,0:T(8,128)S(1)}, u32[]{:S(2)}, u32[]{:S(2)}) %collective-permute-start.27) | collective-permute-done | bytes 131104 | tf_op jit(solution)/shard_map/ppermute | solution.py:262
  105.5 1.1 collective-permute-start.28
  106.6 3.3 %collective-permute-done.28 = f32[4,32,128]{2,1,0:T(8,128)S(1)} collective-permute-done((f32[4,32,128]{2,1,0:T(8,128)S(1)}, f32[4,32,128]{2,1,0:T(8,128)S(1)}, u32[]{:S(2)}, u32[]{:S(2)}) %collective-permute-start.28) | collective-permute-done | bytes 65568 | tf_op jit(solution)/shard_map/ppermute | solution.py:259
  109.9 2.2 %collective-permute-start.29 = (f32[32,128]{1,0:T(8,128)S(1)}, f32[32,128]{1,0:T(8,128)S(1)}, u32[]{:S(2)}, u32[]{:S(2)}) collective-permute-start(f32[32,128]{1,0:T(8,128)S(1)} %get-tuple-element.99), channel_id=1, source_target_pairs={{0,12},{2,14},{4,8},{6,10},{8,4},{10,6},{12,0},{14,2},{1,13},{3,15... | collective-permute-start | bytes 49160 | tf_op jit(solution)/shard_map/ppermute | solution.py:259
  112.1 1.7 %collective-permute-start.31 = (f32[32,128]{1,0:T(8,128)S(1)}, f32[32,128]{1,0:T(8,128)S(1)}, u32[]{:S(2)}, u32[]{:S(2)}) collective-permute-start(f32[32,128]{1,0:T(8,128)S(1)} %get-tuple-element.100), channel_id=1, source_target_pairs={{0,4},{2,6},{4,0},{6,2},{8,12},{10,14},{12,8},{14,10},{1,5},{3,7},... | collective-permute-start | bytes 49160 | tf_op jit(solution)/shard_map/ppermute | solution.py:259
  113.8 1.4 %collective-permute-start.30 = (f32[32,128]{1,0:T(8,128)S(1)}, f32[32,128]{1,0:T(8,128)S(1)}, u32[]{:S(2)}, u32[]{:S(2)}) collective-permute-start(f32[32,128]{1,0:T(8,128)S(1)} %get-tuple-element.101), channel_id=1, source_target_pairs={{0,8},{2,10},{4,12},{6,14},{8,0},{10,2},{12,4},{14,6},{1,9},{3,11}... | collective-permute-start | bytes 49160 | tf_op jit(solution)/shard_map/ppermute | solution.py:259
  115.1 0.3 collective-permute-done.29
  115.5 0.4 collective-permute-done.31
  115.8 2.6 %collective-permute-done.30 = f32[32,128]{1,0:T(8,128)S(1)} collective-permute-done((f32[32,128]{1,0:T(8,128)S(1)}, f32[32,128]{1,0:T(8,128)S(1)}, u32[]{:S(2)}, u32[]{:S(2)}) %collective-permute-start.30) | collective-permute-done | bytes 16416 | tf_op jit(solution)/shard_map/ppermute | solution.py:259
  118.4 0.6 fusion.4
  (40 shorter events, 0.5 us)
Async XLA Ops:
  0.0 2.9 %copy-start = (bf16[128,512]{1,0:T(8,128)(2,1)S(1)}, bf16[128,512]{1,0:T(8,128)(2,1)}, u32[]{:S(2)}) copy-start(bf16[128,512]{1,0:T(8,128)(2,1)} %param.8) | copy-start | bytes 393220
  0.0 9.5 %copy-start.1 = (bf16[1024,128]{1,0:T(8,128)(2,1)S(1)}, bf16[1024,128]{1,0:T(8,128)(2,1)}, u32[]{:S(2)}) copy-start(bf16[1024,128]{1,0:T(8,128)(2,1)} %own_ref) | copy-start | bytes 786436
  0.0 9.5 %collective-permute-start.4 = (bf16[1024,128]{1,0:T(8,128)(2,1)}, bf16[1024,128]{1,0:T(8,128)(2,1)S(1)}, u32[]{:S(2)}, u32[]{:S(2)}) collective-permute-start(bf16[1024,128]{1,0:T(8,128)(2,1)} %own_ref), channel_id=1, source_target_pairs={{0,2},{2,0},{4,6},{6,4},{8,10},{10,8},{12,14},{14,12},{1,3},{3,1},... | collective-permute-start | bytes 786440 | tf_op jit(solution)/shard_map/ppermute | solution.py:259
  3.0 5.4 %collective-permute-start = (bf16[32,512]{1,0:T(8,128)(2,1)S(1)}, bf16[32,512]{1,0:T(8,128)(2,1)S(1)}, u32[]{:S(2)}, u32[]{:S(2)}) collective-permute-start(bf16[32,512]{1,0:T(8,128)(2,1)S(1)} %constant_dynamic-slice_fusion), channel_id=1, source_target_pairs={{0,8},{2,10},{4,12},{6,14},{8,0},{10,2},{12,4},{14,6},{1,9},{3,11}... | collective-permute-start | bytes 98312 | tf_op jit(solution)/shard_map/ppermute | solution.py:259
  8.3 68.9 %copy-start.2 = (s32[4]{0:T(128)S(1)}, s32[4]{0:T(128)}, u32[]{:S(2)}) copy-start(s32[4]{0:T(128)} %param.9) | copy-start | bytes 52
  10.3 8.6 %collective-permute-start.8 = (bf16[16,32,128]{2,1,0:T(8,128)(2,1)S(1)}, bf16[16,32,128]{2,1,0:T(8,128)(2,1)S(1)}, u32[]{:S(2)}, u32[]{:S(2)}) collective-permute-start(bf16[16,32,128]{2,1,0:T(8,128)(2,1)S(1)} %get-tuple-element.61), channel_id=1, source_target_pairs={{0,8},{2,10},{4,12},{6,14},{8,0},{10,2},{12,4},{14,6},{1,9},{3,11}... | collective-permute-start | bytes 393224 | tf_op jit(solution)/shard_map/ppermute | solution.py:259
  13.2 11.2 %collective-permute-start.5 = (bf16[16,32,128]{2,1,0:T(8,128)(2,1)S(1)}, bf16[16,32,128]{2,1,0:T(8,128)(2,1)S(1)}, u32[]{:S(2)}, u32[]{:S(2)}) collective-permute-start(bf16[16,32,128]{2,1,0:T(8,128)(2,1)S(1)} %get-tuple-element.54), channel_id=1, source_target_pairs={{0,2},{2,0},{4,6},{6,4},{8,10},{10,8},{12,14},{14,12},{1,3},{3,1},... | collective-permute-start | bytes 393224 | tf_op jit(solution)/shard_map/ppermute | solution.py:259
  14.7 17.7 %collective-permute-start.7 = (bf16[16,32,128]{2,1,0:T(8,128)(2,1)S(1)}, bf16[16,32,128]{2,1,0:T(8,128)(2,1)S(1)}, u32[]{:S(2)}, u32[]{:S(2)}) collective-permute-start(bf16[16,32,128]{2,1,0:T(8,128)(2,1)S(1)} %get-tuple-element.60), channel_id=1, source_target_pairs={{0,6},{2,4},{4,2},{6,0},{8,14},{10,12},{12,10},{14,8},{1,7},{3,5},... | collective-permute-start | bytes 393224 | tf_op jit(solution)/shard_map/ppermute | solution.py:259
  16.2 16.1 %collective-permute-start.9 = (bf16[16,32,128]{2,1,0:T(8,128)(2,1)S(1)}, bf16[16,32,128]{2,1,0:T(8,128)(2,1)S(1)}, u32[]{:S(2)}, u32[]{:S(2)}) collective-permute-start(bf16[16,32,128]{2,1,0:T(8,128)(2,1)S(1)} %get-tuple-element.62), channel_id=1, source_target_pairs={{0,10},{2,8},{4,14},{6,12},{8,2},{10,0},{12,6},{14,4},{1,11},{3,9}... | collective-permute-start | bytes 393224 | tf_op jit(solution)/shard_map/ppermute | solution.py:259
  17.5 19.3 %collective-permute-start.1 = (bf16[64,512]{1,0:T(8,128)(2,1)S(1)}, bf16[64,512]{1,0:T(8,128)(2,1)S(1)}, u32[]{:S(2)}, u32[]{:S(2)}) collective-permute-start(bf16[64,512]{1,0:T(8,128)(2,1)S(1)} %pad_maximum_fusion.2), channel_id=1, source_target_pairs={{0,4},{2,6},{4,0},{6,2},{8,12},{10,14},{12,8},{14,10},{1,5},{3,7},... | collective-permute-start | bytes 196616 | tf_op jit(solution)/shard_map/ppermute | solution.py:259
  18.9 18.0 %collective-permute-start.10 = (bf16[16,32,128]{2,1,0:T(8,128)(2,1)S(1)}, bf16[16,32,128]{2,1,0:T(8,128)(2,1)S(1)}, u32[]{:S(2)}, u32[]{:S(2)}) collective-permute-start(bf16[16,32,128]{2,1,0:T(8,128)(2,1)S(1)} %get-tuple-element.63), channel_id=1, source_target_pairs={{0,12},{2,14},{4,8},{6,10},{8,4},{10,6},{12,0},{14,2},{1,13},{3,15... | collective-permute-start | bytes 393224 | tf_op jit(solution)/shard_map/ppermute | solution.py:259
  24.4 14.0 %collective-permute-start.11 = (bf16[16,32,128]{2,1,0:T(8,128)(2,1)S(1)}, bf16[16,32,128]{2,1,0:T(8,128)(2,1)S(1)}, u32[]{:S(2)}, u32[]{:S(2)}) collective-permute-start(bf16[16,32,128]{2,1,0:T(8,128)(2,1)S(1)} %get-tuple-element.65), channel_id=1, source_target_pairs={{0,14},{2,12},{4,10},{6,8},{8,6},{10,4},{12,2},{14,0},{1,15},{3,13... | collective-permute-start | bytes 393224 | tf_op jit(solution)/shard_map/ppermute | solution.py:259
  32.4 6.6 %collective-permute-start.6 = (bf16[16,32,128]{2,1,0:T(8,128)(2,1)S(1)}, bf16[16,32,128]{2,1,0:T(8,128)(2,1)S(1)}, u32[]{:S(2)}, u32[]{:S(2)}) collective-permute-start(bf16[16,32,128]{2,1,0:T(8,128)(2,1)S(1)} %get-tuple-element.59), channel_id=1, source_target_pairs={{0,4},{2,6},{4,0},{6,2},{8,12},{10,14},{12,8},{14,10},{1,5},{3,7},... | collective-permute-start | bytes 393224 | tf_op jit(solution)/shard_map/ppermute | solution.py:259
  32.5 19.2 %collective-permute-start.24 = (bf16[7,96,128]{2,1,0:T(8,128)(2,1)S(1)}, bf16[7,96,128]{2,1,0:T(8,128)(2,1)S(1)}, u32[]{:S(2)}, u32[]{:S(2)}) collective-permute-start(bf16[7,96,128]{2,1,0:T(8,128)(2,1)S(1)} %get-tuple-element.93), channel_id=1, source_target_pairs={{0,8},{2,10},{4,12},{6,14},{8,0},{10,2},{12,4},{14,6},{1,9},{3,11}... | collective-permute-start | bytes 516104 | tf_op jit(solution)/shard_map/ppermute | solution.py:259
  36.8 18.8 %collective-permute-start.14 = (bf16[7,96,128]{2,1,0:T(8,128)(2,1)S(1)}, bf16[7,96,128]{2,1,0:T(8,128)(2,1)S(1)}, u32[]{:S(2)}, u32[]{:S(2)}) collective-permute-start(bf16[7,96,128]{2,1,0:T(8,128)(2,1)S(1)} %get-tuple-element.73), channel_id=1, source_target_pairs={{0,10},{2,8},{4,14},{6,12},{8,2},{10,0},{12,6},{14,4},{1,11},{3,9}... | collective-permute-start | bytes 516104 | tf_op jit(solution)/shard_map/ppermute | solution.py:259
  36.9 22.3 %collective-permute-start.2 = (bf16[128,512]{1,0:T(8,128)(2,1)S(1)}, bf16[128,512]{1,0:T(8,128)(2,1)S(1)}, u32[]{:S(2)}, u32[]{:S(2)}) collective-permute-start(bf16[128,512]{1,0:T(8,128)(2,1)S(1)} %pad_maximum_fusion.1), channel_id=1, source_target_pairs={{0,2},{2,0},{4,6},{6,4},{8,10},{10,8},{12,14},{14,12},{1,3},{3,1},... | collective-permute-start | bytes 393224 | tf_op jit(solution)/shard_map/ppermute | solution.py:259
  38.4 20.9 %collective-permute-start.12 = (bf16[16,96,128]{2,1,0:T(8,128)(2,1)S(1)}, bf16[16,96,128]{2,1,0:T(8,128)(2,1)S(1)}, u32[]{:S(2)}, u32[]{:S(2)}) collective-permute-start(bf16[16,96,128]{2,1,0:T(8,128)(2,1)S(1)} %get-tuple-element.68), channel_id=1, source_target_pairs={{0,2},{2,0},{4,6},{6,4},{8,10},{10,8},{12,14},{14,12},{1,3},{3,1},... | collective-permute-start | bytes 1179656 | tf_op jit(solution)/shard_map/ppermute | solution.py:259
  38.9 20.2 %collective-permute-start.18 = (bf16[7,96,128]{2,1,0:T(8,128)(2,1)S(1)}, bf16[7,96,128]{2,1,0:T(8,128)(2,1)S(1)}, u32[]{:S(2)}, u32[]{:S(2)}) collective-permute-start(bf16[7,96,128]{2,1,0:T(8,128)(2,1)S(1)} %get-tuple-element.82), channel_id=1, source_target_pairs={{0,12},{2,14},{4,8},{6,10},{8,4},{10,6},{12,0},{14,2},{1,13},{3,15... | collective-permute-start | bytes 516104 | tf_op jit(solution)/shard_map/ppermute | solution.py:259
  51.7 20.5 %collective-permute-start.13 = (bf16[16,96,128]{2,1,0:T(8,128)(2,1)S(1)}, bf16[16,96,128]{2,1,0:T(8,128)(2,1)S(1)}, u32[]{:S(2)}, u32[]{:S(2)}) collective-permute-start(bf16[16,96,128]{2,1,0:T(8,128)(2,1)S(1)} %get-tuple-element.70), channel_id=1, source_target_pairs={{0,4},{2,6},{4,0},{6,2},{8,12},{10,14},{12,8},{14,10},{1,5},{3,7},... | collective-permute-start | bytes 1179656 | tf_op jit(solution)/shard_map/ppermute | solution.py:259
  55.6 13.7 %collective-permute-start.25 = (bf16[7,96,128]{2,1,0:T(8,128)(2,1)S(1)}, bf16[7,96,128]{2,1,0:T(8,128)(2,1)S(1)}, u32[]{:S(2)}, u32[]{:S(2)}) collective-permute-start(bf16[7,96,128]{2,1,0:T(8,128)(2,1)S(1)} %get-tuple-element.94), channel_id=1, source_target_pairs={{0,14},{2,12},{4,10},{6,8},{8,6},{10,4},{12,2},{14,0},{1,15},{3,13... | collective-permute-start | bytes 516104 | tf_op jit(solution)/shard_map/ppermute | solution.py:259
  59.1 33.5 %collective-permute-start.15 = (bf16[16,96,128]{2,1,0:T(8,128)(2,1)S(1)}, bf16[16,96,128]{2,1,0:T(8,128)(2,1)S(1)}, u32[]{:S(2)}, u32[]{:S(2)}) collective-permute-start(bf16[16,96,128]{2,1,0:T(8,128)(2,1)S(1)} %get-tuple-element.74), channel_id=1, source_target_pairs={{0,6},{2,4},{4,2},{6,0},{8,14},{10,12},{12,10},{14,8},{1,7},{3,5},... | collective-permute-start | bytes 1179656 | tf_op jit(solution)/shard_map/ppermute | solution.py:259
  59.2 16.4 %collective-permute-start.3 = (bf16[256,512]{1,0:T(8,128)(2,1)S(1)}, bf16[256,512]{1,0:T(8,128)(2,1)S(1)}, u32[]{:S(2)}, u32[]{:S(2)}) collective-permute-start(bf16[256,512]{1,0:T(8,128)(2,1)S(1)} %pad_maximum_fusion.refs_0_), channel_id=1, source_target_pairs={{0,1},{1,0},{2,3},{3,2},{4,5},{5,4},{6,7},{7,6},{8,9},{9,8},{10,11... | collective-permute-start | bytes 786440 | tf_op jit(solution)/shard_map/ppermute | solution.py:262
  59.3 18.7 %collective-permute-start.19 = (bf16[6,96,128]{2,1,0:T(8,128)(2,1)S(1)}, bf16[6,96,128]{2,1,0:T(8,128)(2,1)S(1)}, u32[]{:S(2)}, u32[]{:S(2)}) collective-permute-start(bf16[6,96,128]{2,1,0:T(8,128)(2,1)S(1)} %get-tuple-element.83), channel_id=1, source_target_pairs={{0,10},{2,8},{4,14},{6,12},{8,2},{10,0},{12,6},{14,4},{1,11},{3,9}... | collective-permute-start | bytes 442376 | tf_op jit(solution)/shard_map/ppermute | solution.py:259
  69.3 23.4 %collective-permute-start.16 = (bf16[6,96,128]{2,1,0:T(8,128)(2,1)S(1)}, bf16[6,96,128]{2,1,0:T(8,128)(2,1)S(1)}, u32[]{:S(2)}, u32[]{:S(2)}) collective-permute-start(bf16[6,96,128]{2,1,0:T(8,128)(2,1)S(1)} %get-tuple-element.77), channel_id=1, source_target_pairs={{0,8},{2,10},{4,12},{6,14},{8,0},{10,2},{12,4},{14,6},{1,9},{3,11}... | collective-permute-start | bytes 442376 | tf_op jit(solution)/shard_map/ppermute | solution.py:259
  72.2 26.8 %collective-permute-start.26 = (bf16[6,96,128]{2,1,0:T(8,128)(2,1)S(1)}, bf16[6,96,128]{2,1,0:T(8,128)(2,1)S(1)}, u32[]{:S(2)}, u32[]{:S(2)}) collective-permute-start(bf16[6,96,128]{2,1,0:T(8,128)(2,1)S(1)} %get-tuple-element.95), channel_id=1, source_target_pairs={{0,12},{2,14},{4,8},{6,10},{8,4},{10,6},{12,0},{14,2},{1,13},{3,15... | collective-permute-start | bytes 442376 | tf_op jit(solution)/shard_map/ppermute | solution.py:259
  75.6 19.0 %collective-permute-start.21 = (bf16[6,96,128]{2,1,0:T(8,128)(2,1)S(1)}, bf16[6,96,128]{2,1,0:T(8,128)(2,1)S(1)}, u32[]{:S(2)}, u32[]{:S(2)}) collective-permute-start(bf16[6,96,128]{2,1,0:T(8,128)(2,1)S(1)} %get-tuple-element.87), channel_id=1, source_target_pairs={{0,14},{2,12},{4,10},{6,8},{8,6},{10,4},{12,2},{14,0},{1,15},{3,13... | collective-permute-start | bytes 442376 | tf_op jit(solution)/shard_map/ppermute | solution.py:259
  78.0 24.7 %collective-permute-start.20 = (bf16[3,96,128]{2,1,0:T(8,128)(2,1)S(1)}, bf16[3,96,128]{2,1,0:T(8,128)(2,1)S(1)}, u32[]{:S(2)}, u32[]{:S(2)}) collective-permute-start(bf16[3,96,128]{2,1,0:T(8,128)(2,1)S(1)} %get-tuple-element.84), channel_id=1, source_target_pairs={{0,10},{2,8},{4,14},{6,12},{8,2},{10,0},{12,6},{14,4},{1,11},{3,9}... | collective-permute-start | bytes 221192 | tf_op jit(solution)/shard_map/ppermute | solution.py:259
  92.7 10.4 %collective-permute-start.17 = (bf16[3,96,128]{2,1,0:T(8,128)(2,1)S(1)}, bf16[3,96,128]{2,1,0:T(8,128)(2,1)S(1)}, u32[]{:S(2)}, u32[]{:S(2)}) collective-permute-start(bf16[3,96,128]{2,1,0:T(8,128)(2,1)S(1)} %get-tuple-element.78), channel_id=1, source_target_pairs={{0,8},{2,10},{4,12},{6,14},{8,0},{10,2},{12,4},{14,6},{1,9},{3,11}... | collective-permute-start | bytes 221192 | tf_op jit(solution)/shard_map/ppermute | solution.py:259
  92.7 10.4 %collective-permute-start.23 = (bf16[3,96,128]{2,1,0:T(8,128)(2,1)S(1)}, bf16[3,96,128]{2,1,0:T(8,128)(2,1)S(1)}, u32[]{:S(2)}, u32[]{:S(2)}) collective-permute-start(bf16[3,96,128]{2,1,0:T(8,128)(2,1)S(1)} %get-tuple-element.90), channel_id=1, source_target_pairs={{0,14},{2,12},{4,10},{6,8},{8,6},{10,4},{12,2},{14,0},{1,15},{3,13... | collective-permute-start | bytes 221192 | tf_op jit(solution)/shard_map/ppermute | solution.py:259
  94.5 8.5 %collective-permute-start.22 = (bf16[3,96,128]{2,1,0:T(8,128)(2,1)S(1)}, bf16[3,96,128]{2,1,0:T(8,128)(2,1)S(1)}, u32[]{:S(2)}, u32[]{:S(2)}) collective-permute-start(bf16[3,96,128]{2,1,0:T(8,128)(2,1)S(1)} %get-tuple-element.88), channel_id=1, source_target_pairs={{0,12},{2,14},{4,8},{6,10},{8,4},{10,6},{12,0},{14,2},{1,13},{3,15... | collective-permute-start | bytes 221192 | tf_op jit(solution)/shard_map/ppermute | solution.py:259
  104.1 1.4 %collective-permute-start.27 = (f32[4,32,256]{2,1,0:T(8,128)S(1)}, f32[4,32,256]{2,1,0:T(8,128)S(1)}, u32[]{:S(2)}, u32[]{:S(2)}) collective-permute-start(f32[4,32,256]{2,1,0:T(8,128)S(1)} %get-tuple-element.97), channel_id=1, source_target_pairs={{0,1},{1,0},{2,3},{3,2},{4,5},{5,4},{6,7},{7,6},{8,9},{9,8},{10,11... | collective-permute-start | bytes 393224 | tf_op jit(solution)/shard_map/ppermute | solution.py:262
  105.5 4.3 %collective-permute-start.28 = (f32[4,32,128]{2,1,0:T(8,128)S(1)}, f32[4,32,128]{2,1,0:T(8,128)S(1)}, u32[]{:S(2)}, u32[]{:S(2)}) collective-permute-start(f32[4,32,128]{2,1,0:T(8,128)S(1)} %slice_add_fusion), channel_id=1, source_target_pairs={{0,2},{2,0},{4,6},{6,4},{8,10},{10,8},{12,14},{14,12},{1,3},{3,1},... | collective-permute-start | bytes 196616 | tf_op jit(solution)/shard_map/ppermute | solution.py:259
  109.9 5.6 %collective-permute-start.29 = (f32[32,128]{1,0:T(8,128)S(1)}, f32[32,128]{1,0:T(8,128)S(1)}, u32[]{:S(2)}, u32[]{:S(2)}) collective-permute-start(f32[32,128]{1,0:T(8,128)S(1)} %get-tuple-element.99), channel_id=1, source_target_pairs={{0,12},{2,14},{4,8},{6,10},{8,4},{10,6},{12,0},{14,2},{1,13},{3,15... | collective-permute-start | bytes 49160 | tf_op jit(solution)/shard_map/ppermute | solution.py:259
  112.1 3.7 %collective-permute-start.31 = (f32[32,128]{1,0:T(8,128)S(1)}, f32[32,128]{1,0:T(8,128)S(1)}, u32[]{:S(2)}, u32[]{:S(2)}) collective-permute-start(f32[32,128]{1,0:T(8,128)S(1)} %get-tuple-element.100), channel_id=1, source_target_pairs={{0,4},{2,6},{4,0},{6,2},{8,12},{10,14},{12,8},{14,10},{1,5},{3,7},... | collective-permute-start | bytes 49160 | tf_op jit(solution)/shard_map/ppermute | solution.py:259
  113.8 4.6 %collective-permute-start.30 = (f32[32,128]{1,0:T(8,128)S(1)}, f32[32,128]{1,0:T(8,128)S(1)}, u32[]{:S(2)}, u32[]{:S(2)}) collective-permute-start(f32[32,128]{1,0:T(8,128)S(1)} %get-tuple-element.101), channel_id=1, source_target_pairs={{0,8},{2,10},{4,12},{6,14},{8,0},{10,2},{12,4},{14,6},{1,9},{3,11}... | collective-permute-start | bytes 49160 | tf_op jit(solution)/shard_map/ppermute | solution.py:259

commit v6 on v5

--- a/solution.py
+++ b/solution.py
@@ -13,14 +13,14 @@
 WINDOW = 5
 GROUPS = ((0, 7), (7, 13), (13, 16))
 FIRST = 32
-OPEN = (4, 1, 5, 3, 6, 7)
+OPEN = (6, 1, 5, 3, 4, 7)
 ORDER = (
-    ((2, -1), (4, 0), (5, 0), (1, 0), (6, 0), (2, 0), (7, 0), (3, 0))
+    ((2, -1), (5, 0), (4, 0), (1, 0), (6, 0), (2, 0), (7, 0), (3, 0))
     + ((4, 1), (5, 1), (7, 1), (6, 1))
     + ((7, 2), (4, 2), (5, 2), (6, 2))
 )
 RESTDEP = 1
-LAST = (3, 2, 1)
+LAST = (3, 1, 2)
 WHOLE = pl.BlockSpec(memory_space=pltpu.VMEM)
 
 
@@ -190,7 +190,7 @@
     if not last:
         refs[0][...] = total
         return
-    kept, near, away, scratch = refs
+    kept, near, kept_away, near_away, scratch = refs
     scratch[...] = total
     width = side // bas
     piece = kept.shape[1]
@@ -202,11 +202,8 @@
             block = lax.div(row, width) ^ b_here
             start = pl.multiple_of(block * width + lax.rem(row, width), piece)
             value = scratch[pl.ds(start, piece), :]
-            if who:
-                away[ka] = value
-            else:
-                kept[ka] = value[:, :width]
-                near[ka] = value[:, width:]
+            (kept_away if who else kept)[ka] = value[:, :width]
+            (near_away if who else near)[ka] = value[:, width:]
 
 
 def group(aux, bas, lo, hi, metric, early, late, total, where=None):
@@ -219,11 +216,7 @@
     specs = [WHOLE] * len(args)
     if last:
         piece = side // (aux * 2)
-        out = [
-            jax.ShapeDtypeStruct((aux, piece, width), F32),
-            jax.ShapeDtypeStruct((aux, piece, width), F32),
-            jax.ShapeDtypeStruct((aux, piece, side), F32),
-        ]
+        out = [jax.ShapeDtypeStruct((aux, piece, width), F32)] * 4
     else:
         out = jax.ShapeDtypeStruct((side, side), F32)
     rows = metric.shape[0]
@@ -231,7 +224,7 @@
     return pl.pallas_call(
         functools.partial(group_kernel, aux, bas, lo, hi, starts, started, last),
         in_specs=specs,
-        out_specs=[WHOLE] * 3 if last else WHOLE,
+        out_specs=[WHOLE] * 4 if last else WHOLE,
         out_shape=out,
         scratch_shapes=[pltpu.VMEM((side, side), F32)] if last else [],
         compiler_params=params(),
@@ -248,8 +241,7 @@
     orbitals = coefficients.shape[1]
     share = orbitals // chips
     a, b, o = (lax.axis_index(name) for name in ("aux", "bas", "occ"))
-    first = FIRST
-    groups = GROUPS
+    first, groups = FIRST, GROUPS
     inner, outer = (1, 2, 3), (4, 5, 6, 7)
 
     def swap(value, kz=0, kx=0):
@@ -309,12 +301,11 @@
         ]
         place = jnp.stack([a, b, o]).astype(jnp.int32) if g == len(groups) - 1 else None
         total = group(aux, bas, lo, hi, ordered, early, part, total, place)
-    kept, near, away = total
-    away = across(away)
-    width = kept.shape[2]
-    kept = kept + away[:, :, :width]
-    near = near + away[:, :, width:]
-    kept = kept + swap(near, kx=1)
+    kept, near, kept_away, near_away = total
+    near = near + across(near_away)
+    near = swap(near, kx=1)
+    kept = kept + across(kept_away)
+    kept = kept + near
     value = kept[0]
     for kz in LAST:
         value = value + swap(kept[kz], kz=kz)

time: 119 us -> 118 us (level)
  waiting for transfers between devices: 49 us -> 39.1 us
  starting transfers between devices: 53.3 us -> 61.8 us
    ppermute x30, waiting for transfers between devices: 47.6 us -> 38.3 us  [swap(): return lax.ppermute(value, ('aux', 'bas'), pairs)]
    ppermute x30, starting transfers between devices: 53.2 us -> 61.2 us  [swap(): return lax.ppermute(value, ('aux', 'bas'), pairs)]
  transfers between devices with their start and end apart: 32 -> 33, of which waited for: 14 -> 15; matrix products, arithmetic and copies ran while one was open for 1% -> 1% of each run, Pallas kernels for 11% -> 11%
where the time goes in v6:
time: 118 us
  starting transfers between devices  61.8 us (52%)
  waiting for transfers between devices  39.1 us (33%)
  Pallas kernels  15 us (13%)
  other arithmetic  1.55 us (1%)
    ppermute x30, starting transfers between devices, swap(): return lax.ppermute(value, ('aux', 'bas'), pairs)  61.2 us
    ppermute x30, waiting for transfers between devices, swap(): return lax.ppermute(value, ('aux', 'bas'), pairs)  38.3 us
    pallas_call x1, Pallas kernels, rest_products(): pl.pallas_call(functools.partial(rest_kernel, chips, spans), grid=(rest /...  7.03 us
    pallas_call x3, Pallas kernels, group(): pl.pallas_call(functools.partial(group_kernel, aux, bas, lo, hi, starts,...  4.48 us
  transfers between devices with their start and end apart: 33, of which 15 were waited for; matrix products, arithmetic and copies ran while one was open for 1% of the time, Pallas kernels for 11%

profile of v6, /device:TPU:0, one launch (start us, length us, event | category | flops | bytes accessed | tf_op | source)
XLA Modules:
  0.0 117.6 jit_solution(16274791812259252534)
XLA Ops:
  0.0 2.9 %collective-permute-start.4 = (bf16[1024,128]{1,0:T(8,128)(2,1)}, bf16[1024,128]{1,0:T(8,128)(2,1)S(1)}, u32[]{:S(2)}, u32[]{:S(2)}) collective-permute-start(bf16[1024,128]{1,0:T(8,128)(2,1)} %own_ref), channel_id=1, source_target_pairs={{0,2},{2,0},{4,6},{6,4},{8,10},{10,8},{12,14},{14,12},{1,3},{3,1},... | collective-permute-start | bytes 786440 | tf_op jit(solution)/shard_map/ppermute | solution.py:251
  3.0 2.6 %collective-permute-start = (bf16[32,512]{1,0:T(8,128)(2,1)S(1)}, bf16[32,512]{1,0:T(8,128)(2,1)S(1)}, u32[]{:S(2)}, u32[]{:S(2)}) collective-permute-start(bf16[32,512]{1,0:T(8,128)(2,1)S(1)} %constant_dynamic-slice_fusion), channel_id=1, source_target_pairs={{0,8},{2,10},{4,12},{6,14},{8,0},{10,2},{12,4},{14,6},{1,9},{3,11}... | collective-permute-start | bytes 98312 | tf_op jit(solution)/shard_map/ppermute | solution.py:251
  5.5 0.7 add_bitcast_fusion.1.where
  6.3 2.0 %relayout.1.x_ref = bf16[32,256,128]{2,1,0:T(8,128)(2,1)S(1)} custom-call(bf16[2,128,128,128]{3,2,1,0:T(8,128)(2,1)} %bitcast.28), custom_call_target="tpu_custom_call" | custom-call | bytes 4194304 | tf_op jit(solution)/shard_map/relayout/pallas_call | solution.py:42
  8.3 1.2 collective-permute-done.4.other_ref
  9.5 0.8 first_products.1
  10.3 3.9 %collective-permute-start.10 = (bf16[16,32,128]{2,1,0:T(8,128)(2,1)S(1)}, bf16[16,32,128]{2,1,0:T(8,128)(2,1)S(1)}, u32[]{:S(2)}, u32[]{:S(2)}) collective-permute-start(bf16[16,32,128]{2,1,0:T(8,128)(2,1)S(1)} %get-tuple-element.64), channel_id=1, source_target_pairs={{0,12},{2,14},{4,8},{6,10},{8,4},{10,6},{12,0},{14,2},{1,13},{3,15... | collective-permute-start | bytes 393224 | tf_op jit(solution)/shard_map/ppermute | solution.py:251
  14.2 1.5 %collective-permute-start.5 = (bf16[16,32,128]{2,1,0:T(8,128)(2,1)S(1)}, bf16[16,32,128]{2,1,0:T(8,128)(2,1)S(1)}, u32[]{:S(2)}, u32[]{:S(2)}) collective-permute-start(bf16[16,32,128]{2,1,0:T(8,128)(2,1)S(1)} %get-tuple-element.55), channel_id=1, source_target_pairs={{0,2},{2,0},{4,6},{6,4},{8,10},{10,8},{12,14},{14,12},{1,3},{3,1},... | collective-permute-start | bytes 393224 | tf_op jit(solution)/shard_map/ppermute | solution.py:251
  15.7 1.7 %collective-permute-start.9 = (bf16[16,32,128]{2,1,0:T(8,128)(2,1)S(1)}, bf16[16,32,128]{2,1,0:T(8,128)(2,1)S(1)}, u32[]{:S(2)}, u32[]{:S(2)}) collective-permute-start(bf16[16,32,128]{2,1,0:T(8,128)(2,1)S(1)} %get-tuple-element.63), channel_id=1, source_target_pairs={{0,10},{2,8},{4,14},{6,12},{8,2},{10,0},{12,6},{14,4},{1,11},{3,9}... | collective-permute-start | bytes 393224 | tf_op jit(solution)/shard_map/ppermute | solution.py:251
  17.4 0.7 collective-permute-start.1
  18.1 0.3 collective-permute-done.10.refs_7_.refs_8_
  18.4 5.1 %collective-permute-start.8 = (bf16[16,32,128]{2,1,0:T(8,128)(2,1)S(1)}, bf16[16,32,128]{2,1,0:T(8,128)(2,1)S(1)}, u32[]{:S(2)}, u32[]{:S(2)}) collective-permute-start(bf16[16,32,128]{2,1,0:T(8,128)(2,1)S(1)} %get-tuple-element.62), channel_id=1, source_target_pairs={{0,8},{2,10},{4,12},{6,14},{8,0},{10,2},{12,4},{14,6},{1,9},{3,11}... | collective-permute-start | bytes 393224 | tf_op jit(solution)/shard_map/ppermute | solution.py:251
  23.5 1.3 %collective-permute-start.11 = (bf16[16,32,128]{2,1,0:T(8,128)(2,1)S(1)}, bf16[16,32,128]{2,1,0:T(8,128)(2,1)S(1)}, u32[]{:S(2)}, u32[]{:S(2)}) collective-permute-start(bf16[16,32,128]{2,1,0:T(8,128)(2,1)S(1)} %get-tuple-element.66), channel_id=1, source_target_pairs={{0,14},{2,12},{4,10},{6,8},{8,6},{10,4},{12,2},{14,0},{1,15},{3,13... | collective-permute-start | bytes 393224 | tf_op jit(solution)/shard_map/ppermute | solution.py:251
  24.8 7.0 %rest_products.1 = (bf16[7,96,128]{2,1,0:T(8,128)(2,1)S(1)}, bf16[7,96,128]{2,1,0:T(8,128)(2,1)S(1)}, bf16[7,96,128]{2,1,0:T(8,128)(2,1)S(1)}, bf16[7,96,128]{2,...) custom-call(bf16[2,128,128,128]{3,2,1,0:T(8,128)(2,1)} %bitcast.29, ...), custom_call_target="tpu_custom_call" | custom-call | flops 805306368 | bytes 8388608 | tf_op jit(solution)/shard_map/rest_products/pallas_call | solution.py:119
  31.9 0.3 collective-permute-start.6
  32.2 3.8 %collective-permute-start.14 = (bf16[7,96,128]{2,1,0:T(8,128)(2,1)S(1)}, bf16[7,96,128]{2,1,0:T(8,128)(2,1)S(1)}, u32[]{:S(2)}, u32[]{:S(2)}) collective-permute-start(bf16[7,96,128]{2,1,0:T(8,128)(2,1)S(1)} %get-tuple-element.73), channel_id=1, source_target_pairs={{0,8},{2,10},{4,12},{6,14},{8,0},{10,2},{12,4},{14,6},{1,9},{3,11}... | collective-permute-start | bytes 516104 | tf_op jit(solution)/shard_map/ppermute | solution.py:251
  36.0 1.6 %collective-permute-done.8.refs_5_.refs_6_ = bf16[16,32,128]{2,1,0:T(8,128)(2,1)S(1)} collective-permute-done((bf16[16,32,128]{2,1,0:T(8,128)(2,1)S(1)}, bf16[16,32,128]{2,1,0:T(8,128)(2,1)S(1)}, u32[]{:S(2)}, u32[]{:S(2)}) %collective-permute-start.8) | collective-permute-done | bytes 131104 | tf_op jit(solution)/shard_map/ppermute | solution.py:251
  37.7 1.1 collective-permute-start.2
  38.8 0.9 collective-permute-start.12
  39.7 8.2 %collective-permute-start.18 = (bf16[7,96,128]{2,1,0:T(8,128)(2,1)S(1)}, bf16[7,96,128]{2,1,0:T(8,128)(2,1)S(1)}, u32[]{:S(2)}, u32[]{:S(2)}) collective-permute-start(bf16[7,96,128]{2,1,0:T(8,128)(2,1)S(1)} %get-tuple-element.82), channel_id=1, source_target_pairs={{0,12},{2,14},{4,8},{6,10},{8,4},{10,6},{12,0},{14,2},{1,13},{3,15... | collective-permute-start | bytes 516104 | tf_op jit(solution)/shard_map/ppermute | solution.py:251
  47.9 3.7 %collective-permute-done.14.refs_13_ = bf16[7,96,128]{2,1,0:T(8,128)(2,1)S(1)} collective-permute-done((bf16[7,96,128]{2,1,0:T(8,128)(2,1)S(1)}, bf16[7,96,128]{2,1,0:T(8,128)(2,1)S(1)}, u32[]{:S(2)}, u32[]{:S(2)}) %collective-permute-start.14) | collective-permute-done | bytes 172064 | tf_op jit(solution)/shard_map/ppermute | solution.py:251
  51.6 4.2 %collective-permute-done.24.refs_14_ = bf16[7,96,128]{2,1,0:T(8,128)(2,1)S(1)} collective-permute-done((bf16[7,96,128]{2,1,0:T(8,128)(2,1)S(1)}, bf16[7,96,128]{2,1,0:T(8,128)(2,1)S(1)}, u32[]{:S(2)}, u32[]{:S(2)}) %collective-permute-start.24) | collective-permute-done | bytes 172064 | tf_op jit(solution)/shard_map/ppermute | solution.py:251
  55.8 3.5 %collective-permute-start.25 = (bf16[7,96,128]{2,1,0:T(8,128)(2,1)S(1)}, bf16[7,96,128]{2,1,0:T(8,128)(2,1)S(1)}, u32[]{:S(2)}, u32[]{:S(2)}) collective-permute-start(bf16[7,96,128]{2,1,0:T(8,128)(2,1)S(1)} %get-tuple-element.95), channel_id=1, source_target_pairs={{0,14},{2,12},{4,10},{6,8},{8,6},{10,4},{12,2},{14,0},{1,15},{3,13... | collective-permute-start | bytes 516104 | tf_op jit(solution)/shard_map/ppermute | solution.py:251
  59.4 4.5 %collective-permute-start.19 = (bf16[6,96,128]{2,1,0:T(8,128)(2,1)S(1)}, bf16[6,96,128]{2,1,0:T(8,128)(2,1)S(1)}, u32[]{:S(2)}, u32[]{:S(2)}) collective-permute-start(bf16[6,96,128]{2,1,0:T(8,128)(2,1)S(1)} %get-tuple-element.83), channel_id=1, source_target_pairs={{0,10},{2,8},{4,14},{6,12},{8,2},{10,0},{12,6},{14,4},{1,11},{3,9}... | collective-permute-start | bytes 442376 | tf_op jit(solution)/shard_map/ppermute | solution.py:251
  64.0 2.3 %collective-permute-done.25.refs_16_ = bf16[7,96,128]{2,1,0:T(8,128)(2,1)S(1)} collective-permute-done((bf16[7,96,128]{2,1,0:T(8,128)(2,1)S(1)}, bf16[7,96,128]{2,1,0:T(8,128)(2,1)S(1)}, u32[]{:S(2)}, u32[]{:S(2)}) %collective-permute-start.25) | collective-permute-done | bytes 172064 | tf_op jit(solution)/shard_map/ppermute | solution.py:251
  66.3 3.2 %collective-permute-start.16 = (bf16[6,96,128]{2,1,0:T(8,128)(2,1)S(1)}, bf16[6,96,128]{2,1,0:T(8,128)(2,1)S(1)}, u32[]{:S(2)}, u32[]{:S(2)}) collective-permute-start(bf16[6,96,128]{2,1,0:T(8,128)(2,1)S(1)} %get-tuple-element.77), channel_id=1, source_target_pairs={{0,8},{2,10},{4,12},{6,14},{8,0},{10,2},{12,4},{14,6},{1,9},{3,11}... | collective-permute-start | bytes 442376 | tf_op jit(solution)/shard_map/ppermute | solution.py:251
  69.5 3.4 %collective-permute-done.13.refs_11_.refs_12_ = bf16[16,96,128]{2,1,0:T(8,128)(2,1)S(1)} collective-permute-done((bf16[16,96,128]{2,1,0:T(8,128)(2,1)S(1)}, bf16[16,96,128]{2,1,0:T(8,128)(2,1)S(1)}, u32[]{:S(2)}, u32[]{:S(2)}) %collective-permute-start.13) | collective-permute-done | bytes 393248 | tf_op jit(solution)/shard_map/ppermute | solution.py:251
  72.9 1.6 %collective-permute-start.26 = (bf16[6,96,128]{2,1,0:T(8,128)(2,1)S(1)}, bf16[6,96,128]{2,1,0:T(8,128)(2,1)S(1)}, u32[]{:S(2)}, u32[]{:S(2)}) collective-permute-start(bf16[6,96,128]{2,1,0:T(8,128)(2,1)S(1)} %get-tuple-element.96), channel_id=1, source_target_pairs={{0,12},{2,14},{4,8},{6,10},{8,4},{10,6},{12,0},{14,2},{1,13},{3,15... | collective-permute-start | bytes 442376 | tf_op jit(solution)/shard_map/ppermute | solution.py:251
  74.5 2.9 %collective-permute-start.21 = (bf16[6,96,128]{2,1,0:T(8,128)(2,1)S(1)}, bf16[6,96,128]{2,1,0:T(8,128)(2,1)S(1)}, u32[]{:S(2)}, u32[]{:S(2)}) collective-permute-start(bf16[6,96,128]{2,1,0:T(8,128)(2,1)S(1)} %get-tuple-element.87), channel_id=1, source_target_pairs={{0,14},{2,12},{4,10},{6,8},{8,6},{10,4},{12,2},{14,0},{1,15},{3,13... | collective-permute-start | bytes 442376 | tf_op jit(solution)/shard_map/ppermute | solution.py:251
  77.5 0.6 ordered_metric.1.refs_0_.refs_1_
  78.1 2.1 %collective-permute-start.20 = (bf16[3,96,128]{2,1,0:T(8,128)(2,1)S(1)}, bf16[3,96,128]{2,1,0:T(8,128)(2,1)S(1)}, u32[]{:S(2)}, u32[]{:S(2)}) collective-permute-start(bf16[3,96,128]{2,1,0:T(8,128)(2,1)S(1)} %get-tuple-element.84), channel_id=1, source_target_pairs={{0,10},{2,8},{4,14},{6,12},{8,2},{10,0},{12,6},{14,4},{1,11},{3,9}... | collective-permute-start | bytes 221192 | tf_op jit(solution)/shard_map/ppermute | solution.py:251
  80.2 8.5 %collective-permute-done.16.refs_13_ = bf16[6,96,128]{2,1,0:T(8,128)(2,1)S(1)} collective-permute-done((bf16[6,96,128]{2,1,0:T(8,128)(2,1)S(1)}, bf16[6,96,128]{2,1,0:T(8,128)(2,1)S(1)}, u32[]{:S(2)}, u32[]{:S(2)}) %collective-permute-start.16) | collective-permute-done | bytes 147488 | tf_op jit(solution)/shard_map/ppermute | solution.py:251
  88.7 3.4 %collective-permute-start.23 = (bf16[3,96,128]{2,1,0:T(8,128)(2,1)S(1)}, bf16[3,96,128]{2,1,0:T(8,128)(2,1)S(1)}, u32[]{:S(2)}, u32[]{:S(2)}) collective-permute-start(bf16[3,96,128]{2,1,0:T(8,128)(2,1)S(1)} %get-tuple-element.90), channel_id=1, source_target_pairs={{0,14},{2,12},{4,10},{6,8},{8,6},{10,4},{12,2},{14,0},{1,15},{3,13... | collective-permute-start | bytes 221192 | tf_op jit(solution)/shard_map/ppermute | solution.py:251
  92.1 1.8 %group.3.refs_17_ = f32[256,256]{1,0:T(8,128)S(1)} custom-call(bf16[512,512]{1,0:T(8,128)(2,1)S(1)} %ordered_metric.1.refs_0_.refs_1_, bf16[16,32,128]{2,1,0:T(8,128)(2,1)S(1)} %get-tuple-element.54.refs_1_.refs_2_, bf16[16,32,128]{2,1,0:T(8,128)(2,1)S(1)} %collective-permute-done.5._.refs_2_.refs_3_, ...), custom_call_target="tpu_custom_call" | custom-call | flops 1409286144 | bytes 1835008 | tf_op jit(solution)/shard_map/group/pallas_call | solution.py:224
  94.0 1.6 %group.4.refs_18_ = f32[256,256]{1,0:T(8,128)S(1)} custom-call(bf16[512,512]{1,0:T(8,128)(2,1)S(1)} %ordered_metric.1.refs_0_.refs_1_, bf16[16,32,128]{2,1,0:T(8,128)(2,1)S(1)} %get-tuple-element.54.refs_1_.refs_2_, bf16[16,32,128]{2,1,0:T(8,128)(2,1)S(1)} %collective-permute-done.5._.refs_2_.refs_3_, ...), custom_call_target="tpu_custom_call" | custom-call | flops 1207959552 | bytes 1572864 | tf_op jit(solution)/shard_map/group/pallas_call | solution.py:224
  95.7 5.6 %collective-permute-done.20.refs_15_ = bf16[3,96,128]{2,1,0:T(8,128)(2,1)S(1)} collective-permute-done((bf16[3,96,128]{2,1,0:T(8,128)(2,1)S(1)}, bf16[3,96,128]{2,1,0:T(8,128)(2,1)S(1)}, u32[]{:S(2)}, u32[]{:S(2)}) %collective-permute-start.20) | collective-permute-done | bytes 73760 | tf_op jit(solution)/shard_map/ppermute | solution.py:251
  101.3 0.9 collective-permute-done.17.refs_14_
  102.2 1.0 group.5
  103.3 0.5 collective-permute-start.27
  103.8 0.7 collective-permute-done.28
  104.5 1.3 %collective-permute-start.29 = (f32[4,32,128]{2,1,0:T(8,128)S(1)}, f32[4,32,128]{2,1,0:T(8,128)S(1)}, u32[]{:S(2)}, u32[]{:S(2)}) collective-permute-start(f32[4,32,128]{2,1,0:T(8,128)S(1)} %add.31), channel_id=1, source_target_pairs={{0,2},{2,0},{4,6},{6,4},{8,10},{10,8},{12,14},{14,12},{1,3},{3,1},... | collective-permute-start | bytes 196616 | tf_op jit(solution)/shard_map/ppermute | solution.py:251
  105.9 3.0 %collective-permute-done.29 = f32[4,32,128]{2,1,0:T(8,128)S(1)} collective-permute-done((f32[4,32,128]{2,1,0:T(8,128)S(1)}, f32[4,32,128]{2,1,0:T(8,128)S(1)}, u32[]{:S(2)}, u32[]{:S(2)}) %collective-permute-start.29) | collective-permute-done | bytes 65568 | tf_op jit(solution)/shard_map/ppermute | solution.py:251
  108.9 2.9 %collective-permute-start.30 = (f32[32,128]{1,0:T(8,128)S(1)}, f32[32,128]{1,0:T(8,128)S(1)}, u32[]{:S(2)}, u32[]{:S(2)}) collective-permute-start(f32[32,128]{1,0:T(8,128)S(1)} %get-tuple-element.101), channel_id=1, source_target_pairs={{0,12},{2,14},{4,8},{6,10},{8,4},{10,6},{12,0},{14,2},{1,13},{3,15... | collective-permute-start | bytes 49160 | tf_op jit(solution)/shard_map/ppermute | solution.py:251
  111.8 1.4 %collective-permute-start.32 = (f32[32,128]{1,0:T(8,128)S(1)}, f32[32,128]{1,0:T(8,128)S(1)}, u32[]{:S(2)}, u32[]{:S(2)}) collective-permute-start(f32[32,128]{1,0:T(8,128)S(1)} %get-tuple-element.102), channel_id=1, source_target_pairs={{0,8},{2,10},{4,12},{6,14},{8,0},{10,2},{12,4},{14,6},{1,9},{3,11}... | collective-permute-start | bytes 49160 | tf_op jit(solution)/shard_map/ppermute | solution.py:251
  113.3 1.2 collective-permute-done.30
  114.5 2.0 %collective-permute-done.32 = f32[32,128]{1,0:T(8,128)S(1)} collective-permute-done((f32[32,128]{1,0:T(8,128)S(1)}, f32[32,128]{1,0:T(8,128)S(1)}, u32[]{:S(2)}, u32[]{:S(2)}) %collective-permute-start.32) | collective-permute-done | bytes 16416 | tf_op jit(solution)/shard_map/ppermute | solution.py:251
  116.5 0.5 collective-permute-done.31
  117.0 0.6 fusion.3
  (42 shorter events, 0.6 us)
Async XLA Ops:
  0.0 2.9 %copy-start = (bf16[128,512]{1,0:T(8,128)(2,1)S(1)}, bf16[128,512]{1,0:T(8,128)(2,1)}, u32[]{:S(2)}) copy-start(bf16[128,512]{1,0:T(8,128)(2,1)} %param.8) | copy-start | bytes 393220
  0.0 9.5 %copy-start.1 = (bf16[1024,128]{1,0:T(8,128)(2,1)S(1)}, bf16[1024,128]{1,0:T(8,128)(2,1)}, u32[]{:S(2)}) copy-start(bf16[1024,128]{1,0:T(8,128)(2,1)} %own_ref) | copy-start | bytes 786436
  0.0 9.5 %collective-permute-start.4 = (bf16[1024,128]{1,0:T(8,128)(2,1)}, bf16[1024,128]{1,0:T(8,128)(2,1)S(1)}, u32[]{:S(2)}, u32[]{:S(2)}) collective-permute-start(bf16[1024,128]{1,0:T(8,128)(2,1)} %own_ref), channel_id=1, source_target_pairs={{0,2},{2,0},{4,6},{6,4},{8,10},{10,8},{12,14},{14,12},{1,3},{3,1},... | collective-permute-start | bytes 786440 | tf_op jit(solution)/shard_map/ppermute | solution.py:251
  3.0 5.4 %collective-permute-start = (bf16[32,512]{1,0:T(8,128)(2,1)S(1)}, bf16[32,512]{1,0:T(8,128)(2,1)S(1)}, u32[]{:S(2)}, u32[]{:S(2)}) collective-permute-start(bf16[32,512]{1,0:T(8,128)(2,1)S(1)} %constant_dynamic-slice_fusion), channel_id=1, source_target_pairs={{0,8},{2,10},{4,12},{6,14},{8,0},{10,2},{12,4},{14,6},{1,9},{3,11}... | collective-permute-start | bytes 98312 | tf_op jit(solution)/shard_map/ppermute | solution.py:251
  8.3 69.1 %copy-start.2 = (s32[4]{0:T(128)S(1)}, s32[4]{0:T(128)}, u32[]{:S(2)}) copy-start(s32[4]{0:T(128)} %param.9) | copy-start | bytes 52
  10.3 8.1 %collective-permute-start.10 = (bf16[16,32,128]{2,1,0:T(8,128)(2,1)S(1)}, bf16[16,32,128]{2,1,0:T(8,128)(2,1)S(1)}, u32[]{:S(2)}, u32[]{:S(2)}) collective-permute-start(bf16[16,32,128]{2,1,0:T(8,128)(2,1)S(1)} %get-tuple-element.64), channel_id=1, source_target_pairs={{0,12},{2,14},{4,8},{6,10},{8,4},{10,6},{12,0},{14,2},{1,13},{3,15... | collective-permute-start | bytes 393224 | tf_op jit(solution)/shard_map/ppermute | solution.py:251
  14.2 9.3 %collective-permute-start.5 = (bf16[16,32,128]{2,1,0:T(8,128)(2,1)S(1)}, bf16[16,32,128]{2,1,0:T(8,128)(2,1)S(1)}, u32[]{:S(2)}, u32[]{:S(2)}) collective-permute-start(bf16[16,32,128]{2,1,0:T(8,128)(2,1)S(1)} %get-tuple-element.55), channel_id=1, source_target_pairs={{0,2},{2,0},{4,6},{6,4},{8,10},{10,8},{12,14},{14,12},{1,3},{3,1},... | collective-permute-start | bytes 393224 | tf_op jit(solution)/shard_map/ppermute | solution.py:251
  15.7 16.2 %collective-permute-start.7 = (bf16[16,32,128]{2,1,0:T(8,128)(2,1)S(1)}, bf16[16,32,128]{2,1,0:T(8,128)(2,1)S(1)}, u32[]{:S(2)}, u32[]{:S(2)}) collective-permute-start(bf16[16,32,128]{2,1,0:T(8,128)(2,1)S(1)} %get-tuple-element.61), channel_id=1, source_target_pairs={{0,6},{2,4},{4,2},{6,0},{8,14},{10,12},{12,10},{14,8},{1,7},{3,5},... | collective-permute-start | bytes 393224 | tf_op jit(solution)/shard_map/ppermute | solution.py:251
  15.7 16.2 %collective-permute-start.9 = (bf16[16,32,128]{2,1,0:T(8,128)(2,1)S(1)}, bf16[16,32,128]{2,1,0:T(8,128)(2,1)S(1)}, u32[]{:S(2)}, u32[]{:S(2)}) collective-permute-start(bf16[16,32,128]{2,1,0:T(8,128)(2,1)S(1)} %get-tuple-element.63), channel_id=1, source_target_pairs={{0,10},{2,8},{4,14},{6,12},{8,2},{10,0},{12,6},{14,4},{1,11},{3,9}... | collective-permute-start | bytes 393224 | tf_op jit(solution)/shard_map/ppermute | solution.py:251
  17.4 18.7 %collective-permute-start.1 = (bf16[64,512]{1,0:T(8,128)(2,1)S(1)}, bf16[64,512]{1,0:T(8,128)(2,1)S(1)}, u32[]{:S(2)}, u32[]{:S(2)}) collective-permute-start(bf16[64,512]{1,0:T(8,128)(2,1)S(1)} %pad_maximum_fusion.2), channel_id=1, source_target_pairs={{0,4},{2,6},{4,0},{6,2},{8,12},{10,14},{12,8},{14,10},{1,5},{3,7},... | collective-permute-start | bytes 196616 | tf_op jit(solution)/shard_map/ppermute | solution.py:251
  18.4 19.3 %collective-permute-start.8 = (bf16[16,32,128]{2,1,0:T(8,128)(2,1)S(1)}, bf16[16,32,128]{2,1,0:T(8,128)(2,1)S(1)}, u32[]{:S(2)}, u32[]{:S(2)}) collective-permute-start(bf16[16,32,128]{2,1,0:T(8,128)(2,1)S(1)} %get-tuple-element.62), channel_id=1, source_target_pairs={{0,8},{2,10},{4,12},{6,14},{8,0},{10,2},{12,4},{14,6},{1,9},{3,11}... | collective-permute-start | bytes 393224 | tf_op jit(solution)/shard_map/ppermute | solution.py:251
  23.5 15.3 %collective-permute-start.11 = (bf16[16,32,128]{2,1,0:T(8,128)(2,1)S(1)}, bf16[16,32,128]{2,1,0:T(8,128)(2,1)S(1)}, u32[]{:S(2)}, u32[]{:S(2)}) collective-permute-start(bf16[16,32,128]{2,1,0:T(8,128)(2,1)S(1)} %get-tuple-element.66), channel_id=1, source_target_pairs={{0,14},{2,12},{4,10},{6,8},{8,6},{10,4},{12,2},{14,0},{1,15},{3,13... | collective-permute-start | bytes 393224 | tf_op jit(solution)/shard_map/ppermute | solution.py:251
  31.9 7.8 %collective-permute-start.6 = (bf16[16,32,128]{2,1,0:T(8,128)(2,1)S(1)}, bf16[16,32,128]{2,1,0:T(8,128)(2,1)S(1)}, u32[]{:S(2)}, u32[]{:S(2)}) collective-permute-start(bf16[16,32,128]{2,1,0:T(8,128)(2,1)S(1)} %get-tuple-element.60), channel_id=1, source_target_pairs={{0,4},{2,6},{4,0},{6,2},{8,12},{10,14},{12,8},{14,10},{1,5},{3,7},... | collective-permute-start | bytes 393224 | tf_op jit(solution)/shard_map/ppermute | solution.py:251
  32.2 19.4 %collective-permute-start.14 = (bf16[7,96,128]{2,1,0:T(8,128)(2,1)S(1)}, bf16[7,96,128]{2,1,0:T(8,128)(2,1)S(1)}, u32[]{:S(2)}, u32[]{:S(2)}) collective-permute-start(bf16[7,96,128]{2,1,0:T(8,128)(2,1)S(1)} %get-tuple-element.73), channel_id=1, source_target_pairs={{0,8},{2,10},{4,12},{6,14},{8,0},{10,2},{12,4},{14,6},{1,9},{3,11}... | collective-permute-start | bytes 516104 | tf_op jit(solution)/shard_map/ppermute | solution.py:251
  36.0 19.8 %collective-permute-start.24 = (bf16[7,96,128]{2,1,0:T(8,128)(2,1)S(1)}, bf16[7,96,128]{2,1,0:T(8,128)(2,1)S(1)}, u32[]{:S(2)}, u32[]{:S(2)}) collective-permute-start(bf16[7,96,128]{2,1,0:T(8,128)(2,1)S(1)} %get-tuple-element.94), channel_id=1, source_target_pairs={{0,10},{2,8},{4,14},{6,12},{8,2},{10,0},{12,6},{14,4},{1,11},{3,9}... | collective-permute-start | bytes 516104 | tf_op jit(solution)/shard_map/ppermute | solution.py:251
  37.7 21.6 %collective-permute-start.2 = (bf16[128,512]{1,0:T(8,128)(2,1)S(1)}, bf16[128,512]{1,0:T(8,128)(2,1)S(1)}, u32[]{:S(2)}, u32[]{:S(2)}) collective-permute-start(bf16[128,512]{1,0:T(8,128)(2,1)S(1)} %pad_maximum_fusion.1), channel_id=1, source_target_pairs={{0,2},{2,0},{4,6},{6,4},{8,10},{10,8},{12,14},{14,12},{1,3},{3,1},... | collective-permute-start | bytes 393224 | tf_op jit(solution)/shard_map/ppermute | solution.py:251
  38.8 20.6 %collective-permute-start.12 = (bf16[16,96,128]{2,1,0:T(8,128)(2,1)S(1)}, bf16[16,96,128]{2,1,0:T(8,128)(2,1)S(1)}, u32[]{:S(2)}, u32[]{:S(2)}) collective-permute-start(bf16[16,96,128]{2,1,0:T(8,128)(2,1)S(1)} %get-tuple-element.69), channel_id=1, source_target_pairs={{0,2},{2,0},{4,6},{6,4},{8,10},{10,8},{12,14},{14,12},{1,3},{3,1},... | collective-permute-start | bytes 1179656 | tf_op jit(solution)/shard_map/ppermute | solution.py:251
  39.7 19.6 %collective-permute-start.18 = (bf16[7,96,128]{2,1,0:T(8,128)(2,1)S(1)}, bf16[7,96,128]{2,1,0:T(8,128)(2,1)S(1)}, u32[]{:S(2)}, u32[]{:S(2)}) collective-permute-start(bf16[7,96,128]{2,1,0:T(8,128)(2,1)S(1)} %get-tuple-element.82), channel_id=1, source_target_pairs={{0,12},{2,14},{4,8},{6,10},{8,4},{10,6},{12,0},{14,2},{1,13},{3,15... | collective-permute-start | bytes 516104 | tf_op jit(solution)/shard_map/ppermute | solution.py:251
  51.6 21.2 %collective-permute-start.13 = (bf16[16,96,128]{2,1,0:T(8,128)(2,1)S(1)}, bf16[16,96,128]{2,1,0:T(8,128)(2,1)S(1)}, u32[]{:S(2)}, u32[]{:S(2)}) collective-permute-start(bf16[16,96,128]{2,1,0:T(8,128)(2,1)S(1)} %get-tuple-element.71), channel_id=1, source_target_pairs={{0,4},{2,6},{4,0},{6,2},{8,12},{10,14},{12,8},{14,10},{1,5},{3,7},... | collective-permute-start | bytes 1179656 | tf_op jit(solution)/shard_map/ppermute | solution.py:251
  55.8 10.4 %collective-permute-start.25 = (bf16[7,96,128]{2,1,0:T(8,128)(2,1)S(1)}, bf16[7,96,128]{2,1,0:T(8,128)(2,1)S(1)}, u32[]{:S(2)}, u32[]{:S(2)}) collective-permute-start(bf16[7,96,128]{2,1,0:T(8,128)(2,1)S(1)} %get-tuple-element.95), channel_id=1, source_target_pairs={{0,14},{2,12},{4,10},{6,8},{8,6},{10,4},{12,2},{14,0},{1,15},{3,13... | collective-permute-start | bytes 516104 | tf_op jit(solution)/shard_map/ppermute | solution.py:251
  59.3 29.4 %collective-permute-start.15 = (bf16[16,96,128]{2,1,0:T(8,128)(2,1)S(1)}, bf16[16,96,128]{2,1,0:T(8,128)(2,1)S(1)}, u32[]{:S(2)}, u32[]{:S(2)}) collective-permute-start(bf16[16,96,128]{2,1,0:T(8,128)(2,1)S(1)} %get-tuple-element.74), channel_id=1, source_target_pairs={{0,6},{2,4},{4,2},{6,0},{8,14},{10,12},{12,10},{14,8},{1,7},{3,5},... | collective-permute-start | bytes 1179656 | tf_op jit(solution)/shard_map/ppermute | solution.py:251
  59.3 15.1 %collective-permute-start.3 = (bf16[256,512]{1,0:T(8,128)(2,1)S(1)}, bf16[256,512]{1,0:T(8,128)(2,1)S(1)}, u32[]{:S(2)}, u32[]{:S(2)}) collective-permute-start(bf16[256,512]{1,0:T(8,128)(2,1)S(1)} %pad_maximum_fusion.refs_0_), channel_id=1, source_target_pairs={{0,1},{1,0},{2,3},{3,2},{4,5},{5,4},{6,7},{7,6},{8,9},{9,8},{10,11... | collective-permute-start | bytes 786440 | tf_op jit(solution)/shard_map/ppermute | solution.py:254
  59.4 18.7 %collective-permute-start.19 = (bf16[6,96,128]{2,1,0:T(8,128)(2,1)S(1)}, bf16[6,96,128]{2,1,0:T(8,128)(2,1)S(1)}, u32[]{:S(2)}, u32[]{:S(2)}) collective-permute-start(bf16[6,96,128]{2,1,0:T(8,128)(2,1)S(1)} %get-tuple-element.83), channel_id=1, source_target_pairs={{0,10},{2,8},{4,14},{6,12},{8,2},{10,0},{12,6},{14,4},{1,11},{3,9}... | collective-permute-start | bytes 442376 | tf_op jit(solution)/shard_map/ppermute | solution.py:251
  66.3 22.5 %collective-permute-start.16 = (bf16[6,96,128]{2,1,0:T(8,128)(2,1)S(1)}, bf16[6,96,128]{2,1,0:T(8,128)(2,1)S(1)}, u32[]{:S(2)}, u32[]{:S(2)}) collective-permute-start(bf16[6,96,128]{2,1,0:T(8,128)(2,1)S(1)} %get-tuple-element.77), channel_id=1, source_target_pairs={{0,8},{2,10},{4,12},{6,14},{8,0},{10,2},{12,4},{14,6},{1,9},{3,11}... | collective-permute-start | bytes 442376 | tf_op jit(solution)/shard_map/ppermute | solution.py:251
  72.9 21.1 %collective-permute-start.26 = (bf16[6,96,128]{2,1,0:T(8,128)(2,1)S(1)}, bf16[6,96,128]{2,1,0:T(8,128)(2,1)S(1)}, u32[]{:S(2)}, u32[]{:S(2)}) collective-permute-start(bf16[6,96,128]{2,1,0:T(8,128)(2,1)S(1)} %get-tuple-element.96), channel_id=1, source_target_pairs={{0,12},{2,14},{4,8},{6,10},{8,4},{10,6},{12,0},{14,2},{1,13},{3,15... | collective-permute-start | bytes 442376 | tf_op jit(solution)/shard_map/ppermute | solution.py:251
  74.5 19.5 %collective-permute-start.21 = (bf16[6,96,128]{2,1,0:T(8,128)(2,1)S(1)}, bf16[6,96,128]{2,1,0:T(8,128)(2,1)S(1)}, u32[]{:S(2)}, u32[]{:S(2)}) collective-permute-start(bf16[6,96,128]{2,1,0:T(8,128)(2,1)S(1)} %get-tuple-element.87), channel_id=1, source_target_pairs={{0,14},{2,12},{4,10},{6,8},{8,6},{10,4},{12,2},{14,0},{1,15},{3,13... | collective-permute-start | bytes 442376 | tf_op jit(solution)/shard_map/ppermute | solution.py:251
  78.1 23.2 %collective-permute-start.20 = (bf16[3,96,128]{2,1,0:T(8,128)(2,1)S(1)}, bf16[3,96,128]{2,1,0:T(8,128)(2,1)S(1)}, u32[]{:S(2)}, u32[]{:S(2)}) collective-permute-start(bf16[3,96,128]{2,1,0:T(8,128)(2,1)S(1)} %get-tuple-element.84), channel_id=1, source_target_pairs={{0,10},{2,8},{4,14},{6,12},{8,2},{10,0},{12,6},{14,4},{1,11},{3,9}... | collective-permute-start | bytes 221192 | tf_op jit(solution)/shard_map/ppermute | solution.py:251
  88.7 13.4 %collective-permute-start.17 = (bf16[3,96,128]{2,1,0:T(8,128)(2,1)S(1)}, bf16[3,96,128]{2,1,0:T(8,128)(2,1)S(1)}, u32[]{:S(2)}, u32[]{:S(2)}) collective-permute-start(bf16[3,96,128]{2,1,0:T(8,128)(2,1)S(1)} %get-tuple-element.78), channel_id=1, source_target_pairs={{0,8},{2,10},{4,12},{6,14},{8,0},{10,2},{12,4},{14,6},{1,9},{3,11}... | collective-permute-start | bytes 221192 | tf_op jit(solution)/shard_map/ppermute | solution.py:251
  88.7 13.4 %collective-permute-start.23 = (bf16[3,96,128]{2,1,0:T(8,128)(2,1)S(1)}, bf16[3,96,128]{2,1,0:T(8,128)(2,1)S(1)}, u32[]{:S(2)}, u32[]{:S(2)}) collective-permute-start(bf16[3,96,128]{2,1,0:T(8,128)(2,1)S(1)} %get-tuple-element.90), channel_id=1, source_target_pairs={{0,14},{2,12},{4,10},{6,8},{8,6},{10,4},{12,2},{14,0},{1,15},{3,13... | collective-permute-start | bytes 221192 | tf_op jit(solution)/shard_map/ppermute | solution.py:251
  93.9 8.2 %collective-permute-start.22 = (bf16[3,96,128]{2,1,0:T(8,128)(2,1)S(1)}, bf16[3,96,128]{2,1,0:T(8,128)(2,1)S(1)}, u32[]{:S(2)}, u32[]{:S(2)}) collective-permute-start(bf16[3,96,128]{2,1,0:T(8,128)(2,1)S(1)} %get-tuple-element.88), channel_id=1, source_target_pairs={{0,12},{2,14},{4,8},{6,10},{8,4},{10,6},{12,0},{14,2},{1,13},{3,15... | collective-permute-start | bytes 221192 | tf_op jit(solution)/shard_map/ppermute | solution.py:251
  103.2 1.3 %collective-permute-start.28 = (f32[4,32,128]{2,1,0:T(8,128)S(1)}, f32[4,32,128]{2,1,0:T(8,128)S(1)}, u32[]{:S(2)}, u32[]{:S(2)}) collective-permute-start(f32[4,32,128]{2,1,0:T(8,128)S(1)} %get-tuple-element.100), channel_id=1, source_target_pairs={{0,1},{1,0},{2,3},{3,2},{4,5},{5,4},{6,7},{7,6},{8,9},{9,8},{10,11... | collective-permute-start | bytes 196616 | tf_op jit(solution)/shard_map/ppermute | solution.py:254
  103.3 2.6 %collective-permute-start.27 = (f32[4,32,128]{2,1,0:T(8,128)S(1)}, f32[4,32,128]{2,1,0:T(8,128)S(1)}, u32[]{:S(2)}, u32[]{:S(2)}) collective-permute-start(f32[4,32,128]{2,1,0:T(8,128)S(1)} %get-tuple-element.98), channel_id=1, source_target_pairs={{0,1},{1,0},{2,3},{3,2},{4,5},{5,4},{6,7},{7,6},{8,9},{9,8},{10,11... | collective-permute-start | bytes 196616 | tf_op jit(solution)/shard_map/ppermute | solution.py:254
  104.5 4.3 %collective-permute-start.29 = (f32[4,32,128]{2,1,0:T(8,128)S(1)}, f32[4,32,128]{2,1,0:T(8,128)S(1)}, u32[]{:S(2)}, u32[]{:S(2)}) collective-permute-start(f32[4,32,128]{2,1,0:T(8,128)S(1)} %add.31), channel_id=1, source_target_pairs={{0,2},{2,0},{4,6},{6,4},{8,10},{10,8},{12,14},{14,12},{1,3},{3,1},... | collective-permute-start | bytes 196616 | tf_op jit(solution)/shard_map/ppermute | solution.py:251
  108.9 5.6 %collective-permute-start.30 = (f32[32,128]{1,0:T(8,128)S(1)}, f32[32,128]{1,0:T(8,128)S(1)}, u32[]{:S(2)}, u32[]{:S(2)}) collective-permute-start(f32[32,128]{1,0:T(8,128)S(1)} %get-tuple-element.101), channel_id=1, source_target_pairs={{0,12},{2,14},{4,8},{6,10},{8,4},{10,6},{12,0},{14,2},{1,13},{3,15... | collective-permute-start | bytes 49160 | tf_op jit(solution)/shard_map/ppermute | solution.py:251
  111.8 4.6 %collective-permute-start.32 = (f32[32,128]{1,0:T(8,128)S(1)}, f32[32,128]{1,0:T(8,128)S(1)}, u32[]{:S(2)}, u32[]{:S(2)}) collective-permute-start(f32[32,128]{1,0:T(8,128)S(1)} %get-tuple-element.102), channel_id=1, source_target_pairs={{0,8},{2,10},{4,12},{6,14},{8,0},{10,2},{12,4},{14,6},{1,9},{3,11}... | collective-permute-start | bytes 49160 | tf_op jit(solution)/shard_map/ppermute | solution.py:251
  113.3 3.7 %collective-permute-start.31 = (f32[32,128]{1,0:T(8,128)S(1)}, f32[32,128]{1,0:T(8,128)S(1)}, u32[]{:S(2)}, u32[]{:S(2)}) collective-permute-start(f32[32,128]{1,0:T(8,128)S(1)} %get-tuple-element.103), channel_id=1, source_target_pairs={{0,4},{2,6},{4,0},{6,2},{8,12},{10,14},{12,8},{14,10},{1,5},{3,7},... | collective-permute-start | bytes 49160 | tf_op jit(solution)/shard_map/ppermute | solution.py:251

commit v7 on v6

--- a/solution.py
+++ b/solution.py
@@ -70,10 +70,10 @@
         name = where[0, 2 + s]
         away = lax.div(name, held) != where[0, 1]
         start = pl.multiple_of(lax.rem(name, held) * block, block)
-        mine = own_ref[pl.ds(start, block), :].astype(F32)
-        theirs = other_ref[pl.ds(start, block), :].astype(F32)
+        mine = own_ref[pl.ds(start, block), :]
+        theirs = other_ref[pl.ds(start, block), :]
         picked = jnp.where(away, theirs, mine)
-        plain[:, s * block : (s + 1) * block] = picked.T.astype(BF16)
+        plain[:, s * block : (s + 1) * block] = picked.T
     me = where[0, 0]
     for k in range(chips):
         start = pl.multiple_of((me ^ k) * share, share)

time: 118 us -> 118 us (level)
  no operation moved by 1% of the time
where the time goes in v7:
time: 118 us
  starting transfers between devices  61.6 us (52%)
  waiting for transfers between devices  39.2 us (33%)
  Pallas kernels  14.9 us (13%)
  other arithmetic  1.55 us (1%)
    ppermute x30, starting transfers between devices, swap(): return lax.ppermute(value, ('aux', 'bas'), pairs)  61 us
    ppermute x30, waiting for transfers between devices, swap(): return lax.ppermute(value, ('aux', 'bas'), pairs)  38.5 us
    pallas_call x1, Pallas kernels, rest_products(): pl.pallas_call(functools.partial(rest_kernel, chips, spans), grid=(rest /...  7.04 us
    pallas_call x3, Pallas kernels, group(): pl.pallas_call(functools.partial(group_kernel, aux, bas, lo, hi, starts,...  4.48 us
  transfers between devices with their start and end apart: 33, of which 15 were waited for; matrix products, arithmetic and copies ran while one was open for 1% of the time, Pallas kernels for 11%

profile of v7, /device:TPU:0, one launch (start us, length us, event | category | flops | bytes accessed | tf_op | source)
XLA Modules:
  0.0 117.6 jit_solution(11915902620685203359)
XLA Ops:
  0.0 2.9 %collective-permute-start.4 = (bf16[1024,128]{1,0:T(8,128)(2,1)}, bf16[1024,128]{1,0:T(8,128)(2,1)S(1)}, u32[]{:S(2)}, u32[]{:S(2)}) collective-permute-start(bf16[1024,128]{1,0:T(8,128)(2,1)} %own_ref), channel_id=1, source_target_pairs={{0,2},{2,0},{4,6},{6,4},{8,10},{10,8},{12,14},{14,12},{1,3},{3,1},... | collective-permute-start | bytes 786440 | tf_op jit(solution)/shard_map/ppermute | solution.py:251
  3.0 2.6 %collective-permute-start = (bf16[32,512]{1,0:T(8,128)(2,1)S(1)}, bf16[32,512]{1,0:T(8,128)(2,1)S(1)}, u32[]{:S(2)}, u32[]{:S(2)}) collective-permute-start(bf16[32,512]{1,0:T(8,128)(2,1)S(1)} %constant_dynamic-slice_fusion), channel_id=1, source_target_pairs={{0,8},{2,10},{4,12},{6,14},{8,0},{10,2},{12,4},{14,6},{1,9},{3,11}... | collective-permute-start | bytes 98312 | tf_op jit(solution)/shard_map/ppermute | solution.py:251
  5.5 0.7 add_bitcast_fusion.1.where
  6.3 2.0 %relayout.1.x_ref = bf16[32,256,128]{2,1,0:T(8,128)(2,1)S(1)} custom-call(bf16[2,128,128,128]{3,2,1,0:T(8,128)(2,1)} %bitcast.28), custom_call_target="tpu_custom_call" | custom-call | bytes 4194304 | tf_op jit(solution)/shard_map/relayout/pallas_call | solution.py:42
  8.3 1.2 collective-permute-done.4.other_ref
  9.5 0.8 first_products.1
  10.3 3.9 %collective-permute-start.10 = (bf16[16,32,128]{2,1,0:T(8,128)(2,1)S(1)}, bf16[16,32,128]{2,1,0:T(8,128)(2,1)S(1)}, u32[]{:S(2)}, u32[]{:S(2)}) collective-permute-start(bf16[16,32,128]{2,1,0:T(8,128)(2,1)S(1)} %get-tuple-element.64), channel_id=1, source_target_pairs={{0,12},{2,14},{4,8},{6,10},{8,4},{10,6},{12,0},{14,2},{1,13},{3,15... | collective-permute-start | bytes 393224 | tf_op jit(solution)/shard_map/ppermute | solution.py:251
  14.2 1.5 %collective-permute-start.5 = (bf16[16,32,128]{2,1,0:T(8,128)(2,1)S(1)}, bf16[16,32,128]{2,1,0:T(8,128)(2,1)S(1)}, u32[]{:S(2)}, u32[]{:S(2)}) collective-permute-start(bf16[16,32,128]{2,1,0:T(8,128)(2,1)S(1)} %get-tuple-element.55), channel_id=1, source_target_pairs={{0,2},{2,0},{4,6},{6,4},{8,10},{10,8},{12,14},{14,12},{1,3},{3,1},... | collective-permute-start | bytes 393224 | tf_op jit(solution)/shard_map/ppermute | solution.py:251
  15.7 1.7 %collective-permute-start.9 = (bf16[16,32,128]{2,1,0:T(8,128)(2,1)S(1)}, bf16[16,32,128]{2,1,0:T(8,128)(2,1)S(1)}, u32[]{:S(2)}, u32[]{:S(2)}) collective-permute-start(bf16[16,32,128]{2,1,0:T(8,128)(2,1)S(1)} %get-tuple-element.63), channel_id=1, source_target_pairs={{0,10},{2,8},{4,14},{6,12},{8,2},{10,0},{12,6},{14,4},{1,11},{3,9}... | collective-permute-start | bytes 393224 | tf_op jit(solution)/shard_map/ppermute | solution.py:251
  17.3 0.7 collective-permute-start.1
  18.0 0.3 collective-permute-done.10.refs_7_.refs_8_
  18.3 5.2 %collective-permute-start.8 = (bf16[16,32,128]{2,1,0:T(8,128)(2,1)S(1)}, bf16[16,32,128]{2,1,0:T(8,128)(2,1)S(1)}, u32[]{:S(2)}, u32[]{:S(2)}) collective-permute-start(bf16[16,32,128]{2,1,0:T(8,128)(2,1)S(1)} %get-tuple-element.62), channel_id=1, source_target_pairs={{0,8},{2,10},{4,12},{6,14},{8,0},{10,2},{12,4},{14,6},{1,9},{3,11}... | collective-permute-start | bytes 393224 | tf_op jit(solution)/shard_map/ppermute | solution.py:251
  23.5 1.3 %collective-permute-start.11 = (bf16[16,32,128]{2,1,0:T(8,128)(2,1)S(1)}, bf16[16,32,128]{2,1,0:T(8,128)(2,1)S(1)}, u32[]{:S(2)}, u32[]{:S(2)}) collective-permute-start(bf16[16,32,128]{2,1,0:T(8,128)(2,1)S(1)} %get-tuple-element.66), channel_id=1, source_target_pairs={{0,14},{2,12},{4,10},{6,8},{8,6},{10,4},{12,2},{14,0},{1,15},{3,13... | collective-permute-start | bytes 393224 | tf_op jit(solution)/shard_map/ppermute | solution.py:251
  24.8 7.0 %rest_products.1 = (bf16[7,96,128]{2,1,0:T(8,128)(2,1)S(1)}, bf16[7,96,128]{2,1,0:T(8,128)(2,1)S(1)}, bf16[7,96,128]{2,1,0:T(8,128)(2,1)S(1)}, bf16[7,96,128]{2,...) custom-call(bf16[2,128,128,128]{3,2,1,0:T(8,128)(2,1)} %bitcast.29, ...), custom_call_target="tpu_custom_call" | custom-call | flops 805306368 | bytes 8388608 | tf_op jit(solution)/shard_map/rest_products/pallas_call | solution.py:119
  31.8 0.3 collective-permute-start.6
  32.2 3.8 %collective-permute-start.14 = (bf16[7,96,128]{2,1,0:T(8,128)(2,1)S(1)}, bf16[7,96,128]{2,1,0:T(8,128)(2,1)S(1)}, u32[]{:S(2)}, u32[]{:S(2)}) collective-permute-start(bf16[7,96,128]{2,1,0:T(8,128)(2,1)S(1)} %get-tuple-element.73), channel_id=1, source_target_pairs={{0,8},{2,10},{4,12},{6,14},{8,0},{10,2},{12,4},{14,6},{1,9},{3,11}... | collective-permute-start | bytes 516104 | tf_op jit(solution)/shard_map/ppermute | solution.py:251
  36.0 1.6 %collective-permute-done.8.refs_5_.refs_6_ = bf16[16,32,128]{2,1,0:T(8,128)(2,1)S(1)} collective-permute-done((bf16[16,32,128]{2,1,0:T(8,128)(2,1)S(1)}, bf16[16,32,128]{2,1,0:T(8,128)(2,1)S(1)}, u32[]{:S(2)}, u32[]{:S(2)}) %collective-permute-start.8) | collective-permute-done | bytes 131104 | tf_op jit(solution)/shard_map/ppermute | solution.py:251
  37.6 1.1 collective-permute-start.2
  38.7 0.9 collective-permute-start.12
  39.7 8.2 %collective-permute-start.18 = (bf16[7,96,128]{2,1,0:T(8,128)(2,1)S(1)}, bf16[7,96,128]{2,1,0:T(8,128)(2,1)S(1)}, u32[]{:S(2)}, u32[]{:S(2)}) collective-permute-start(bf16[7,96,128]{2,1,0:T(8,128)(2,1)S(1)} %get-tuple-element.82), channel_id=1, source_target_pairs={{0,12},{2,14},{4,8},{6,10},{8,4},{10,6},{12,0},{14,2},{1,13},{3,15... | collective-permute-start | bytes 516104 | tf_op jit(solution)/shard_map/ppermute | solution.py:251
  47.9 3.7 %collective-permute-done.14.refs_13_ = bf16[7,96,128]{2,1,0:T(8,128)(2,1)S(1)} collective-permute-done((bf16[7,96,128]{2,1,0:T(8,128)(2,1)S(1)}, bf16[7,96,128]{2,1,0:T(8,128)(2,1)S(1)}, u32[]{:S(2)}, u32[]{:S(2)}) %collective-permute-start.14) | collective-permute-done | bytes 172064 | tf_op jit(solution)/shard_map/ppermute | solution.py:251
  51.6 4.2 %collective-permute-done.24.refs_14_ = bf16[7,96,128]{2,1,0:T(8,128)(2,1)S(1)} collective-permute-done((bf16[7,96,128]{2,1,0:T(8,128)(2,1)S(1)}, bf16[7,96,128]{2,1,0:T(8,128)(2,1)S(1)}, u32[]{:S(2)}, u32[]{:S(2)}) %collective-permute-start.24) | collective-permute-done | bytes 172064 | tf_op jit(solution)/shard_map/ppermute | solution.py:251
  55.8 3.4 %collective-permute-start.25 = (bf16[7,96,128]{2,1,0:T(8,128)(2,1)S(1)}, bf16[7,96,128]{2,1,0:T(8,128)(2,1)S(1)}, u32[]{:S(2)}, u32[]{:S(2)}) collective-permute-start(bf16[7,96,128]{2,1,0:T(8,128)(2,1)S(1)} %get-tuple-element.95), channel_id=1, source_target_pairs={{0,14},{2,12},{4,10},{6,8},{8,6},{10,4},{12,2},{14,0},{1,15},{3,13... | collective-permute-start | bytes 516104 | tf_op jit(solution)/shard_map/ppermute | solution.py:251
  59.4 4.6 %collective-permute-start.19 = (bf16[6,96,128]{2,1,0:T(8,128)(2,1)S(1)}, bf16[6,96,128]{2,1,0:T(8,128)(2,1)S(1)}, u32[]{:S(2)}, u32[]{:S(2)}) collective-permute-start(bf16[6,96,128]{2,1,0:T(8,128)(2,1)S(1)} %get-tuple-element.83), channel_id=1, source_target_pairs={{0,10},{2,8},{4,14},{6,12},{8,2},{10,0},{12,6},{14,4},{1,11},{3,9}... | collective-permute-start | bytes 442376 | tf_op jit(solution)/shard_map/ppermute | solution.py:251
  63.9 2.3 %collective-permute-done.25.refs_16_ = bf16[7,96,128]{2,1,0:T(8,128)(2,1)S(1)} collective-permute-done((bf16[7,96,128]{2,1,0:T(8,128)(2,1)S(1)}, bf16[7,96,128]{2,1,0:T(8,128)(2,1)S(1)}, u32[]{:S(2)}, u32[]{:S(2)}) %collective-permute-start.25) | collective-permute-done | bytes 172064 | tf_op jit(solution)/shard_map/ppermute | solution.py:251
  66.2 3.1 %collective-permute-start.16 = (bf16[6,96,128]{2,1,0:T(8,128)(2,1)S(1)}, bf16[6,96,128]{2,1,0:T(8,128)(2,1)S(1)}, u32[]{:S(2)}, u32[]{:S(2)}) collective-permute-start(bf16[6,96,128]{2,1,0:T(8,128)(2,1)S(1)} %get-tuple-element.77), channel_id=1, source_target_pairs={{0,8},{2,10},{4,12},{6,14},{8,0},{10,2},{12,4},{14,6},{1,9},{3,11}... | collective-permute-start | bytes 442376 | tf_op jit(solution)/shard_map/ppermute | solution.py:251
  69.4 3.4 %collective-permute-done.13.refs_11_.refs_12_ = bf16[16,96,128]{2,1,0:T(8,128)(2,1)S(1)} collective-permute-done((bf16[16,96,128]{2,1,0:T(8,128)(2,1)S(1)}, bf16[16,96,128]{2,1,0:T(8,128)(2,1)S(1)}, u32[]{:S(2)}, u32[]{:S(2)}) %collective-permute-start.13) | collective-permute-done | bytes 393248 | tf_op jit(solution)/shard_map/ppermute | solution.py:251
  72.9 1.5 %collective-permute-start.26 = (bf16[6,96,128]{2,1,0:T(8,128)(2,1)S(1)}, bf16[6,96,128]{2,1,0:T(8,128)(2,1)S(1)}, u32[]{:S(2)}, u32[]{:S(2)}) collective-permute-start(bf16[6,96,128]{2,1,0:T(8,128)(2,1)S(1)} %get-tuple-element.96), channel_id=1, source_target_pairs={{0,12},{2,14},{4,8},{6,10},{8,4},{10,6},{12,0},{14,2},{1,13},{3,15... | collective-permute-start | bytes 442376 | tf_op jit(solution)/shard_map/ppermute | solution.py:251
  74.4 3.0 %collective-permute-start.21 = (bf16[6,96,128]{2,1,0:T(8,128)(2,1)S(1)}, bf16[6,96,128]{2,1,0:T(8,128)(2,1)S(1)}, u32[]{:S(2)}, u32[]{:S(2)}) collective-permute-start(bf16[6,96,128]{2,1,0:T(8,128)(2,1)S(1)} %get-tuple-element.87), channel_id=1, source_target_pairs={{0,14},{2,12},{4,10},{6,8},{8,6},{10,4},{12,2},{14,0},{1,15},{3,13... | collective-permute-start | bytes 442376 | tf_op jit(solution)/shard_map/ppermute | solution.py:251
  77.5 0.6 ordered_metric.1.refs_0_.refs_1_
  78.1 2.2 %collective-permute-start.20 = (bf16[3,96,128]{2,1,0:T(8,128)(2,1)S(1)}, bf16[3,96,128]{2,1,0:T(8,128)(2,1)S(1)}, u32[]{:S(2)}, u32[]{:S(2)}) collective-permute-start(bf16[3,96,128]{2,1,0:T(8,128)(2,1)S(1)} %get-tuple-element.84), channel_id=1, source_target_pairs={{0,10},{2,8},{4,14},{6,12},{8,2},{10,0},{12,6},{14,4},{1,11},{3,9}... | collective-permute-start | bytes 221192 | tf_op jit(solution)/shard_map/ppermute | solution.py:251
  80.3 8.4 %collective-permute-done.16.refs_13_ = bf16[6,96,128]{2,1,0:T(8,128)(2,1)S(1)} collective-permute-done((bf16[6,96,128]{2,1,0:T(8,128)(2,1)S(1)}, bf16[6,96,128]{2,1,0:T(8,128)(2,1)S(1)}, u32[]{:S(2)}, u32[]{:S(2)}) %collective-permute-start.16) | collective-permute-done | bytes 147488 | tf_op jit(solution)/shard_map/ppermute | solution.py:251
  88.7 3.2 %collective-permute-start.23 = (bf16[3,96,128]{2,1,0:T(8,128)(2,1)S(1)}, bf16[3,96,128]{2,1,0:T(8,128)(2,1)S(1)}, u32[]{:S(2)}, u32[]{:S(2)}) collective-permute-start(bf16[3,96,128]{2,1,0:T(8,128)(2,1)S(1)} %get-tuple-element.90), channel_id=1, source_target_pairs={{0,14},{2,12},{4,10},{6,8},{8,6},{10,4},{12,2},{14,0},{1,15},{3,13... | collective-permute-start | bytes 221192 | tf_op jit(solution)/shard_map/ppermute | solution.py:251
  91.9 1.8 %group.3.refs_17_ = f32[256,256]{1,0:T(8,128)S(1)} custom-call(bf16[512,512]{1,0:T(8,128)(2,1)S(1)} %ordered_metric.1.refs_0_.refs_1_, bf16[16,32,128]{2,1,0:T(8,128)(2,1)S(1)} %get-tuple-element.54.refs_1_.refs_2_, bf16[16,32,128]{2,1,0:T(8,128)(2,1)S(1)} %collective-permute-done.5._.refs_2_.refs_3_, ...), custom_call_target="tpu_custom_call" | custom-call | flops 1409286144 | bytes 1835008 | tf_op jit(solution)/shard_map/group/pallas_call | solution.py:224
  93.8 1.6 %group.4.refs_18_ = f32[256,256]{1,0:T(8,128)S(1)} custom-call(bf16[512,512]{1,0:T(8,128)(2,1)S(1)} %ordered_metric.1.refs_0_.refs_1_, bf16[16,32,128]{2,1,0:T(8,128)(2,1)S(1)} %get-tuple-element.54.refs_1_.refs_2_, bf16[16,32,128]{2,1,0:T(8,128)(2,1)S(1)} %collective-permute-done.5._.refs_2_.refs_3_, ...), custom_call_target="tpu_custom_call" | custom-call | flops 1207959552 | bytes 1572864 | tf_op jit(solution)/shard_map/group/pallas_call | solution.py:224
  95.4 5.8 %collective-permute-done.20.refs_15_ = bf16[3,96,128]{2,1,0:T(8,128)(2,1)S(1)} collective-permute-done((bf16[3,96,128]{2,1,0:T(8,128)(2,1)S(1)}, bf16[3,96,128]{2,1,0:T(8,128)(2,1)S(1)}, u32[]{:S(2)}, u32[]{:S(2)}) %collective-permute-start.20) | collective-permute-done | bytes 73760 | tf_op jit(solution)/shard_map/ppermute | solution.py:251
  101.2 0.9 collective-permute-done.17.refs_14_
  102.1 1.0 group.5
  103.2 0.5 collective-permute-start.27
  103.7 0.7 collective-permute-done.28
  104.5 1.3 %collective-permute-start.29 = (f32[4,32,128]{2,1,0:T(8,128)S(1)}, f32[4,32,128]{2,1,0:T(8,128)S(1)}, u32[]{:S(2)}, u32[]{:S(2)}) collective-permute-start(f32[4,32,128]{2,1,0:T(8,128)S(1)} %add.31), channel_id=1, source_target_pairs={{0,2},{2,0},{4,6},{6,4},{8,10},{10,8},{12,14},{14,12},{1,3},{3,1},... | collective-permute-start | bytes 196616 | tf_op jit(solution)/shard_map/ppermute | solution.py:251
  105.8 3.0 %collective-permute-done.29 = f32[4,32,128]{2,1,0:T(8,128)S(1)} collective-permute-done((f32[4,32,128]{2,1,0:T(8,128)S(1)}, f32[4,32,128]{2,1,0:T(8,128)S(1)}, u32[]{:S(2)}, u32[]{:S(2)}) %collective-permute-start.29) | collective-permute-done | bytes 65568 | tf_op jit(solution)/shard_map/ppermute | solution.py:251
  108.8 2.9 %collective-permute-start.30 = (f32[32,128]{1,0:T(8,128)S(1)}, f32[32,128]{1,0:T(8,128)S(1)}, u32[]{:S(2)}, u32[]{:S(2)}) collective-permute-start(f32[32,128]{1,0:T(8,128)S(1)} %get-tuple-element.101), channel_id=1, source_target_pairs={{0,12},{2,14},{4,8},{6,10},{8,4},{10,6},{12,0},{14,2},{1,13},{3,15... | collective-permute-start | bytes 49160 | tf_op jit(solution)/shard_map/ppermute | solution.py:251
  111.7 1.5 %collective-permute-start.32 = (f32[32,128]{1,0:T(8,128)S(1)}, f32[32,128]{1,0:T(8,128)S(1)}, u32[]{:S(2)}, u32[]{:S(2)}) collective-permute-start(f32[32,128]{1,0:T(8,128)S(1)} %get-tuple-element.102), channel_id=1, source_target_pairs={{0,8},{2,10},{4,12},{6,14},{8,0},{10,2},{12,4},{14,6},{1,9},{3,11}... | collective-permute-start | bytes 49160 | tf_op jit(solution)/shard_map/ppermute | solution.py:251
  113.3 1.2 collective-permute-done.30
  114.4 1.9 %collective-permute-done.32 = f32[32,128]{1,0:T(8,128)S(1)} collective-permute-done((f32[32,128]{1,0:T(8,128)S(1)}, f32[32,128]{1,0:T(8,128)S(1)}, u32[]{:S(2)}, u32[]{:S(2)}) %collective-permute-start.32) | collective-permute-done | bytes 16416 | tf_op jit(solution)/shard_map/ppermute | solution.py:251
  116.4 0.6 collective-permute-done.31
  116.9 0.6 fusion.3
  (42 shorter events, 0.6 us)
Async XLA Ops:
  0.0 2.9 %copy-start = (bf16[128,512]{1,0:T(8,128)(2,1)S(1)}, bf16[128,512]{1,0:T(8,128)(2,1)}, u32[]{:S(2)}) copy-start(bf16[128,512]{1,0:T(8,128)(2,1)} %param.8) | copy-start | bytes 393220
  0.0 9.5 %copy-start.1 = (bf16[1024,128]{1,0:T(8,128)(2,1)S(1)}, bf16[1024,128]{1,0:T(8,128)(2,1)}, u32[]{:S(2)}) copy-start(bf16[1024,128]{1,0:T(8,128)(2,1)} %own_ref) | copy-start | bytes 786436
  0.0 9.5 %collective-permute-start.4 = (bf16[1024,128]{1,0:T(8,128)(2,1)}, bf16[1024,128]{1,0:T(8,128)(2,1)S(1)}, u32[]{:S(2)}, u32[]{:S(2)}) collective-permute-start(bf16[1024,128]{1,0:T(8,128)(2,1)} %own_ref), channel_id=1, source_target_pairs={{0,2},{2,0},{4,6},{6,4},{8,10},{10,8},{12,14},{14,12},{1,3},{3,1},... | collective-permute-start | bytes 786440 | tf_op jit(solution)/shard_map/ppermute | solution.py:251
  3.0 5.4 %collective-permute-start = (bf16[32,512]{1,0:T(8,128)(2,1)S(1)}, bf16[32,512]{1,0:T(8,128)(2,1)S(1)}, u32[]{:S(2)}, u32[]{:S(2)}) collective-permute-start(bf16[32,512]{1,0:T(8,128)(2,1)S(1)} %constant_dynamic-slice_fusion), channel_id=1, source_target_pairs={{0,8},{2,10},{4,12},{6,14},{8,0},{10,2},{12,4},{14,6},{1,9},{3,11}... | collective-permute-start | bytes 98312 | tf_op jit(solution)/shard_map/ppermute | solution.py:251
  8.3 69.1 %copy-start.2 = (s32[4]{0:T(128)S(1)}, s32[4]{0:T(128)}, u32[]{:S(2)}) copy-start(s32[4]{0:T(128)} %param.9) | copy-start | bytes 52
  10.3 8.1 %collective-permute-start.10 = (bf16[16,32,128]{2,1,0:T(8,128)(2,1)S(1)}, bf16[16,32,128]{2,1,0:T(8,128)(2,1)S(1)}, u32[]{:S(2)}, u32[]{:S(2)}) collective-permute-start(bf16[16,32,128]{2,1,0:T(8,128)(2,1)S(1)} %get-tuple-element.64), channel_id=1, source_target_pairs={{0,12},{2,14},{4,8},{6,10},{8,4},{10,6},{12,0},{14,2},{1,13},{3,15... | collective-permute-start | bytes 393224 | tf_op jit(solution)/shard_map/ppermute | solution.py:251
  14.2 9.3 %collective-permute-start.5 = (bf16[16,32,128]{2,1,0:T(8,128)(2,1)S(1)}, bf16[16,32,128]{2,1,0:T(8,128)(2,1)S(1)}, u32[]{:S(2)}, u32[]{:S(2)}) collective-permute-start(bf16[16,32,128]{2,1,0:T(8,128)(2,1)S(1)} %get-tuple-element.55), channel_id=1, source_target_pairs={{0,2},{2,0},{4,6},{6,4},{8,10},{10,8},{12,14},{14,12},{1,3},{3,1},... | collective-permute-start | bytes 393224 | tf_op jit(solution)/shard_map/ppermute | solution.py:251
  15.7 16.2 %collective-permute-start.7 = (bf16[16,32,128]{2,1,0:T(8,128)(2,1)S(1)}, bf16[16,32,128]{2,1,0:T(8,128)(2,1)S(1)}, u32[]{:S(2)}, u32[]{:S(2)}) collective-permute-start(bf16[16,32,128]{2,1,0:T(8,128)(2,1)S(1)} %get-tuple-element.61), channel_id=1, source_target_pairs={{0,6},{2,4},{4,2},{6,0},{8,14},{10,12},{12,10},{14,8},{1,7},{3,5},... | collective-permute-start | bytes 393224 | tf_op jit(solution)/shard_map/ppermute | solution.py:251
  15.7 16.2 %collective-permute-start.9 = (bf16[16,32,128]{2,1,0:T(8,128)(2,1)S(1)}, bf16[16,32,128]{2,1,0:T(8,128)(2,1)S(1)}, u32[]{:S(2)}, u32[]{:S(2)}) collective-permute-start(bf16[16,32,128]{2,1,0:T(8,128)(2,1)S(1)} %get-tuple-element.63), channel_id=1, source_target_pairs={{0,10},{2,8},{4,14},{6,12},{8,2},{10,0},{12,6},{14,4},{1,11},{3,9}... | collective-permute-start | bytes 393224 | tf_op jit(solution)/shard_map/ppermute | solution.py:251
  17.3 18.6 %collective-permute-start.1 = (bf16[64,512]{1,0:T(8,128)(2,1)S(1)}, bf16[64,512]{1,0:T(8,128)(2,1)S(1)}, u32[]{:S(2)}, u32[]{:S(2)}) collective-permute-start(bf16[64,512]{1,0:T(8,128)(2,1)S(1)} %pad_maximum_fusion.2), channel_id=1, source_target_pairs={{0,4},{2,6},{4,0},{6,2},{8,12},{10,14},{12,8},{14,10},{1,5},{3,7},... | collective-permute-start | bytes 196616 | tf_op jit(solution)/shard_map/ppermute | solution.py:251
  18.3 19.3 %collective-permute-start.8 = (bf16[16,32,128]{2,1,0:T(8,128)(2,1)S(1)}, bf16[16,32,128]{2,1,0:T(8,128)(2,1)S(1)}, u32[]{:S(2)}, u32[]{:S(2)}) collective-permute-start(bf16[16,32,128]{2,1,0:T(8,128)(2,1)S(1)} %get-tuple-element.62), channel_id=1, source_target_pairs={{0,8},{2,10},{4,12},{6,14},{8,0},{10,2},{12,4},{14,6},{1,9},{3,11}... | collective-permute-start | bytes 393224 | tf_op jit(solution)/shard_map/ppermute | solution.py:251
  23.5 15.2 %collective-permute-start.11 = (bf16[16,32,128]{2,1,0:T(8,128)(2,1)S(1)}, bf16[16,32,128]{2,1,0:T(8,128)(2,1)S(1)}, u32[]{:S(2)}, u32[]{:S(2)}) collective-permute-start(bf16[16,32,128]{2,1,0:T(8,128)(2,1)S(1)} %get-tuple-element.66), channel_id=1, source_target_pairs={{0,14},{2,12},{4,10},{6,8},{8,6},{10,4},{12,2},{14,0},{1,15},{3,13... | collective-permute-start | bytes 393224 | tf_op jit(solution)/shard_map/ppermute | solution.py:251
  31.8 7.8 %collective-permute-start.6 = (bf16[16,32,128]{2,1,0:T(8,128)(2,1)S(1)}, bf16[16,32,128]{2,1,0:T(8,128)(2,1)S(1)}, u32[]{:S(2)}, u32[]{:S(2)}) collective-permute-start(bf16[16,32,128]{2,1,0:T(8,128)(2,1)S(1)} %get-tuple-element.60), channel_id=1, source_target_pairs={{0,4},{2,6},{4,0},{6,2},{8,12},{10,14},{12,8},{14,10},{1,5},{3,7},... | collective-permute-start | bytes 393224 | tf_op jit(solution)/shard_map/ppermute | solution.py:251
  32.2 19.4 %collective-permute-start.14 = (bf16[7,96,128]{2,1,0:T(8,128)(2,1)S(1)}, bf16[7,96,128]{2,1,0:T(8,128)(2,1)S(1)}, u32[]{:S(2)}, u32[]{:S(2)}) collective-permute-start(bf16[7,96,128]{2,1,0:T(8,128)(2,1)S(1)} %get-tuple-element.73), channel_id=1, source_target_pairs={{0,8},{2,10},{4,12},{6,14},{8,0},{10,2},{12,4},{14,6},{1,9},{3,11}... | collective-permute-start | bytes 516104 | tf_op jit(solution)/shard_map/ppermute | solution.py:251
  36.0 19.8 %collective-permute-start.24 = (bf16[7,96,128]{2,1,0:T(8,128)(2,1)S(1)}, bf16[7,96,128]{2,1,0:T(8,128)(2,1)S(1)}, u32[]{:S(2)}, u32[]{:S(2)}) collective-permute-start(bf16[7,96,128]{2,1,0:T(8,128)(2,1)S(1)} %get-tuple-element.94), channel_id=1, source_target_pairs={{0,10},{2,8},{4,14},{6,12},{8,2},{10,0},{12,6},{14,4},{1,11},{3,9}... | collective-permute-start | bytes 516104 | tf_op jit(solution)/shard_map/ppermute | solution.py:251
  37.6 21.6 %collective-permute-start.2 = (bf16[128,512]{1,0:T(8,128)(2,1)S(1)}, bf16[128,512]{1,0:T(8,128)(2,1)S(1)}, u32[]{:S(2)}, u32[]{:S(2)}) collective-permute-start(bf16[128,512]{1,0:T(8,128)(2,1)S(1)} %pad_maximum_fusion.1), channel_id=1, source_target_pairs={{0,2},{2,0},{4,6},{6,4},{8,10},{10,8},{12,14},{14,12},{1,3},{3,1},... | collective-permute-start | bytes 393224 | tf_op jit(solution)/shard_map/ppermute | solution.py:251
  38.7 20.6 %collective-permute-start.12 = (bf16[16,96,128]{2,1,0:T(8,128)(2,1)S(1)}, bf16[16,96,128]{2,1,0:T(8,128)(2,1)S(1)}, u32[]{:S(2)}, u32[]{:S(2)}) collective-permute-start(bf16[16,96,128]{2,1,0:T(8,128)(2,1)S(1)} %get-tuple-element.69), channel_id=1, source_target_pairs={{0,2},{2,0},{4,6},{6,4},{8,10},{10,8},{12,14},{14,12},{1,3},{3,1},... | collective-permute-start | bytes 1179656 | tf_op jit(solution)/shard_map/ppermute | solution.py:251
  39.7 19.6 %collective-permute-start.18 = (bf16[7,96,128]{2,1,0:T(8,128)(2,1)S(1)}, bf16[7,96,128]{2,1,0:T(8,128)(2,1)S(1)}, u32[]{:S(2)}, u32[]{:S(2)}) collective-permute-start(bf16[7,96,128]{2,1,0:T(8,128)(2,1)S(1)} %get-tuple-element.82), channel_id=1, source_target_pairs={{0,12},{2,14},{4,8},{6,10},{8,4},{10,6},{12,0},{14,2},{1,13},{3,15... | collective-permute-start | bytes 516104 | tf_op jit(solution)/shard_map/ppermute | solution.py:251
  51.6 21.3 %collective-permute-start.13 = (bf16[16,96,128]{2,1,0:T(8,128)(2,1)S(1)}, bf16[16,96,128]{2,1,0:T(8,128)(2,1)S(1)}, u32[]{:S(2)}, u32[]{:S(2)}) collective-permute-start(bf16[16,96,128]{2,1,0:T(8,128)(2,1)S(1)} %get-tuple-element.71), channel_id=1, source_target_pairs={{0,4},{2,6},{4,0},{6,2},{8,12},{10,14},{12,8},{14,10},{1,5},{3,7},... | collective-permute-start | bytes 1179656 | tf_op jit(solution)/shard_map/ppermute | solution.py:251
  55.8 10.4 %collective-permute-start.25 = (bf16[7,96,128]{2,1,0:T(8,128)(2,1)S(1)}, bf16[7,96,128]{2,1,0:T(8,128)(2,1)S(1)}, u32[]{:S(2)}, u32[]{:S(2)}) collective-permute-start(bf16[7,96,128]{2,1,0:T(8,128)(2,1)S(1)} %get-tuple-element.95), channel_id=1, source_target_pairs={{0,14},{2,12},{4,10},{6,8},{8,6},{10,4},{12,2},{14,0},{1,15},{3,13... | collective-permute-start | bytes 516104 | tf_op jit(solution)/shard_map/ppermute | solution.py:251
  59.2 29.4 %collective-permute-start.15 = (bf16[16,96,128]{2,1,0:T(8,128)(2,1)S(1)}, bf16[16,96,128]{2,1,0:T(8,128)(2,1)S(1)}, u32[]{:S(2)}, u32[]{:S(2)}) collective-permute-start(bf16[16,96,128]{2,1,0:T(8,128)(2,1)S(1)} %get-tuple-element.74), channel_id=1, source_target_pairs={{0,6},{2,4},{4,2},{6,0},{8,14},{10,12},{12,10},{14,8},{1,7},{3,5},... | collective-permute-start | bytes 1179656 | tf_op jit(solution)/shard_map/ppermute | solution.py:251
  59.3 15.1 %collective-permute-start.3 = (bf16[256,512]{1,0:T(8,128)(2,1)S(1)}, bf16[256,512]{1,0:T(8,128)(2,1)S(1)}, u32[]{:S(2)}, u32[]{:S(2)}) collective-permute-start(bf16[256,512]{1,0:T(8,128)(2,1)S(1)} %pad_maximum_fusion.refs_0_), channel_id=1, source_target_pairs={{0,1},{1,0},{2,3},{3,2},{4,5},{5,4},{6,7},{7,6},{8,9},{9,8},{10,11... | collective-permute-start | bytes 786440 | tf_op jit(solution)/shard_map/ppermute | solution.py:254
  59.4 18.8 %collective-permute-start.19 = (bf16[6,96,128]{2,1,0:T(8,128)(2,1)S(1)}, bf16[6,96,128]{2,1,0:T(8,128)(2,1)S(1)}, u32[]{:S(2)}, u32[]{:S(2)}) collective-permute-start(bf16[6,96,128]{2,1,0:T(8,128)(2,1)S(1)} %get-tuple-element.83), channel_id=1, source_target_pairs={{0,10},{2,8},{4,14},{6,12},{8,2},{10,0},{12,6},{14,4},{1,11},{3,9}... | collective-permute-start | bytes 442376 | tf_op jit(solution)/shard_map/ppermute | solution.py:251
  66.2 22.4 %collective-permute-start.16 = (bf16[6,96,128]{2,1,0:T(8,128)(2,1)S(1)}, bf16[6,96,128]{2,1,0:T(8,128)(2,1)S(1)}, u32[]{:S(2)}, u32[]{:S(2)}) collective-permute-start(bf16[6,96,128]{2,1,0:T(8,128)(2,1)S(1)} %get-tuple-element.77), channel_id=1, source_target_pairs={{0,8},{2,10},{4,12},{6,14},{8,0},{10,2},{12,4},{14,6},{1,9},{3,11}... | collective-permute-start | bytes 442376 | tf_op jit(solution)/shard_map/ppermute | solution.py:251
  72.9 20.9 %collective-permute-start.26 = (bf16[6,96,128]{2,1,0:T(8,128)(2,1)S(1)}, bf16[6,96,128]{2,1,0:T(8,128)(2,1)S(1)}, u32[]{:S(2)}, u32[]{:S(2)}) collective-permute-start(bf16[6,96,128]{2,1,0:T(8,128)(2,1)S(1)} %get-tuple-element.96), channel_id=1, source_target_pairs={{0,12},{2,14},{4,8},{6,10},{8,4},{10,6},{12,0},{14,2},{1,13},{3,15... | collective-permute-start | bytes 442376 | tf_op jit(solution)/shard_map/ppermute | solution.py:251
  74.4 19.3 %collective-permute-start.21 = (bf16[6,96,128]{2,1,0:T(8,128)(2,1)S(1)}, bf16[6,96,128]{2,1,0:T(8,128)(2,1)S(1)}, u32[]{:S(2)}, u32[]{:S(2)}) collective-permute-start(bf16[6,96,128]{2,1,0:T(8,128)(2,1)S(1)} %get-tuple-element.87), channel_id=1, source_target_pairs={{0,14},{2,12},{4,10},{6,8},{8,6},{10,4},{12,2},{14,0},{1,15},{3,13... | collective-permute-start | bytes 442376 | tf_op jit(solution)/shard_map/ppermute | solution.py:251
  78.1 23.1 %collective-permute-start.20 = (bf16[3,96,128]{2,1,0:T(8,128)(2,1)S(1)}, bf16[3,96,128]{2,1,0:T(8,128)(2,1)S(1)}, u32[]{:S(2)}, u32[]{:S(2)}) collective-permute-start(bf16[3,96,128]{2,1,0:T(8,128)(2,1)S(1)} %get-tuple-element.84), channel_id=1, source_target_pairs={{0,10},{2,8},{4,14},{6,12},{8,2},{10,0},{12,6},{14,4},{1,11},{3,9}... | collective-permute-start | bytes 221192 | tf_op jit(solution)/shard_map/ppermute | solution.py:251
  88.7 13.4 %collective-permute-start.17 = (bf16[3,96,128]{2,1,0:T(8,128)(2,1)S(1)}, bf16[3,96,128]{2,1,0:T(8,128)(2,1)S(1)}, u32[]{:S(2)}, u32[]{:S(2)}) collective-permute-start(bf16[3,96,128]{2,1,0:T(8,128)(2,1)S(1)} %get-tuple-element.78), channel_id=1, source_target_pairs={{0,8},{2,10},{4,12},{6,14},{8,0},{10,2},{12,4},{14,6},{1,9},{3,11}... | collective-permute-start | bytes 221192 | tf_op jit(solution)/shard_map/ppermute | solution.py:251
  88.7 13.4 %collective-permute-start.23 = (bf16[3,96,128]{2,1,0:T(8,128)(2,1)S(1)}, bf16[3,96,128]{2,1,0:T(8,128)(2,1)S(1)}, u32[]{:S(2)}, u32[]{:S(2)}) collective-permute-start(bf16[3,96,128]{2,1,0:T(8,128)(2,1)S(1)} %get-tuple-element.90), channel_id=1, source_target_pairs={{0,14},{2,12},{4,10},{6,8},{8,6},{10,4},{12,2},{14,0},{1,15},{3,13... | collective-permute-start | bytes 221192 | tf_op jit(solution)/shard_map/ppermute | solution.py:251
  93.7 8.4 %collective-permute-start.22 = (bf16[3,96,128]{2,1,0:T(8,128)(2,1)S(1)}, bf16[3,96,128]{2,1,0:T(8,128)(2,1)S(1)}, u32[]{:S(2)}, u32[]{:S(2)}) collective-permute-start(bf16[3,96,128]{2,1,0:T(8,128)(2,1)S(1)} %get-tuple-element.88), channel_id=1, source_target_pairs={{0,12},{2,14},{4,8},{6,10},{8,4},{10,6},{12,0},{14,2},{1,13},{3,15... | collective-permute-start | bytes 221192 | tf_op jit(solution)/shard_map/ppermute | solution.py:251
  103.1 1.3 %collective-permute-start.28 = (f32[4,32,128]{2,1,0:T(8,128)S(1)}, f32[4,32,128]{2,1,0:T(8,128)S(1)}, u32[]{:S(2)}, u32[]{:S(2)}) collective-permute-start(f32[4,32,128]{2,1,0:T(8,128)S(1)} %get-tuple-element.100), channel_id=1, source_target_pairs={{0,1},{1,0},{2,3},{3,2},{4,5},{5,4},{6,7},{7,6},{8,9},{9,8},{10,11... | collective-permute-start | bytes 196616 | tf_op jit(solution)/shard_map/ppermute | solution.py:254
  103.2 2.6 %collective-permute-start.27 = (f32[4,32,128]{2,1,0:T(8,128)S(1)}, f32[4,32,128]{2,1,0:T(8,128)S(1)}, u32[]{:S(2)}, u32[]{:S(2)}) collective-permute-start(f32[4,32,128]{2,1,0:T(8,128)S(1)} %get-tuple-element.98), channel_id=1, source_target_pairs={{0,1},{1,0},{2,3},{3,2},{4,5},{5,4},{6,7},{7,6},{8,9},{9,8},{10,11... | collective-permute-start | bytes 196616 | tf_op jit(solution)/shard_map/ppermute | solution.py:254
  104.5 4.3 %collective-permute-start.29 = (f32[4,32,128]{2,1,0:T(8,128)S(1)}, f32[4,32,128]{2,1,0:T(8,128)S(1)}, u32[]{:S(2)}, u32[]{:S(2)}) collective-permute-start(f32[4,32,128]{2,1,0:T(8,128)S(1)} %add.31), channel_id=1, source_target_pairs={{0,2},{2,0},{4,6},{6,4},{8,10},{10,8},{12,14},{14,12},{1,3},{3,1},... | collective-permute-start | bytes 196616 | tf_op jit(solution)/shard_map/ppermute | solution.py:251
  108.8 5.6 %collective-permute-start.30 = (f32[32,128]{1,0:T(8,128)S(1)}, f32[32,128]{1,0:T(8,128)S(1)}, u32[]{:S(2)}, u32[]{:S(2)}) collective-permute-start(f32[32,128]{1,0:T(8,128)S(1)} %get-tuple-element.101), channel_id=1, source_target_pairs={{0,12},{2,14},{4,8},{6,10},{8,4},{10,6},{12,0},{14,2},{1,13},{3,15... | collective-permute-start | bytes 49160 | tf_op jit(solution)/shard_map/ppermute | solution.py:251
  111.7 4.6 %collective-permute-start.32 = (f32[32,128]{1,0:T(8,128)S(1)}, f32[32,128]{1,0:T(8,128)S(1)}, u32[]{:S(2)}, u32[]{:S(2)}) collective-permute-start(f32[32,128]{1,0:T(8,128)S(1)} %get-tuple-element.102), channel_id=1, source_target_pairs={{0,8},{2,10},{4,12},{6,14},{8,0},{10,2},{12,4},{14,6},{1,9},{3,11}... | collective-permute-start | bytes 49160 | tf_op jit(solution)/shard_map/ppermute | solution.py:251
  113.2 3.7 %collective-permute-start.31 = (f32[32,128]{1,0:T(8,128)S(1)}, f32[32,128]{1,0:T(8,128)S(1)}, u32[]{:S(2)}, u32[]{:S(2)}) collective-permute-start(f32[32,128]{1,0:T(8,128)S(1)} %get-tuple-element.103), channel_id=1, source_target_pairs={{0,4},{2,6},{4,0},{6,2},{8,12},{10,14},{12,8},{14,10},{1,5},{3,7},... | collective-permute-start | bytes 49160 | tf_op jit(solution)/shard_map/ppermute | solution.py:251
